TPU v7x, 32 devices: a whole 2x2x4 slice. The times are simulated.
32 devices in a mesh: grp: 8 (over z, x), exp: 4 (over y, core).
Axes of the slice: x: 2, y: 2, z: 4, core: 2. Of those that a mesh axis runs over, the one named last changes fastest.
Arguments:
- tokens: bfloat16 [24576, 1536], P(('grp', 'exp')), may hold values from -6 to 6
- cotangent: bfloat16 [24576, 1536], P(('grp', 'exp')), may hold values from -6 to 6
- gate_logits: float32 [24576, 4], P(('grp', 'exp')), may hold values from -3 to 3
- routes: int32 [24576, 4], P(('grp', 'exp')), may hold values from 0 to 31, all different within a row; in each aligned block of 768 rows (0 to 767, 768 to 1535, ...) at most 112 rows name the same one
- piece_starts: int32 [32, 3], P(('grp', 'exp')), may hold values from 0 to 768, as said below
- piece_kinds: int32 [32, 3], P(('grp', 'exp')), may hold values from 0 to 1, as said below
- q_weight: bfloat16 [1536, 1536], P('grp'), may hold values from -0.15625 to 0.15625
- k_weight: bfloat16 [1536, 256], P('grp'), may hold values from -0.15625 to 0.15625
- v_weight: bfloat16 [1536, 256], P('grp'), may hold values from -0.15625 to 0.15625
- o_weight: bfloat16 [1536, 1536], P('grp'), may hold values from -1.25 to 1.25
- attn_gain: bfloat16 [1536], P('grp'), may hold values from 0.25 to 1.75
- moe_gain: bfloat16 [1536], P('grp'), may hold values from 0.25 to 1.75
- gate_weight: bfloat16 [32, 1536, 768], P('exp'), may hold values from -0.15625 to 0.15625
- up_weight: bfloat16 [32, 1536, 768], P('exp'), may hold values from -0.15625 to 0.15625
- down_weight: bfloat16 [32, 1536, 768], P('exp'), may hold values from -0.4375 to 0.4375
Outputs:
- layer_out: bfloat16 [24576, 1536], P(('grp', 'exp'))
- tokens_grad: bfloat16 [24576, 1536], P(('grp', 'exp'))
- logits_grad: float32 [24576, 4], P(('grp', 'exp'))
- q_grad: float32 [1536, 1536], P(('grp', 'exp'))
- k_grad: float32 [1536, 256], P(('grp', 'exp'))
- v_grad: float32 [1536, 256], P(('grp', 'exp'))
- o_grad: float32 [1536, 1536], P(('grp', 'exp'))
- attn_gain_grad: float32 [1536], P(('grp', 'exp'))
- moe_gain_grad: float32 [1536], P(('grp', 'exp'))
- gate_grad: float32 [32, 1536, 768], P('exp', 'grp')
- up_grad: float32 [32, 1536, 768], P('exp', 'grp')
- down_grad: float32 [32, 1536, 768], P('exp', 'grp')
Inputs may be any that keep to these rules, and one draw needn't show every extreme that they name: `routes`: each token names 4 different experts. Among the 768 tokens of one sequence at most 112 assignments go to one expert, and in some sequence some expert gets exactly 112. `piece_starts`: in each sequence the pieces begin at these positions in order, the first at 0, never falling; a piece runs to the next start or to the sequence's end, and equal starts leave a piece empty. `piece_kinds`: A piece of kind 1 spans exactly 256 positions; each sequence has at least one piece of kind 0.
All inputs are finite; a program needn't handle non-finite values.
Results may differ from a plain program's by a relative error of at most 0.015.
Values may be sent and summed in bfloat16 or wider, within the bound.
A program may use at most 448 MiB of HBM per device.

v0:
```python
import jax
import jax.numpy as jnp
from jax import lax
from jax.sharding import PartitionSpec as P

HEADS = 12
KV_HEADS = 2
HEAD_DIM = 128
EXPERTS = 32
TOP = 4
QBLOCK = 768
CAP = 112


EPSILON = 1e-06
THETA = 1000000.0


def norm_forward(values, gain_vec):
    inverse = lax.rsqrt(jnp.mean(values * values, axis=-1, keepdims=True) + EPSILON)
    normal = values * inverse
    return (normal * gain_vec, normal, inverse)


def norm_backward(upstream, normal, inverse, gain_vec):
    scaled = upstream * gain_vec
    return inverse * (scaled - normal * jnp.mean(scaled * normal, axis=-1, keepdims=True))


def rope_tables(length, head_width):
    half_width = head_width // 2
    frequency = THETA ** (-2.0 * jnp.arange(half_width, dtype=jnp.float32) / head_width)
    angles = jnp.arange(length, dtype=jnp.float32)[:, None] * frequency[None, :]
    cosine = jnp.concatenate([jnp.cos(angles), jnp.cos(angles)], axis=-1)[:, None, :]
    sine_part = jnp.concatenate([jnp.sin(angles), jnp.sin(angles)], axis=-1)[:, None, :]
    return (cosine, sine_part)


def rotate(values, cosine, sine_part):
    half_width = values.shape[-1] // 2
    turned = jnp.concatenate([-values[..., half_width:], values[..., :half_width]], axis=-1)
    return values * cosine + turned * sine_part


def unrotate(values, cosine, sine_part):
    half_width = values.shape[-1] // 2
    turned = jnp.concatenate([values[..., half_width:], -values[..., :half_width]], axis=-1)
    return values * cosine + turned * sine_part


def piece_visible(starts, kinds, length):
    places = jnp.arange(length, dtype=jnp.int32)
    piece_of = jnp.sum((places[:, None] >= starts[None, :]).astype(jnp.int32), axis=1) - 1
    slot_ids = jnp.arange(starts.shape[0], dtype=jnp.int32)
    kind_of = jnp.sum(jnp.where(piece_of[:, None] == slot_ids[None, :], kinds[None, :], 0), axis=1)
    inside = (piece_of[:, None] == piece_of[None, :]) & (kind_of[:, None] == 1)
    return (places[None, :] <= places[:, None]) | inside


def slot_positions(routes):
    chosen = routes.reshape(-1)
    onehot = (chosen[:, None] == jnp.arange(EXPERTS, dtype=jnp.int32)[None, :]).astype(jnp.int32)
    earlier = jnp.cumsum(onehot, axis=0) - onehot
    return chosen * CAP + jnp.sum(earlier * onehot, axis=1)


def masked_scores(query_blk, key_rot, visible_blk, score_scale):
    scores = (
        jnp.einsum("qkgd,skd->kgqs", query_blk, key_rot, preferred_element_type=jnp.float32)
        * score_scale
    )
    return jnp.where(visible_blk[None, None], scores, -1e30)


def shards(
    tokens,
    cotangent,
    gate_logits,
    routes,
    piece_starts,
    piece_kinds,
    q_weight,
    k_weight,
    v_weight,
    o_weight,
    attn_gain,
    moe_gain,
    gate_weight,
    up_weight,
    down_weight,
):
    q_full, k_full, v_full, o_full, gain_one, gain_two = (
        lax.all_gather(q_weight, "grp", axis=0, tiled=True),
        lax.all_gather(k_weight, "grp", axis=0, tiled=True),
        lax.all_gather(v_weight, "grp", axis=0, tiled=True),
        lax.all_gather(o_weight, "grp", axis=0, tiled=True),
        lax.all_gather(attn_gain, "grp", axis=0, tiled=True),
        lax.all_gather(moe_gain, "grp", axis=0, tiled=True),
    )
    length = tokens.shape[0]
    model_width = tokens.shape[1]
    group_size = HEADS // KV_HEADS
    score_scale = HEAD_DIM ** (-0.5)
    n_exp = lax.axis_size("exp")
    local_experts = gate_weight.shape[0]
    gain_one_f = gain_one.astype(jnp.float32)
    gain_two_f = gain_two.astype(jnp.float32)
    x_rows = tokens.astype(jnp.float32)
    normed_f, normal_one, inverse_one = norm_forward(x_rows, gain_one_f)
    normed = normed_f.astype(jnp.bfloat16)
    query_lin = jnp.dot(normed, q_full, preferred_element_type=jnp.float32)
    key_lin = jnp.dot(normed, k_full, preferred_element_type=jnp.float32)
    value_rows = (
        jnp.dot(normed, v_full, preferred_element_type=jnp.float32)
        .astype(jnp.bfloat16)
        .reshape(length, KV_HEADS, HEAD_DIM)
    )
    cosine, sine_part = rope_tables(length, HEAD_DIM)
    query_rot = (
        rotate(query_lin.reshape(length, HEADS, HEAD_DIM), cosine, sine_part)
        .astype(jnp.bfloat16)
        .reshape(length, KV_HEADS, group_size, HEAD_DIM)
    )
    key_rot = rotate(key_lin.reshape(length, KV_HEADS, HEAD_DIM), cosine, sine_part).astype(
        jnp.bfloat16
    )
    visible = piece_visible(piece_starts[0], piece_kinds[0], length)
    scores = masked_scores(query_rot, key_rot, visible, score_scale)
    row_max = jnp.max(scores, axis=-1, keepdims=True)
    weights = jnp.exp(scores - row_max)
    row_total = jnp.sum(weights, axis=-1, keepdims=True)
    attn_probs = (weights / row_total).astype(jnp.bfloat16)
    block_out = jnp.einsum(
        "kgqs,skd->qkgd", attn_probs, value_rows, preferred_element_type=jnp.float32
    )
    mixed_parts = block_out.reshape(QBLOCK, HEADS * HEAD_DIM)
    log_totals = [row_max + jnp.log(row_total)]
    mixed = mixed_parts.astype(jnp.bfloat16)
    hidden = x_rows + jnp.dot(mixed, o_full, preferred_element_type=jnp.float32)
    normed_two_f, normal_two, inverse_two = norm_forward(hidden, gain_two_f)
    normed_two = normed_two_f.astype(jnp.bfloat16)
    positions = slot_positions(routes)
    assign_ids = jnp.arange(length * TOP, dtype=jnp.int32)
    slot_assign = jnp.full((EXPERTS * CAP,), length * TOP, jnp.int32).at[positions].set(assign_ids)
    slot_token = slot_assign // TOP
    padded_rows = jnp.concatenate([normed_two, jnp.zeros((1, model_width), jnp.bfloat16)], axis=0)
    send_rows = padded_rows[slot_token].reshape(n_exp, local_experts, CAP, model_width)
    received = lax.all_to_all(send_rows, "exp", split_axis=0, concat_axis=0, tiled=True)
    gate_in = jnp.einsum(
        "secd,edf->secf", received, gate_weight, preferred_element_type=jnp.float32
    )
    up_in = jnp.einsum("secd,edf->secf", received, up_weight, preferred_element_type=jnp.float32)
    sigmoid_gate = jax.nn.sigmoid(gate_in)
    silu_gate = gate_in * sigmoid_gate
    act = (silu_gate * up_in).astype(jnp.bfloat16)
    expert_out = jnp.einsum(
        "secf,edf->secd", act, down_weight, preferred_element_type=jnp.float32
    ).astype(jnp.bfloat16)
    returned = lax.all_to_all(expert_out, "exp", split_axis=0, concat_axis=0, tiled=True)
    back_rows = returned.reshape(EXPERTS * CAP, model_width)[positions].reshape(
        length, TOP, model_width
    )
    gates = jax.nn.softmax(gate_logits, axis=-1)
    layer_out = (hidden + jnp.sum(gates[:, :, None] * back_rows, axis=1)).astype(jnp.bfloat16)
    upstream = cotangent.astype(jnp.float32)
    d_gates = jnp.sum(upstream[:, None, :] * back_rows, axis=-1)
    logits_grad = gates * (d_gates - jnp.sum(gates * d_gates, axis=-1, keepdims=True))
    gate_pad = jnp.concatenate([gates.reshape(-1), jnp.zeros((1,), jnp.float32)], axis=0)
    upstream_pad = jnp.concatenate([upstream, jnp.zeros((1, model_width), jnp.float32)], axis=0)
    slot_grad = (upstream_pad[slot_token] * gate_pad[slot_assign][:, None]).astype(jnp.bfloat16)
    grad_received = lax.all_to_all(
        slot_grad.reshape(n_exp, local_experts, CAP, model_width),
        "exp",
        split_axis=0,
        concat_axis=0,
        tiled=True,
    )
    d_act = jnp.einsum(
        "secd,edf->secf", grad_received, down_weight, preferred_element_type=jnp.float32
    )
    grad_down = jnp.einsum("secd,secf->edf", grad_received, act, preferred_element_type=jnp.float32)
    d_gate_in = (d_act * up_in * sigmoid_gate * (1.0 + gate_in * (1.0 - sigmoid_gate))).astype(
        jnp.bfloat16
    )
    d_up_in = (d_act * silu_gate).astype(jnp.bfloat16)
    grad_gate = jnp.einsum(
        "secd,secf->edf", received, d_gate_in, preferred_element_type=jnp.float32
    )
    grad_up = jnp.einsum("secd,secf->edf", received, d_up_in, preferred_element_type=jnp.float32)
    d_slot_rows = jnp.einsum(
        "secf,edf->secd", d_gate_in, gate_weight, preferred_element_type=jnp.float32
    )
    d_slot_rows = d_slot_rows + jnp.einsum(
        "secf,edf->secd", d_up_in, up_weight, preferred_element_type=jnp.float32
    )
    returned_grad = lax.all_to_all(
        d_slot_rows.astype(jnp.bfloat16), "exp", split_axis=0, concat_axis=0, tiled=True
    )
    d_normed_two = jnp.sum(
        returned_grad.reshape(EXPERTS * CAP, model_width)[positions]
        .reshape(length, TOP, model_width)
        .astype(jnp.float32),
        axis=1,
    )
    d_hidden = upstream + norm_backward(d_normed_two, normal_two, inverse_two, gain_two_f)
    moe_gain_grad = jnp.sum(d_normed_two * normal_two, axis=0)
    d_branch = d_hidden.astype(jnp.bfloat16)
    grad_out_proj = jnp.einsum("ti,td->id", mixed, d_branch, preferred_element_type=jnp.float32)
    d_mixed = jnp.einsum("td,id->ti", d_branch, o_full, preferred_element_type=jnp.float32).astype(
        jnp.bfloat16
    )
    d_mixed = d_mixed.reshape(length, KV_HEADS, group_size, HEAD_DIM)
    d_key_rot = jnp.zeros((length, KV_HEADS, HEAD_DIM), jnp.float32)
    d_value = jnp.zeros((length, KV_HEADS, HEAD_DIM), jnp.float32)
    d_query_parts = []
    for block_id, offset in enumerate(range(0, length, QBLOCK)):
        scores = masked_scores(query_rot, key_rot, visible, score_scale)
        probs_full = jnp.exp(scores - log_totals[block_id])
        d_probs = jnp.einsum(
            "qkgd,skd->kgqs", d_mixed, value_rows, preferred_element_type=jnp.float32
        )
        d_scores = (
            probs_full * (d_probs - jnp.sum(probs_full * d_probs, axis=-1, keepdims=True))
        ).astype(jnp.bfloat16)
        d_value = jnp.einsum(
            "kgqs,qkgd->skd",
            probs_full.astype(jnp.bfloat16),
            d_mixed,
            preferred_element_type=jnp.float32,
        )
        d_query_parts.append(
            jnp.einsum("kgqs,skd->qkgd", d_scores, key_rot, preferred_element_type=jnp.float32)
            * score_scale
        )
        d_key_rot = (
            jnp.einsum("kgqs,qkgd->skd", d_scores, query_rot, preferred_element_type=jnp.float32)
            * score_scale
        )
    d_query_rot = d_query_parts[0].reshape(length, HEADS, HEAD_DIM)
    d_query = (
        unrotate(d_query_rot, cosine, sine_part)
        .reshape(length, HEADS * HEAD_DIM)
        .astype(jnp.bfloat16)
    )
    d_key = (
        unrotate(d_key_rot, cosine, sine_part)
        .reshape(length, KV_HEADS * HEAD_DIM)
        .astype(jnp.bfloat16)
    )
    d_value = d_value.reshape(length, KV_HEADS * HEAD_DIM).astype(jnp.bfloat16)
    grad_query = jnp.einsum("ti,tj->ij", normed, d_query, preferred_element_type=jnp.float32)
    grad_key = jnp.einsum("ti,tj->ij", normed, d_key, preferred_element_type=jnp.float32)
    grad_value = jnp.einsum("ti,tj->ij", normed, d_value, preferred_element_type=jnp.float32)
    d_normed = jnp.einsum("tj,ij->ti", d_query, q_full, preferred_element_type=jnp.float32)
    d_normed = d_normed + jnp.einsum("tj,ij->ti", d_key, k_full, preferred_element_type=jnp.float32)
    d_normed = d_normed + jnp.einsum(
        "tj,ij->ti", d_value, v_full, preferred_element_type=jnp.float32
    )
    attn_gain_grad = jnp.sum(d_normed * normal_one, axis=0)
    tokens_grad = (d_hidden + norm_backward(d_normed, normal_one, inverse_one, gain_one_f)).astype(
        jnp.bfloat16
    )
    q_sum, k_sum, v_sum, o_sum, attn_gain_sum, moe_gain_sum = (
        lax.psum_scatter(grad_query, ("grp", "exp"), scatter_dimension=0, tiled=True),
        lax.psum_scatter(grad_key, ("grp", "exp"), scatter_dimension=0, tiled=True),
        lax.psum_scatter(grad_value, ("grp", "exp"), scatter_dimension=0, tiled=True),
        lax.psum_scatter(grad_out_proj, ("grp", "exp"), scatter_dimension=0, tiled=True),
        lax.psum_scatter(attn_gain_grad, ("grp", "exp"), scatter_dimension=0, tiled=True),
        lax.psum_scatter(moe_gain_grad, ("grp", "exp"), scatter_dimension=0, tiled=True),
    )
    gate_sum, up_sum, down_sum = (
        lax.psum_scatter(
            grad_gate.astype(jnp.bfloat16), "grp", scatter_dimension=1, tiled=True
        ).astype(jnp.float32),
        lax.psum_scatter(
            grad_up.astype(jnp.bfloat16), "grp", scatter_dimension=1, tiled=True
        ).astype(jnp.float32),
        lax.psum_scatter(
            grad_down.astype(jnp.bfloat16), "grp", scatter_dimension=1, tiled=True
        ).astype(jnp.float32),
    )
    return (
        layer_out,
        tokens_grad,
        logits_grad,
        q_sum,
        k_sum,
        v_sum,
        o_sum,
        attn_gain_sum,
        moe_gain_sum,
        gate_sum,
        up_sum,
        down_sum,
    )


def solution(mesh):
    placed = (
        P(("grp", "exp"), None),
        P(("grp", "exp"), None),
        P(("grp", "exp"), None),
        P(("grp", "exp"), None),
        P(("grp", "exp"), None),
        P(("grp", "exp"), None),
        P("grp", None),
        P("grp", None),
        P("grp", None),
        P("grp", None),
        P("grp"),
        P("grp"),
        P("exp", None, None),
        P("exp", None, None),
        P("exp", None, None),
    )
    return jax.shard_map(
        shards,
        mesh=mesh,
        in_specs=placed,
        out_specs=(
            P(("grp", "exp"), None),
            P(("grp", "exp"), None),
            P(("grp", "exp"), None),
            P(("grp", "exp"), None),
            P(("grp", "exp"), None),
            P(("grp", "exp"), None),
            P(("grp", "exp"), None),
            P(("grp", "exp")),
            P(("grp", "exp")),
            P("exp", "grp", None),
            P("exp", "grp", None),
            P("exp", "grp", None),
        ),
        check_vma=False,
    )
```

profile of v0, /device:TPU:0, one launch (start us, length us, event | category | flops | bytes accessed | tf_op | source)
XLA Modules:
  0.0 1952.3 jit_solution(9602459643502093290)
XLA Ops:
  16.4 24.1 %all-reduce.7 = (bf16[1536]{0:T(1024)(128)(2,1)S(1)}, bf16[1536]{0:T(1024)(128)(2,1)S(1)}) all-reduce(bf16[1536]{0:T(1024)(128)(2,1)S(1)} %dynamic-update-slice, bf16[1536]{0:T(1024)(128)(2,1)S(1)} %dynamic-update-slice.1), channel_id=1, replica_groups=mesh['grp'=8,'exp'=4] {'grp'}, use_global_device_ids=true, to_apply=%add.2 | all-reduce | flops 3072 | bytes 12288
  74.1 33.9 %all_gather.20 = bf16[1536,256]{1,0:T(8,128)(2,1)S(1)} all-gather(bf16[192,256]{1,0:T(8,128)(2,1)S(1)} %copy-done.37), channel_id=1, replica_groups=mesh['grp'=8,'exp'=4] {'grp'}, dimensions={0}, use_global_device_ids=true | all-gather | bytes 884736 | tf_op jit(solution)/shard_map/all_gather | solution.py:94
  107.9 33.9 %all_gather.19 = bf16[1536,256]{1,0:T(8,128)(2,1)S(1)} all-gather(bf16[192,256]{1,0:T(8,128)(2,1)} %param.23), channel_id=1, replica_groups=mesh['grp'=8,'exp'=4] {'grp'}, dimensions={0}, use_global_device_ids=true | all-gather | bytes 884736 | tf_op jit(solution)/shard_map/all_gather | solution.py:95
  223.5 18.9 gather_fusion.3
  245.2 24.3 %gather_fusion.2 = f32[3584,1536]{1,0:T(8,128)} fusion(f32[769,1536]{1,0:T(8,128)} %concatenate.39, s32[4096]{0:T(1024)S(1)} %get-tuple-element.75), kind=kCustom, calls=%fused_computation.2 | custom fusion | bytes 44054528 | tf_op jit(solution)/shard_map/gather | solution.py:170
  281.7 60.6 %all-to-all-done = bf16[4,8,112,1536]{3,2,1,0:T(8,128)(2,1)} async-done(((bf16[4,8,112,1536]{3,2,1,0:T(8,128)(2,1)}), bf16[4,8,112,1536]{3,2,1,0:T(8,128)(2,1)}, u32[]{:S(2)}, u32[]{:S(2)}) %all-to-all-start) | async-done | bytes 11010080 | tf_op jit(solution)/shard_map/all_to_all | solution.py:148
  348.5 19.2 fusion.7
  367.7 19.2 fusion.11
  387.0 82.7 %all-to-all-done.2 = bf16[4,8,112,1536]{3,2,1,0:T(8,128)(2,1)} async-done(((bf16[4,8,112,1536]{3,2,1,0:T(8,128)(2,1)}), bf16[4,8,112,1536]{3,2,1,0:T(8,128)(2,1)}, u32[]{:S(2)}, u32[]{:S(2)}) %all-to-all-start.2) | async-done | bytes 11010080 | tf_op jit(solution)/shard_map/all_to_all | solution.py:171
  469.7 27.2 %fusion.28 = (bf16[4,8,112,768]{3,2,0,1:T(8,128)(2,1)}, bf16[4,8,112,768]{3,2,0,1:T(8,128)(2,1)}, bf16[4,8,112,768]{3,2,0,1:T(8,128)(2,1)}) fusion(f32[8,4,112,768]{3,2,1,0:T(8,128)} %fusion.7, f32[8,4,112,768]{3,2,1,0:T(8,128)} %fusion.11, bf16[8,1536,768]{2,1,0:T(8,128)(2,1)} %param.29, bf16[4,8,112,1536]{3,2,1,0:T(8,128)(2,1)} %all-to-all-done.2), kind=kOutput, calls=%fused_computation.44 | convolution fusion | flops 8497004544 | bytes 68419584 | tf_op jit(solution)/shard_map/secd,edf->secf/dot_general | solution.py:178
  496.9 17.8 bitcast_convert_fusion
  514.8 17.7 bitcast_convert_fusion.2
  532.6 18.2 bitcast_convert_fusion.1
  584.2 21.2 %fusion.5 = f32[8,4,112,1536]{3,2,1,0:T(8,128)} fusion(bf16[4,8,112,768]{3,2,0,1:T(8,128)(2,1)} %get-tuple-element.48, bf16[8,1536,768]{2,1,0:T(8,128)(2,1)} %param.28), kind=kOutput, calls=%fused_computation.22 | convolution fusion | flops 8455716864 | bytes 46399488 | tf_op jit(solution)/shard_map/secf,edf->secd/dot_general | solution.py:193
  605.4 22.6 %fusion.39 = bf16[4,8,112,1536]{3,2,0,1:T(8,128)(2,1)} fusion(f32[8,4,112,1536]{3,2,1,0:T(8,128)} %fusion.5, bf16[4,8,112,768]{3,2,0,1:T(8,128)(2,1)} %get-tuple-element.46, bf16[8,1536,768]{2,1,0:T(8,128)(2,1)} %param.27), kind=kOutput, calls=%fused_computation.57 | convolution fusion | flops 8466726912 | bytes 57409536 | tf_op jit(solution)/shard_map/secf,edf->secd/dot_general | solution.py:190
  637.9 67.5 %all-to-all-done.1 = bf16[4,8,112,1536]{3,2,1,0:T(8,128)(2,1)} async-done(((bf16[4,8,112,1536]{3,2,1,0:T(8,128)(2,1)}), bf16[4,8,112,1536]{3,2,1,0:T(8,128)(2,1)}, u32[]{:S(2)}, u32[]{:S(2)}) %all-to-all-start.1) | async-done | bytes 11010080 | tf_op jit(solution)/shard_map/all_to_all | solution.py:159
  714.6 24.9 %gather_fusion.1 = bf16[3072,1536]{1,0:T(8,128)(2,1)} fusion(bf16[3584,1536]{1,0:T(8,128)(2,1)} %bitcast.30, s32[3072]{0:T(1024)S(1)} %broadcast_clamp_fusion), kind=kCustom, calls=%fused_computation.1 | custom fusion | bytes 18886656 | tf_op jit(solution)/shard_map/gather | solution.py:160
  739.5 17.9 reshape.265
  757.4 75.3 %all-to-all-done.3 = bf16[4,8,112,1536]{3,2,1,0:T(8,128)(2,1)} async-done(((bf16[4,8,112,1536]{3,2,1,0:T(8,128)(2,1)}), bf16[4,8,112,1536]{3,2,1,0:T(8,128)(2,1)}, u32[]{:S(2)}, u32[]{:S(2)}) %all-to-all-start.3) | async-done | bytes 11010080 | tf_op jit(solution)/shard_map/all_to_all | solution.py:196
  832.8 25.7 %gather_fusion.4 = bf16[3072,1536]{1,0:T(8,128)(2,1)} fusion(bf16[3584,1536]{1,0:T(8,128)(2,1)} %bitcast.37, s32[3072]{0:T(1024)S(1)} %broadcast_clamp_fusion), kind=kCustom, calls=%fused_computation.4 | custom fusion | bytes 18886656 | tf_op jit(solution)/shard_map/gather | solution.py:200
  858.4 17.9 reshape.266
  876.4 18.0 reduce_sum.155
  900.1 24.0 %multiply_reduce_fusion = (f32[768,4]{1,0:T(8,128)}, f32[768,1536]{1,0:T(8,128)}) fusion(f32[768,4,1536]{2,1,0:T(4,128)} %reshape.265, f32[768,1536]{1,0:T(8,128)} %convert_element_type.167, f32[768,4]{1,0:T(8,128)S(1)} %copy-done.16), kind=kLoop, calls=%fused_computation.34 | loop fusion | flops 17691648 | bytes 28336128 | tf_op jit(solution)/shard_map/reduce_sum | solution.py:166
  958.4 21.4 %fusion = (f32[2,6,768]{2,1,0:T(8,128)S(1)}, f32[2,768,768,6]{2,1,3,0:T(8,128)}) fusion(f32[2,6,768,768]{2,3,1,0:T(8,128)} %get-tuple-element.66, f32[2,6,768]{2,1,0:T(8,128)S(1)} %log_add_fusion, bf16[768,2,128,1]{0,2,3,1:T(8,128)(2,1)S(1)} %bitcast.223, bf16[768,2,6,128]{0,3,2,1:T(8,128)(2,1)S(1)} %bitcast.210), kind=kOutput, calls=%fused_computation.11 | convolution fusion | flops 1833163776 | bytes 59449344 | tf_op jit(solution)/shard_map/qkgd,skd->kgqs/dot_general | solution.py:219
  979.8 24.6 %fusion.2 = bf16[2,6,768,768]{2,3,1,0:T(8,128)(2,1)} fusion(f32[2,768,768,6]{2,1,3,0:T(8,128)} %get-tuple-element.70, f32[2,6,768,768]{2,3,1,0:T(8,128)} %get-tuple-element.66, f32[2,6,768]{2,1,0:T(8,128)S(1)} %get-tuple-element.69, f32[2,6,768]{2,1,0:T(8,128)S(1)} %log_add_fusion), kind=kLoop, calls=%fused_computation.13 | loop fusion | flops 28311552 | bytes 70852608 | tf_op jit(solution)/shard_map/convert_element_type | solution.py:224
  1059.8 41.2 %all-reduce.6 = (f32[1536]{0:T(1024)S(1)}, f32[1536]{0:T(1024)S(1)}) all-reduce(f32[1536]{0:T(1024)S(1)} %get-tuple-element.40, f32[1536]{0:T(1024)S(1)} %copy-done.49), channel_id=6, replica_groups=mesh['grp'=8,'exp'=4] {'grp','exp'}, use_global_device_ids=true, to_apply=%region_24.25.clone | all-reduce | flops 3072 | bytes 24576
  1113.0 29.3 %reduce-scatter.16.cloned.1.call-done = bf16[8,192,768]{2,1,0:T(8,128)(2,1)} async-done(((bf16[8,1536,768]{2,1,0:T(8,128)(2,1)}), bf16[8,192,768]{2,1,0:T(8,128)(2,1)}) %reduce-scatter.16.cloned.1.call-update) | async-done | bytes 2359312 | tf_op jit(solution)/shard_map/reduce_scatter | solution.py:272
  1146.6 312.0 %reduce-scatter.18.cloned.1.call-done = bf16[8,192,768]{2,1,0:T(8,128)(2,1)} async-done(((bf16[8,1536,768]{2,1,0:T(8,128)(2,1)}), bf16[8,192,768]{2,1,0:T(8,128)(2,1)}) %reduce-scatter.18.cloned.1.call-update) | async-done | bytes 2359312 | tf_op jit(solution)/shard_map/reduce_scatter | solution.py:275
  1462.8 97.6 %reduce-scatter.12.cloned.1.call-done = f32[48,256]{1,0:T(8,128)} async-done(((f32[1536,256]{1,0:T(8,128)}), f32[48,256]{1,0:T(8,128)}) %reduce-scatter.12.cloned.1.call-update) | async-done | bytes 49168 | tf_op jit(solution)/shard_map/reduce_scatter | solution.py:266
  1560.4 101.9 %reduce-scatter.10.cloned.1.call-done = f32[48,256]{1,0:T(8,128)} async-done(((f32[1536,256]{1,0:T(8,128)}), f32[48,256]{1,0:T(8,128)}) %reduce-scatter.10.cloned.1.call-update) | async-done | bytes 49168 | tf_op jit(solution)/shard_map/reduce_scatter | solution.py:265
  1662.3 141.2 %reduce-scatter.14.cloned.1.call-done = f32[48,1536]{1,0:T(8,128)} async-done(((f32[1536,1536]{1,0:T(8,128)}), f32[48,1536]{1,0:T(8,128)}) %reduce-scatter.14.cloned.1.call-update) | async-done | bytes 294928 | tf_op jit(solution)/shard_map/reduce_scatter | solution.py:267
  1803.5 142.1 %reduce-scatter.8.cloned.1.call-done = f32[48,1536]{1,0:T(8,128)} async-done(((f32[1536,1536]{1,0:T(8,128)}), f32[48,1536]{1,0:T(8,128)}) %reduce-scatter.8.cloned.1.call-update) | async-done | bytes 294928 | tf_op jit(solution)/shard_map/reduce_scatter | solution.py:264
  (234 shorter events, 312.6 us)
Async XLA Ops:
  7.2 139.2 %all-gather.3.cloned.1.call-start = ((), (), s32[]{:S(2)}) async-start(), calls=%async_computation.11 | async-start | bytes 5308416 | tf_op jit(solution)/shard_map/all_gather | solution.py:93
  7.9 184.9 %all-gather.5.cloned.1.call-start = ((), (), s32[]{:S(2)}) async-start(), calls=%async_computation.12 | async-start | bytes 5308416 | tf_op jit(solution)/shard_map/all_gather | solution.py:96
  10.5 63.5 %copy-start.37 = (bf16[192,256]{1,0:T(8,128)(2,1)S(1)}, bf16[192,256]{1,0:T(8,128)(2,1)}, u32[]{:S(2)}) copy-start(bf16[192,256]{1,0:T(8,128)(2,1)} %param.22) | copy-start | bytes 294916
  14.5 127.4 %copy-start.5 = (bf16[768,1536]{1,0:T(8,128)(2,1)S(1)}, bf16[768,1536]{1,0:T(8,128)(2,1)}, u32[]{:S(2)}) copy-start(bf16[768,1536]{1,0:T(8,128)(2,1)} %param.15) | copy-start | bytes 7077892
  14.5 131.9 %copy-start.47 = (f32[768]{0:T(1024)}, f32[768]{0:T(1024)S(1)}, u32[]{:S(2)}) copy-start(f32[768]{0:T(1024)S(1)} %add_rsqrt_fusion.1) | copy-start | bytes 9220
  40.5 105.9 %copy-start.38 = (f32[1536]{0:T(1024)}, f32[1536]{0:T(1024)S(1)}, u32[]{:S(2)}) copy-start(f32[1536]{0:T(1024)S(1)} %convert_element_type.147) | copy-start | bytes 18436
  40.5 159.2 %copy-start.33 = (f32[1536]{0:T(1024)}, f32[1536]{0:T(1024)S(1)}, u32[]{:S(2)}) copy-start(f32[1536]{0:T(1024)S(1)} %convert_element_type.157) | copy-start | bytes 18436
  41.8 112.0 %copy-start.10 = (f32[768,128]{0,1:T(8,128)}, f32[768,128]{0,1:T(8,128)S(1)}, u32[]{:S(2)}) copy-start(f32[768,128]{0,1:T(8,128)S(1)} %pad_maximum_fusion.1) | copy-start | bytes 1179652
  61.4 81.6 %copy-start.45 = (s32[3072,1]{0,1:T(1,128)}, s32[3072,1]{0,1:T(1,128)S(1)}, u32[]{:S(2)}) copy-start(s32[3072,1]{0,1:T(1,128)S(1)} %compare_select_fusion) | copy-start | bytes 36868
  74.1 69.0 %copy-start.12 = (f32[768,128]{0,1:T(8,128)}, f32[768,128]{0,1:T(8,128)S(1)}, u32[]{:S(2)}) copy-start(f32[768,128]{0,1:T(8,128)S(1)} %get-tuple-element.60) | copy-start | bytes 1179652
  107.9 36.0 %copy-start.21 = (bf16[1536,256]{1,0:T(8,128)(2,1)}, bf16[1536,256]{1,0:T(8,128)(2,1)S(1)}, u32[]{:S(2)}) copy-start(bf16[1536,256]{1,0:T(8,128)(2,1)S(1)} %all_gather.20) | copy-start | bytes 2359300
  214.8 127.5 %all-to-all-start = ((bf16[4,8,112,1536]{3,2,1,0:T(8,128)(2,1)}), bf16[4,8,112,1536]{3,2,1,0:T(8,128)(2,1)}, u32[]{:S(2)}, u32[]{:S(2)}) async-start(bf16[4,8,112,1536]{3,2,1,0:T(8,128)(2,1)} %bitcast.205), calls=%async_computation | async-start | bytes 22020096 | tf_op jit(solution)/shard_map/all_to_all | solution.py:148
  223.4 18.9 copy-start.3
  342.3 127.4 %all-to-all-start.2 = ((bf16[4,8,112,1536]{3,2,1,0:T(8,128)(2,1)}), bf16[4,8,112,1536]{3,2,1,0:T(8,128)(2,1)}, u32[]{:S(2)}, u32[]{:S(2)}) async-start(bf16[4,8,112,1536]{3,2,1,0:T(8,128)(2,1)} %multiply_convert_fusion), calls=%async_computation.2 | async-start | bytes 22020096 | tf_op jit(solution)/shard_map/all_to_all | solution.py:171
  348.5 760.3 %reduce-scatter.20.cloned.1.call-start = ((), (), s32[]{:S(2)}) async-start(), calls=%async_computation.19 | async-start | bytes 21233664 | tf_op jit(solution)/shard_map/reduce_scatter | solution.py:278
  514.8 627.5 %reduce-scatter.16.cloned.1.call-start = ((), (), s32[]{:S(2)}) async-start(), calls=%async_computation.17 | async-start | bytes 21233664 | tf_op jit(solution)/shard_map/reduce_scatter | solution.py:272
  532.5 926.0 %reduce-scatter.18.cloned.1.call-start = ((), (), s32[]{:S(2)}) async-start(), calls=%async_computation.18 | async-start | bytes 21233664 | tf_op jit(solution)/shard_map/reduce_scatter | solution.py:275
  578.0 127.4 %all-to-all-start.1 = ((bf16[4,8,112,1536]{3,2,1,0:T(8,128)(2,1)}), bf16[4,8,112,1536]{3,2,1,0:T(8,128)(2,1)}, u32[]{:S(2)}, u32[]{:S(2)}) async-start(bf16[4,8,112,1536]{3,2,1,0:T(8,128)(2,1)} %copy.130), calls=%async_computation.1 | async-start | bytes 22020096 | tf_op jit(solution)/shard_map/all_to_all | solution.py:159
  637.9 73.9 %copy-start.4 = (bf16[768,1536]{1,0:T(8,128)(2,1)S(1)}, bf16[768,1536]{1,0:T(8,128)(2,1)}, u32[]{:S(2)}) copy-start(bf16[768,1536]{1,0:T(8,128)(2,1)} %param.16) | copy-start | bytes 7077892
  705.4 127.3 %all-to-all-start.3 = ((bf16[4,8,112,1536]{3,2,1,0:T(8,128)(2,1)}), bf16[4,8,112,1536]{3,2,1,0:T(8,128)(2,1)}, u32[]{:S(2)}, u32[]{:S(2)}) async-start(bf16[4,8,112,1536]{3,2,1,0:T(8,128)(2,1)} %copy.133), calls=%async_computation.3 | async-start | bytes 22020096 | tf_op jit(solution)/shard_map/all_to_all | solution.py:196
  711.5 848.8 %reduce-scatter.12.cloned.1.call-start = ((), (), s32[]{:S(2)}) async-start(), calls=%async_computation.15 | async-start | bytes 1622016 | tf_op jit(solution)/shard_map/reduce_scatter | solution.py:266
  876.3 18.0 copy-start.34
  876.3 18.0 copy-start.42
  894.3 29.9 %slice-start = ((s8[4718592]{0:T(1024)(128)(4,1)}), s8[4194304]{0:T(1024)(128)(4,1)S(1)}, s32[]{:S(2)}) async-start(s8[4718592]{0:T(1024)(128)(4,1)} %bitcast.206), calls=%async_computation.20 | async-start | bytes 8388608
  900.1 24.1 %slice-start.1 = ((s8[4718592]{0:T(1024)(128)(4,1)}), s8[524288]{0:T(1024)(128)(4,1)S(1)}, s32[]{:S(2)}) async-start(s8[4718592]{0:T(1024)(128)(4,1)} %bitcast.206), calls=%async_computation.21 | async-start | bytes 1048576
  979.7 682.5 %reduce-scatter.10.cloned.1.call-start = ((), (), s32[]{:S(2)}) async-start(), calls=%async_computation.14 | async-start | bytes 1622016 | tf_op jit(solution)/shard_map/reduce_scatter | solution.py:265
  979.8 24.6 %copy-start.2 = (bf16[768,2,6,128]{0,3,2,1:T(8,128)(2,1)S(1)}, bf16[768,2,6,128]{0,3,2,1:T(8,128)(2,1)}, u32[]{:S(2)}) copy-start(bf16[768,2,6,128]{0,3,2,1:T(8,128)(2,1)} %copy-done.1) | copy-start | bytes 7077892
  1019.0 784.5 %reduce-scatter.14.cloned.1.call-start = ((), (), s32[]{:S(2)}) async-start(), calls=%async_computation.16 | async-start | bytes 9732096 | tf_op jit(solution)/shard_map/reduce_scatter | solution.py:267
  1028.3 917.3 %reduce-scatter.8.cloned.1.call-start = ((), (), s32[]{:S(2)}) async-start(), calls=%async_computation.13 | async-start | bytes 9732096 | tf_op jit(solution)/shard_map/reduce_scatter | solution.py:264
  1055.9 46.3 %copy-start.30 = (f32[768,4]{0,1:T(4,128)S(1)}, f32[768,4]{0,1:T(4,128)}, u32[]{:S(2)}) copy-start(f32[768,4]{0,1:T(4,128)} %param.17) | copy-start | bytes 36868
  1055.9 46.3 %copy-start.36 = (f32[768]{0:T(1024)S(1)}, f32[768]{0:T(1024)}, u32[]{:S(2)}) copy-start(f32[768]{0:T(1024)} %copy-done.35) | copy-start | bytes 9220
  1055.9 46.3 %copy-start.44 = (f32[768]{0:T(1024)S(1)}, f32[768]{0:T(1024)}, u32[]{:S(2)}) copy-start(f32[768]{0:T(1024)} %copy-done.43) | copy-start | bytes 9220
  (37 other events, 186.5 us)
Sparse Core Ops, SparseCore 0:
  10.2 92.2 all-gather.2
  104.7 82.5 all-gather.4
  514.9 310.1 reduce-scatter.19
  828.8 313.4 reduce-scatter.15
  1146.0 312.4 reduce-scatter.17
  1464.2 96.1 reduce-scatter.11
  1566.2 96.0 reduce-scatter.9
  1668.7 134.6 reduce-scatter.13
  1811.0 134.5 reduce-scatter.7
where the time goes:
time: 1960 us; the launch traced here: 1950 us
  waiting for transfers between devices  1110 us (57%)
  matrix products  314 us (16%)
  local copies, waits for them, and re-layouts  197 us (10%)
  other arithmetic  155 us (8%)
  blocking collectives  133 us (7%)
  starting transfers between devices  25.1 us (1%)
    reduce_scatter x1, waiting for transfers between devices, shards(): lax.psum_scatter(grad_up.astype(jnp.bfloat16), 'grp', scatter_dimension=1...  312 us
    reduce_scatter x1, waiting for transfers between devices, shards(): lax.psum_scatter(grad_query, ('grp', 'exp'), scatter_dimension=0, tiled=T...  142 us
    reduce_scatter x1, waiting for transfers between devices, shards(): lax.psum_scatter(grad_out_proj, ('grp', 'exp'), scatter_dimension=0, tile...  141 us
    reduce_scatter x1, waiting for transfers between devices, shards(): lax.psum_scatter(grad_key, ('grp', 'exp'), scatter_dimension=0, tiled=True)  102 us
    reduce_scatter x1, waiting for transfers between devices, shards(): lax.psum_scatter(grad_value, ('grp', 'exp'), scatter_dimension=0, tiled=T...  97.6 us
    all_to_all x1, waiting for transfers between devices, shards(): lax.all_to_all(slot_grad.reshape(n_exp, local_experts, CAP, model_width),...  82.7 us
    all_to_all x1, waiting for transfers between devices, shards(): lax.all_to_all(d_slot_rows.astype(jnp.bfloat16), 'exp', split_axis=0, con...  75.3 us
    all_to_all x1, waiting for transfers between devices, shards(): lax.all_to_all(expert_out, 'exp', split_axis=0, concat_axis=0, tiled=True)  67.5 us
  transfers between devices with their start and end apart: 13, of which 10 were waited for; matrix products, arithmetic and copies ran while one was open for 30% of the time, Pallas kernels for 0%

commit v1 on v0

v1 whole, which is shorter than its diff:
```python
import functools

import jax
import jax.numpy as jnp
from jax import lax
from jax.experimental import pallas as pl
from jax.experimental.pallas import tpu as pltpu
from jax.sharding import PartitionSpec as P

HEADS = 12
KV_HEADS = 2
HEAD_DIM = 128
EXPERTS = 32
TOP = 4
CAP = 112
EPSILON = 1e-06
THETA = 1000000.0
SCALE = HEAD_DIM ** (-0.5)
CORE = 1
PAIR = 2
VMEM = 58 * 1024 * 1024
BF16 = jnp.bfloat16
F32 = jnp.float32


class Flow:
    def __init__(self):
        self.last = None

    def after(self, *arrays):
        if self.last is None:
            return arrays if len(arrays) > 1 else arrays[0]
        out = lax.optimization_barrier(tuple(arrays) + (self.last,))[:-1]
        return out if len(out) > 1 else out[0]

    def mark(self, value):
        self.last = value
        return value


def swap(values, axis, bit):
    size = lax.axis_size(axis)
    return lax.ppermute(values, axis, [(i, i ^ bit) for i in range(size)])


def bits_of(size):
    return [1 << i for i in range(size.bit_length() - 1)]


def bit_at(index, bit):
    return (index // bit) % 2


def rope_tables(length):
    half = HEAD_DIM // 2
    frequency = THETA ** (-2.0 * jnp.arange(half, dtype=F32) / HEAD_DIM)
    angles = jnp.arange(length, dtype=F32)[:, None] * frequency[None, :]
    cosine, sine = jnp.cos(angles), jnp.sin(angles)
    return jnp.concatenate([cosine, cosine], axis=-1), jnp.concatenate([-sine, sine], axis=-1)


def piece_tags(starts, kinds, length):
    places = jnp.arange(length, dtype=jnp.int32)
    piece_of = jnp.sum((places[:, None] >= starts[None, :]).astype(jnp.int32), axis=1) - 1
    slot_ids = jnp.arange(starts.shape[0], dtype=jnp.int32)
    kind_of = jnp.sum(jnp.where(piece_of[:, None] == slot_ids[None, :], kinds[None, :], 0), axis=1)
    return jnp.where(kind_of == 1, piece_of + 1, 0)


def call(body, **kw):
    params = pltpu.CompilerParams(vmem_limit_bytes=VMEM)
    cost = pl.CostEstimate(flops=1, bytes_accessed=1, transcendentals=0)
    return pl.pallas_call(body, compiler_params=params, cost_estimate=cost, **kw)


def shape(*dims, dtype=BF16):
    return jax.ShapeDtypeStruct(dims, dtype)


def dot(a, b, ca=1, cb=0):
    return lax.dot_general(a, b, (((ca,), (cb,)), ((), ())), preferred_element_type=F32)


ANY = pl.BlockSpec(memory_space=pl.ANY)
WHOLE = pl.BlockSpec(memory_space=pltpu.VMEM)
SCALAR = pl.BlockSpec(memory_space=pltpu.SMEM)


def fixed(*dims):
    return pl.BlockSpec(dims, lambda *_: (0,) * len(dims))


def attend_body(
    x_ref, gain_ref, wq_ref, wk_ref, wv_ref, cos_ref, sin_ref, tagc_ref, tagr_ref,
    n1_ref, inv_ref, qr_ref, kr_ref, v_ref, mix_ref, lse_ref,
    mask_ref,
):
    step = pl.program_id(0)
    length = x_ref.shape[0]
    block = 256
    pairs_per_group = pl.num_programs(0) // KV_HEADS

    @pl.when(step == 0)
    def _():
        for r in range(0, length, block):
            x = x_ref[r : r + block].astype(F32)
            inverse = lax.rsqrt(jnp.mean(x * x, axis=-1, keepdims=True) + EPSILON)
            inv_ref[r : r + block] = inverse
            n1_ref[r : r + block] = (x * inverse * gain_ref[...]).astype(BF16)
            row = lax.broadcasted_iota(jnp.int32, (block, length), 0) + r
            col = lax.broadcasted_iota(jnp.int32, (block, length), 1)
            tag = tagc_ref[r : r + block]
            inside = (tag == tagr_ref[...]) & (tag > 0)
            mask_ref[r : r + block] = jnp.where((col <= row) | inside, 0.0, -1e30)

    def turn(u):
        return u * cos_ref[...] + pltpu.roll(u, HEAD_DIM // 2, 1) * sin_ref[...]

    @pl.when(step % pairs_per_group == 0)
    def _():
        kr_ref[...] = turn(dot(n1_ref[...], wk_ref[...])).astype(BF16)
        v_ref[...] = dot(n1_ref[...], wv_ref[...]).astype(BF16)

    q2 = dot(n1_ref[...], wq_ref[...])
    for h in range(2):
        cols = slice(h * HEAD_DIM, (h + 1) * HEAD_DIM)
        qr_ref[:, cols] = turn(q2[:, cols]).astype(BF16)
        for r in range(0, length, block):
            keys = min(length, r + 2 * block)
            s = dot(qr_ref[r : r + block, cols], kr_ref[:keys], 1, 1) * SCALE
            s = s + mask_ref[r : r + block, :keys]
            top = jnp.max(s, axis=-1, keepdims=True)
            e = jnp.exp(s - top)
            total = jnp.sum(e, axis=-1, keepdims=True)
            p = (e * (1.0 / total)).astype(BF16)
            mix_ref[r : r + block, cols] = dot(p, v_ref[:keys]).astype(BF16)
            lse_ref[h, r : r + block] = top + jnp.log(total)


def attend(x, gain, w, cosine, sine, tagc, tagr):
    length, width = x.shape
    pairs = HEADS // 2
    per = pairs // KV_HEADS
    q_blocks = HEADS
    return call(
        attend_body,
        grid=(pairs,),
        in_specs=[
            fixed(length, width),
            fixed(1, width),
            pl.BlockSpec((width, 2 * HEAD_DIM), lambda p: (0, p)),
            pl.BlockSpec((width, HEAD_DIM), lambda p: (0, q_blocks + p // per)),
            pl.BlockSpec((width, HEAD_DIM), lambda p: (0, q_blocks + KV_HEADS + p // per)),
            fixed(length, HEAD_DIM),
            fixed(length, HEAD_DIM),
            fixed(length, 1),
            fixed(1, length),
        ],
        out_specs=[
            fixed(length, width),
            fixed(length, 1),
            pl.BlockSpec((length, 2 * HEAD_DIM), lambda p: (0, p)),
            pl.BlockSpec((length, HEAD_DIM), lambda p: (0, p // per)),
            pl.BlockSpec((length, HEAD_DIM), lambda p: (0, p // per)),
            pl.BlockSpec((length, 2 * HEAD_DIM), lambda p: (0, p)),
            pl.BlockSpec((2, length, 1), lambda p: (p, 0, 0)),
        ],
        out_shape=[
            shape(length, width),
            shape(length, 1, dtype=F32),
            shape(length, HEADS * HEAD_DIM),
            shape(length, KV_HEADS * HEAD_DIM),
            shape(length, KV_HEADS * HEAD_DIM),
            shape(length, HEADS * HEAD_DIM),
            shape(HEADS, length, 1, dtype=F32),
        ],
        scratch_shapes=[pltpu.VMEM((length, length), F32)],
        name="attend",
    )(x, gain, w, w, w, cosine, sine, tagc, tagr)


def project_body(x_ref, mix_ref, wo_ref, gain_ref, hid_ref, n2_ref, inv_ref):
    rows = x_ref.shape[0]
    block = rows // 2
    for r in range(0, rows, block):
        h = x_ref[r : r + block].astype(F32) + dot(mix_ref[r : r + block], wo_ref[...])
        inverse = lax.rsqrt(jnp.mean(h * h, axis=-1, keepdims=True) + EPSILON)
        hid_ref[r : r + block] = h
        inv_ref[r : r + block] = inverse
        n2_ref[r : r + block] = (h * inverse * gain_ref[...]).astype(BF16)


def project(x, mixed, wo, gain):
    length, width = x.shape
    inner = mixed.shape[1]
    steps = 2
    rows = length // steps
    by_row = pl.BlockSpec((rows, width), lambda i: (i, 0))
    return call(
        project_body,
        grid=(steps,),
        in_specs=[by_row, pl.BlockSpec((rows, inner), lambda i: (i, 0)), fixed(inner, width), fixed(1, width)],
        out_specs=[by_row, by_row, pl.BlockSpec((rows, 1), lambda i: (i, 0))],
        out_shape=[shape(length, width, dtype=F32), shape(length, width), shape(length, 1, dtype=F32)],
        name="project",
    )(x, mixed, wo, gain)


def hot_rows(rank, s, local, length):
    spot = lax.broadcasted_iota(jnp.int32, (CAP, length), 0)
    picked = rank[s]
    return jnp.concatenate(
        [(picked[e : e + 1] == spot).astype(F32).astype(BF16) for e in range(local)], axis=0
    )


def collect_body(counts, local, rank_ref, *refs):
    total, count = sum(counts), len(counts)
    out_ref, in_buf, out_buf, in_sem, out_sem = refs[total:]
    items, at = [], 0
    for parts in counts:
        items.append(refs[at : at + parts])
        at += parts
    length, width = in_buf.shape[1:]
    half = length // 2
    chunk = 512

    def fetch(i, slot):
        parts = items[i] if len(items[i]) == 2 else [items[i][0].at[pl.ds(p * half, half)] for p in range(2)]
        for p in range(2):
            pltpu.make_async_copy(parts[p], in_buf.at[slot, pl.ds(p * half, half)], in_sem.at[slot, p]).start()

    def leaving(s, slot, e):
        return pltpu.make_async_copy(
            out_buf.at[slot, pl.ds(e * CAP, CAP)],
            out_ref.at[e, pl.ds(pl.multiple_of(s * CAP, 16), CAP)],
            out_sem.at[slot, e],
        )

    fetch(0, 0)

    def body(s, carry):
        slot = s % 2
        for i in range(1, count):
            @pl.when(s + 1 == i)
            def _():
                fetch(i, i % 2)

        for p in range(2):
            rows = in_buf.at[slot, pl.ds(p * half, half)]
            pltpu.make_async_copy(rows, rows, in_sem.at[slot, p]).wait()

        @pl.when(s >= 2)
        def _():
            for e in range(local):
                leaving(s - 2, slot, e).wait()

        hot = hot_rows(rank_ref, s, local, length)
        for c in range(0, width, chunk):
            out_buf[slot, :, c : c + chunk] = dot(hot, in_buf[slot, :, c : c + chunk]).astype(BF16)
        for e in range(local):
            leaving(s, slot, e).start()
        return carry

    lax.fori_loop(0, count, body, 0)
    for s in (count - 2, count - 1):
        for e in range(local):
            leaving(s, s % 2, e).wait()


def collect(rank, items):
    count, local, length = rank.shape
    width = items[0][0].shape[1]
    counts = [len(item) for item in items]
    return call(
        functools.partial(collect_body, counts, local),
        in_specs=[WHOLE] + [ANY] * sum(counts),
        out_specs=ANY,
        out_shape=shape(local, count * CAP, width),
        scratch_shapes=[
            pltpu.VMEM((2, length, width), BF16),
            pltpu.VMEM((2, local * CAP, width), BF16),
            pltpu.SemaphoreType.DMA((2, 2)),
            pltpu.SemaphoreType.DMA((2, local)),
        ],
        name="collect",
    )(rank, *[part for item in items for part in item])


def combine_body(count, local, *refs):
    rank_ref = refs[0]
    far, near, in_buf, out_buf, in_sem, out_sem = refs[-6:]
    rows = refs[1:-6]
    rows = rows if len(rows) == local else [rows[0].at[e] for e in range(local)]
    length, width = out_buf.shape[1:]
    chunk = 512
    first = count // 2

    def coming(s, slot, e):
        return pltpu.make_async_copy(
            rows[e].at[pl.ds(pl.multiple_of(s * CAP, 16), CAP)],
            in_buf.at[slot, pl.ds(e * CAP, CAP)],
            in_sem.at[slot, e],
        )

    for e in range(local):
        coming(first, 0, e).start()

    def body(step, carry):
        slot = step % 2
        s = (step + first) % count

        @pl.when(step + 1 < count)
        def _():
            for e in range(local):
                coming((step + 1 + first) % count, 1 - slot, e).start()

        for e in range(local):
            coming(s, slot, e).wait()

        @pl.when(step >= 2)
        def _():
            pltpu.make_async_copy(out_buf.at[slot], far.at[0], out_sem.at[slot]).wait()

        hot = hot_rows(rank_ref, s, local, length)
        for c in range(0, width, chunk):
            out_buf[slot, :, c : c + chunk] = dot(hot, in_buf[slot, :, c : c + chunk], 0, 0).astype(BF16)

        @pl.when(step < first)
        def _():
            pltpu.make_async_copy(out_buf.at[slot], far.at[step], out_sem.at[slot]).start()

        @pl.when(step >= first)
        def _():
            pltpu.make_async_copy(out_buf.at[slot], near.at[step - first], out_sem.at[slot]).start()

        return carry

    lax.fori_loop(0, count, body, 0)
    for step in (count - 2, count - 1):
        pltpu.make_async_copy(out_buf.at[step % 2], far.at[0], out_sem.at[step % 2]).wait()


def combine(rank, rows, width):
    count, local, length = rank.shape
    return call(
        functools.partial(combine_body, count, local),
        in_specs=[WHOLE] + [ANY] * len(rows),
        out_specs=[ANY] * 2,
        out_shape=[shape(count // 2, length, width)] * 2,
        scratch_shapes=[
            pltpu.VMEM((2, local * CAP, width), BF16),
            pltpu.VMEM((2, length, width), BF16),
            pltpu.SemaphoreType.DMA((2, local)),
            pltpu.SemaphoreType.DMA((2,)),
        ],
        name="combine",
    )(rank, *rows)


def upstream_body(first_ref, y_ref, w_ref, t_ref):
    t_ref[0] = dot(y_ref[0], w_ref[0])


def upstream_product(first, y, w):
    local, rows, width = y.shape
    ff = w.shape[2]
    grid_spec = pltpu.PrefetchScalarGridSpec(
        num_scalar_prefetch=1,
        grid=(local,),
        in_specs=[
            pl.BlockSpec((1, rows, width), lambda e, f: (e, 0, 0)),
            pl.BlockSpec((1, width, ff), lambda e, f: (f[0] + e, 0, 0)),
        ],
        out_specs=pl.BlockSpec((1, rows, ff), lambda e, f: (e, 0, 0)),
    )
    return call(
        upstream_body, grid_spec=grid_spec, out_shape=shape(local, rows, ff, dtype=F32), name="upstream"
    )(first, y, w)


def output_body(first_ref, *refs):
    acts, w_ref, out_ref = refs[:-2], refs[-2], refs[-1]
    step = pl.program_id(0)
    for e, act in enumerate(acts):
        @pl.when(step == e)
        def _():
            out_ref[0] = dot(act[...], w_ref[0], 1, 1).astype(BF16)


def output_rows(first, acts, w):
    local = len(acts)
    rows, ff = acts[0].shape
    width = w.shape[1]
    grid_spec = pltpu.PrefetchScalarGridSpec(
        num_scalar_prefetch=1,
        grid=(local,),
        in_specs=[pl.BlockSpec((rows, ff), lambda e, f: (0, 0))] * local
        + [pl.BlockSpec((1, width, ff), lambda e, f: (f[0] + e, 0, 0))],
        out_specs=pl.BlockSpec((1, rows, width), lambda e, f: (e, 0, 0)),
    )
    return call(
        output_body, grid_spec=grid_spec, out_shape=shape(local, rows, width), name="output"
    )(first, *acts, w)


def expert_body(
    expert, n_grp, info_ref, x_hbm, y_hbm, t_hbm, gate_ref, wg_hbm, wu_hbm,
    out_theirs, out_mine, out_dx, out_act, dg_ref,
    x, y, t, w, gu, d, act, theirs, mine, dx, sems,
):
    rows, width = x.shape
    ff = t.shape[1]
    block = 448 if rows % 448 == 0 else rows
    index = info_ref[0] + expert
    place = info_ref[1]
    copies = [
        pltpu.make_async_copy(x_hbm.at[expert], x, sems.at[0]),
        pltpu.make_async_copy(wg_hbm.at[index], w.at[:, pl.ds(0, ff)], sems.at[1]),
        pltpu.make_async_copy(wu_hbm.at[index], w.at[:, pl.ds(ff, ff)], sems.at[2]),
        pltpu.make_async_copy(t_hbm.at[expert], t, sems.at[3]),
        pltpu.make_async_copy(y_hbm.at[expert], y, sems.at[4]),
    ]
    for copy in copies:
        copy.start()
    for copy in copies[:3]:
        copy.wait()

    def forward(b, carry):
        at = pl.ds(pl.multiple_of(b * block, 16), block)
        gu[...] = dot(x[at], w[...])

        @pl.when(b == 0)
        def _():
            copies[3].wait()

        def point(i, carry):
            inner = pl.ds(pl.multiple_of(i * 32, 32), 32)
            outer = pl.ds(pl.multiple_of(b * block + i * 32, 32), 32)
            g, u = gu[inner, :ff], gu[inner, ff:]
            tt, gate = t[outer], gate_ref[0, outer]
            sig = 1.0 / (1.0 + jnp.exp(-g))
            silu = g * sig
            a = (silu * u).astype(BF16)
            a32 = a.astype(F32)
            dg_ref[outer] = jnp.sum(a32 * tt, axis=-1, keepdims=True)
            act[outer] = (a32 * gate).astype(BF16)
            da = gate * tt
            d[outer, :ff] = (da * u * sig * (1.0 + g * (1.0 - sig))).astype(BF16)
            d[outer, ff:] = (da * silu).astype(BF16)
            return carry

        return lax.fori_loop(0, block // 32, point, carry)

    lax.fori_loop(0, rows // block, forward, 0)
    copies[4].wait()
    act_out = pltpu.make_async_copy(act, out_act, sems.at[0])
    act_out.start()

    piece = width // n_grp
    band = 384
    keep = band // 2

    def split(j, k, res):
        res = res.astype(BF16)
        for p in range(band // (2 * piece)):
            low = res[2 * p * piece : (2 * p + 1) * piece]
            high = res[(2 * p + 1) * piece : (2 * p + 2) * piece]
            at = pl.ds(pl.multiple_of(j * keep + p * piece, 16), piece)

            @pl.when(place == 0)
            def _():
                theirs[k, at] = high
                mine[k, at] = low

            @pl.when(place != 0)
            def _():
                theirs[k, at] = low
                mine[k, at] = high

    def band_down(j, carry):
        cols = pl.ds(pl.multiple_of(j * band, 128), band)
        split(j, 2, dot(y[:, cols], act[...], 0, 0))
        return carry

    def band_gate(j, carry):
        cols = pl.ds(pl.multiple_of(j * band, 128), band)
        res = dot(x[:, cols], d[...], 0, 0)
        split(j, 0, res[:, :ff])
        split(j, 1, res[:, ff:])
        return carry

    bands = width // band
    lax.fori_loop(0, bands, band_gate, 0)
    early = [
        pltpu.make_async_copy(theirs.at[pl.ds(0, 2)], out_theirs.at[pl.ds(0, 2)], sems.at[1]),
        pltpu.make_async_copy(mine.at[pl.ds(0, 2)], out_mine.at[pl.ds(0, 2)], sems.at[2]),
    ]
    for copy in early:
        copy.start()
    lax.fori_loop(0, bands, band_down, 0)
    late = [
        pltpu.make_async_copy(theirs.at[2], out_theirs.at[2], sems.at[5]),
        pltpu.make_async_copy(mine.at[2], out_mine.at[2], sems.at[6]),
    ]
    for copy in late:
        copy.start()

    def back(b, carry):
        at = pl.ds(pl.multiple_of(b * block, 16), block)
        for c in range(0, width, 512):
            dx[at, c : c + 512] = dot(d[at], w[c : c + 512], 1, 1).astype(BF16)
        return carry

    lax.fori_loop(0, rows // block, back, 0)
    dx_out = pltpu.make_async_copy(dx, out_dx, sems.at[7])
    dx_out.start()
    for copy in [act_out] + early + late + [dx_out]:
        copy.wait()


def expert_step(expert, n_grp, info, x, y, t, gate, w_gate, w_up):
    local, rows, width = x.shape
    ff = t.shape[2]
    half = shape(3, width // 2, ff)
    return call(
        functools.partial(expert_body, expert, n_grp),
        grid=(1,),
        in_specs=[SCALAR, ANY, ANY, ANY, pl.BlockSpec((1, rows, 1), lambda _: (expert, 0, 0)), ANY, ANY],
        out_specs=[ANY] * 4 + [fixed(rows, 1)],
        out_shape=[half] * 2 + [shape(rows, width), shape(rows, ff), shape(rows, 1, dtype=F32)],
        scratch_shapes=[
            pltpu.VMEM((rows, width), BF16),
            pltpu.VMEM((rows, width), BF16),
            pltpu.VMEM((rows, ff), F32),
            pltpu.VMEM((width, 2 * ff), BF16),
            pltpu.VMEM((448 if rows % 448 == 0 else rows, 2 * ff), F32),
            pltpu.VMEM((rows, 2 * ff), BF16),
            pltpu.VMEM((rows, ff), BF16),
            pltpu.VMEM((3, width // 2, ff), BF16),
            pltpu.VMEM((3, width // 2, ff), BF16),
            pltpu.VMEM((rows, width), BF16),
            pltpu.SemaphoreType.DMA((8,)),
        ],
        name="expert",
    )(info, x, y, t, gate, w_gate, w_up)


def attend_back_body(
    q_ref, k_ref, v_ref, dm_ref, lse_ref, delta_ref, cos_ref, sin_ref, tagc_ref, tagr_ref,
    dq_ref, dk_ref, dv_ref,
    mask_ref, dk_acc, dv_acc, dq_acc,
):
    step = pl.program_id(0)
    per = pl.num_programs(0) // KV_HEADS
    length = q_ref.shape[0]
    block = 256

    @pl.when(step == 0)
    def _():
        for r in range(0, length, block):
            key = lax.broadcasted_iota(jnp.int32, (block, length), 0) + r
            query = lax.broadcasted_iota(jnp.int32, (block, length), 1)
            tag = tagc_ref[r : r + block]
            inside = (tag == tagr_ref[...]) & (tag > 0)
            mask_ref[r : r + block] = jnp.where((key <= query) | inside, 0.0, -1e30)

    @pl.when(step % per == 0)
    def _():
        dk_acc[...] = jnp.zeros_like(dk_acc)
        dv_acc[...] = jnp.zeros_like(dv_acc)

    def unturn(w):
        return w * cos_ref[...] - pltpu.roll(w, HEAD_DIM // 2, 1) * sin_ref[...]

    for h in range(2):
        cols = slice(h * HEAD_DIM, (h + 1) * HEAD_DIM)
        dq_acc[...] = jnp.zeros_like(dq_acc)
        for r in range(0, length, block):
            low = max(0, r - block)
            q, dm = q_ref[low:, cols], dm_ref[low:, cols]
            k, v = k_ref[r : r + block], v_ref[r : r + block]
            s = dot(k, q, 1, 1) * SCALE + mask_ref[r : r + block, low:]
            p = jnp.exp(s - lse_ref[h, :, low:])
            dp = dot(v, dm, 1, 1)
            ds = (p * (dp - delta_ref[h, :, low:])).astype(BF16)
            dk_acc[r : r + block] += dot(ds, q)
            dv_acc[r : r + block] += dot(p.astype(BF16), dm)
            dq_acc[low:] += dot(ds, k, 0, 0)
        dq_ref[:, cols] = unturn(dq_acc[...] * SCALE).astype(BF16)

    @pl.when(step % per == per - 1)
    def _():
        dk_ref[...] = unturn(dk_acc[...] * SCALE).astype(BF16)
        dv_ref[...] = dv_acc[...].astype(BF16)


def attend_back(q, k, v, dm, lse, delta, cosine, sine, tagc, tagr):
    length = q.shape[0]
    pairs = HEADS // 2
    per = pairs // KV_HEADS
    two = pl.BlockSpec((length, 2 * HEAD_DIM), lambda p: (0, p))
    one = pl.BlockSpec((length, HEAD_DIM), lambda p: (0, p // per))
    line = pl.BlockSpec((2, 1, length), lambda p: (p, 0, 0))
    return call(
        attend_back_body,
        grid=(pairs,),
        in_specs=[two, one, one, two, line, line, fixed(length, HEAD_DIM), fixed(length, HEAD_DIM), fixed(length, 1), fixed(1, length)],
        out_specs=[two, one, one],
        out_shape=[shape(length, HEADS * HEAD_DIM), shape(length, KV_HEADS * HEAD_DIM), shape(length, KV_HEADS * HEAD_DIM)],
        scratch_shapes=[
            pltpu.VMEM((length, length), F32),
            pltpu.VMEM((length, HEAD_DIM), F32),
            pltpu.VMEM((length, HEAD_DIM), F32),
            pltpu.VMEM((length, HEAD_DIM), F32),
        ],
        name="attend_back",
    )(q, k, v, dm, lse, delta, cosine, sine, tagc, tagr)


def cluster_steps():
    return [("exp", bit) for bit in bits_of(lax.axis_size("exp"))[1:]]


def gather_now(own):
    half = own.shape[0] // 2
    steps = cluster_steps()
    items = [own]
    for axis, bit in steps[:-1]:
        items = items + [swap(item, axis, bit) for item in items]
    axis, bit = steps[-1]
    along = [swap(item, axis, bit) for item in items]
    across = [swap(item, "grp", PAIR) for item in items]
    corner = [(swap(z[:half], axis, bit), swap(y[half:], "grp", PAIR)) for y, z in zip(along, across)]
    items = [(item,) for item in items + along + across] + corner
    return items + [tuple(swap(part, "exp", CORE) for part in item) for item in items]


def gather_late(own, first, gate_value):
    steps = cluster_steps()
    own = lax.optimization_barrier((own, first))[0]
    items = [own]
    for axis, bit in steps:
        items = items + [swap(item, axis, bit) for item in items]
    held = lax.optimization_barrier((own, gate_value))[0]
    across = [swap(held, "grp", PAIR)]
    for axis, bit in steps:
        across = across + [swap(item, axis, bit) for item in across]
    items = items + across
    items = items + [swap(item, "exp", CORE) for item in items]
    return [(item,) for item in items]


def gather_small(own):
    items = [own]
    for axis, bit in cluster_steps() + [("grp", PAIR), ("exp", CORE)]:
        block = jnp.stack(items)
        items = items + list(swap(block, axis, bit))
    return items


def add(first, second):
    return (first.astype(F32) + second.astype(F32)).astype(BF16)


class Return:
    def __init__(self, far, near, flow):
        self.flow = flow
        count, length, width = near.shape
        self.dims = (4, count // 4, length, width)
        self.near = near
        self.came = swap(far, "exp", CORE)
        self.stage = 0

    def step(self):
        self.stage += 1
        flow = self.flow
        axis, bit = cluster_steps()[-1]
        half = self.dims[2] // 2
        if self.stage == 1:
            near, came = flow.after(self.near, self.came)
            near, came = near.reshape(self.dims), came.reshape(self.dims)

            def part(index, rows):
                return add(near[index, :, rows], came[index, :, rows])

            low, high = slice(0, half), slice(half, None)
            zc = part(slice(2, 4), low)
            yc = part(slice(1, 4, 2), high)
            zc, yc = flow.mark(lax.optimization_barrier((zc, yc)))
            self.zc, self.yc = swap(zc, "grp", PAIR), swap(yc, axis, bit)
            near, came = flow.after(near, came)
            self.low, self.high = part(0, low), part(0, high)
            self.y_low, self.z_high = part(1, low), part(2, high)
        elif self.stage == 2:
            zc, yc = flow.after(self.zc, self.yc)
            y_low, z_high = flow.mark(
                lax.optimization_barrier((add(self.y_low, zc[1]), add(self.z_high, yc[1])))
            )
            self.y_low, self.z_high = swap(y_low, axis, bit), swap(z_high, "grp", PAIR)
            self.zc, self.yc = zc[0], yc[0]
        else:
            y_low, z_high = flow.after(self.y_low, self.z_high)
            low = self.low.astype(F32) + self.zc.astype(F32) + y_low.astype(F32)
            high = self.high.astype(F32) + self.yc.astype(F32) + z_high.astype(F32)
            total = jnp.concatenate([low, high], axis=1)
            for axis, bit in reversed(cluster_steps()[:-1]):
                count = total.shape[0] // 2
                total = total[:count] + swap(total[count:].astype(BF16), axis, bit).astype(F32)
            return total[0]


def exchange_small(items):
    steps = cluster_steps() + [("grp", PAIR), ("exp", CORE)]
    block = jnp.stack(items)
    for axis, bit in reversed(steps):
        count = block.shape[0] // 2
        block = jnp.concatenate([block[:count], swap(block[count:], axis, bit)], axis=2)
    return block[0]


def ring_order(size):
    return list(range(0, size, 2)) + list(range(size - 1, 0, -2))


def ring_origins():
    size = lax.axis_size("grp")
    order = ring_order(size)
    place = [0] * size
    for i, value in enumerate(order):
        place[value] = i
    spot = jnp.array(place, jnp.int32)[lax.axis_index("grp")]
    ahead = [(spot - step) % size for step in range(size // 2 + 1)]
    behind = [(spot + step) % size for step in range(1, size - size // 2)]
    return jnp.array(order, jnp.int32)[jnp.stack(ahead + behind)]


def ring_pieces(own):
    size = lax.axis_size("grp")
    order = ring_order(size)
    onward = [(order[i], order[(i + 1) % size]) for i in range(size)]
    back = [(order[(i + 1) % size], order[i]) for i in range(size)]
    first, second = [own], []
    for step in range(1, size // 2 + 1):
        first.append(lax.ppermute(first[-1], "grp", onward))
        if step < size - size // 2:
            second.append(lax.ppermute(second[-1] if second else own, "grp", back))
    return first + second


def assemble_body(count, info_ref, *refs):
    out, sems = refs[-2:]
    rows, half = refs[0].shape
    core = info_ref[count]
    copies = []
    for i in range(count):
        at = pl.ds(pl.multiple_of(info_ref[i] * rows, 16), rows)
        for side in range(2):
            column = side * (1 - core) + (1 - side) * core
            to = out.at[at, pl.ds(pl.multiple_of(column * half, 128), half)]
            copies.append(pltpu.make_async_copy(refs[2 * i + side], to, sems.at[i, side]))
    for copy in copies:
        copy.start()
    for copy in copies:
        copy.wait()


def gather_weights(shard, origins, core):
    rows, width = shard.shape
    half = width // 2
    mine = lax.dynamic_slice_in_dim(shard, core * half, half, 1)
    pieces = ring_pieces(mine)
    others = [swap(piece, "exp", CORE) for piece in pieces]
    count = len(pieces)
    info = jnp.concatenate([origins, core[None]])
    both = [part for pair in zip(pieces, others) for part in pair]
    whole = call(
        functools.partial(assemble_body, count),
        in_specs=[SCALAR] + [ANY] * (2 * count),
        out_specs=WHOLE,
        out_shape=shape(count * rows, width),
        scratch_shapes=[pltpu.SemaphoreType.DMA((count, 2))],
        name="assemble",
    )(info, *both)
    return whole, pieces[count // 2]


class GradSum:
    def __init__(self, theirs, mine, flow):
        kinds, rows, width = mine.shape
        bits = bits_of(lax.axis_size("grp"))
        self.flow = flow
        self.left = list(reversed(bits[1:]))
        self.todo = [bit for bit in bits[1:] if bit != PAIR] + [PAIR]
        self.dims = [kinds] + [2] * len(self.left) + [rows >> len(self.left), width]
        self.mine = mine
        self.coming = swap(theirs, "grp", bits[0])
        self.done = False

    def step(self):
        if self.done:
            return
        mine, coming = self.flow.after(self.mine, self.coming)
        block = self.flow.mark(add(mine, coming)).reshape(self.dims)
        bit = self.todo.pop(0)
        axis = self.left.index(bit) + 1
        self.left.pop(axis - 1)
        self.dims.pop(axis)
        place = bit_at(lax.axis_index("grp"), bit)
        theirs = lax.dynamic_index_in_dim(block, 1 - place, axis, keepdims=False)
        self.mine = lax.dynamic_index_in_dim(block, place, axis, keepdims=False)
        self.coming = swap(theirs, "grp", bit)
        self.done = not self.todo


class AllSum:
    def __init__(self, block, flow):
        self.flow = flow
        rows, width = block.shape
        n_grp, n_exp = lax.axis_size("grp"), lax.axis_size("exp")
        grp_bits, exp_bits = bits_of(n_grp), bits_of(n_exp)
        self.left = [("grp", bit) for bit in reversed(grp_bits)] + [("exp", bit) for bit in reversed(exp_bits)]
        others = [bit for bit in reversed(grp_bits) if bit != PAIR]
        self.todo = [("exp", bit) for bit in exp_bits] + [("grp", bit) for bit in [PAIR] + others]
        self.block = block.reshape([2] * len(self.left) + [rows // (n_grp * n_exp), width])
        self.coming = None
        self.send()

    def send(self):
        name, bit = self.todo.pop(0)
        axis = self.left.index((name, bit))
        self.left.pop(axis)
        place = bit_at(lax.axis_index(name), bit)
        theirs = lax.dynamic_index_in_dim(self.block, 1 - place, axis, keepdims=False)
        self.mine = lax.dynamic_index_in_dim(self.block, place, axis, keepdims=False)
        self.coming = swap(theirs, name, bit)

    def step(self):
        if self.coming is None:
            return
        mine, coming = self.flow.after(self.mine, self.coming)
        if self.todo:
            self.block = self.flow.mark(add(mine, coming) if mine.dtype == BF16 else mine + coming)
            self.send()
        else:
            self.block = mine.astype(F32) + coming.astype(F32)
            self.coming = None


def norm_backward(upstream, normal, inverse, gain_vec):
    scaled = upstream * gain_vec
    return inverse * (scaled - normal * jnp.mean(scaled * normal, axis=-1, keepdims=True))


def shards(
    tokens,
    cotangent,
    gate_logits,
    routes,
    piece_starts,
    piece_kinds,
    q_weight,
    k_weight,
    v_weight,
    o_weight,
    attn_gain,
    moe_gain,
    gate_weight,
    up_weight,
    down_weight,
):
    grp, exp = lax.axis_index("grp"), lax.axis_index("exp")
    n_grp = lax.axis_size("grp")
    core = exp % 2
    pair = bit_at(grp, PAIR)
    length, width = tokens.shape
    held = gate_weight.shape[0]
    local = held // 2
    q_width, kv_width = q_weight.shape[1], k_weight.shape[1]

    gates = jax.nn.softmax(gate_logits, axis=-1)
    small_all = jnp.stack(gather_small(jnp.concatenate([routes.astype(F32), gates], axis=1)))
    gain = jnp.stack([attn_gain, moe_gain]).astype(F32)[None]
    for bit in bits_of(n_grp):
        gain = jnp.concatenate([gain, swap(gain, "grp", bit)], axis=0)
    gain = gain[jnp.arange(n_grp, dtype=jnp.int32) ^ grp]
    gain_one = gain[:, 0].reshape(1, width)
    gain_two = gain[:, 1].reshape(1, width)
    origins = ring_origins()
    qkv_full, last = gather_weights(jnp.concatenate([q_weight, k_weight, v_weight], axis=1), origins, core)
    o_full, last = gather_weights(lax.optimization_barrier((o_weight, last))[0], origins, core)
    dy_items = gather_late(cotangent, small_all, last)

    cosine, sine = rope_tables(length)
    tags = piece_tags(piece_starts[0], piece_kinds[0], length)
    tagc, tagr = tags.reshape(length, 1), tags.reshape(1, length)

    routes_all = small_all[:, :, :TOP].astype(jnp.int32)
    gates_all = small_all[:, :, TOP:]
    seqs = routes_all.shape[0]
    first_expert = exp * held + pair * local
    chosen = routes_all[:, :, :, None] == (first_expert + jnp.arange(local, dtype=jnp.int32))
    member = jnp.any(chosen, axis=2)
    gate_te = jnp.sum(jnp.where(chosen, gates_all[:, :, :, None], 0.0), axis=2)
    places = jnp.arange(length, dtype=jnp.int32)
    earlier = (places[None, :] < places[:, None]).astype(BF16)
    order = jnp.einsum("ut,ste->seu", earlier, member.astype(BF16), preferred_element_type=F32)
    rank = jnp.where(jnp.swapaxes(member, 1, 2), order.astype(jnp.int32), -1)
    hot = jnp.swapaxes(rank, 0, 1)[:, :, None, :] == jnp.arange(CAP, dtype=jnp.int32)[None, None, :, None]
    gate_slot = jnp.sum(jnp.where(hot, jnp.transpose(gate_te, (2, 0, 1))[:, :, None, :], 0.0), axis=-1)
    gate_slot = gate_slot.reshape(local, seqs * CAP, 1)

    flow = Flow()
    normed, inverse_one, query_rot, key_rot, value_rows, mixed, log_total = attend(
        tokens, gain_one, qkv_full, cosine, sine, tagc, tagr
    )
    hidden, normed_two, inverse_two = project(tokens, mixed, o_full, gain_two)
    flow.mark(inverse_two)
    n2_items = gather_now(normed_two)

    rank, gate_slot = flow.after(rank, gate_slot)
    y_rows = collect(rank, dy_items)
    first = jnp.reshape(pair * local, (1,))
    t_rows = flow.mark(upstream_product(first, y_rows, down_weight))
    rank = flow.after(rank)
    x_rows = flow.mark(collect(rank, n2_items))
    info = jnp.stack([pair * local, bit_at(grp, 1)])
    sums, d_rows, d_gate_slots, acts = [], [], [], []
    for e in range(local):
        gate_slot = flow.after(gate_slot)
        theirs, mine, dx, act, d_gate = expert_step(
            e, n_grp, info, x_rows, y_rows, t_rows, gate_slot, gate_weight, up_weight
        )
        flow.mark(d_gate)
        sums.append(GradSum(theirs, mine, flow))
        d_rows.append(dx)
        acts.append(act)
        d_gate_slots.append(d_gate.reshape(seqs, CAP))

    def pump(group):
        if group < local:
            sums[group].step()

    pump(0)
    rank = flow.after(rank)
    far, near = combine(rank, d_rows, width)
    flow.mark(near)
    d_return = Return(far, near, flow)
    first = flow.after(first)
    out_rows = flow.mark(output_rows(first, acts, down_weight))
    d_return.step()
    rank = flow.after(rank)
    far, near = combine(rank, [out_rows], width)
    flow.mark(near)
    out_return = Return(far, near, flow)
    pump(1)
    d_return.step()
    pump(0)
    d_normed_two = d_return.step()

    normal_two = hidden * inverse_two
    upstream = cotangent.astype(F32)
    d_hidden = upstream + norm_backward(d_normed_two, normal_two, inverse_two, gain_two)
    moe_gain_grad = jnp.sum(d_normed_two * normal_two, axis=0)
    d_branch = d_hidden.astype(BF16)
    d_mixed = jnp.einsum("td,id->ti", d_branch, o_full, preferred_element_type=F32).astype(BF16)
    delta = jnp.sum(
        (d_mixed.astype(F32) * mixed.astype(F32)).reshape(length, HEADS, HEAD_DIM), axis=-1
    )
    flow.mark(delta)
    out_return.step()
    d_branch = flow.after(d_branch)
    grad_out = flow.mark(jnp.einsum("ti,td->id", mixed, d_branch, preferred_element_type=F32).astype(BF16))
    o_sum = AllSum(grad_out, flow)
    delta = flow.after(delta)
    d_query, d_key, d_value = attend_back(
        query_rot, key_rot, value_rows, d_mixed,
        log_total.reshape(HEADS, 1, length), delta.T.reshape(HEADS, 1, length),
        cosine, sine, tagc, tagr,
    )
    flow.mark(d_key)
    pump(2)
    pump(1)
    o_sum.step()
    d_query = flow.after(d_query)
    d_qkv = jnp.concatenate([d_query, d_key, d_value], axis=1)
    d_normed = jnp.einsum("tj,ij->ti", d_qkv, qkv_full, preferred_element_type=F32)
    normal_one = tokens.astype(F32) * inverse_one
    attn_gain_grad = jnp.sum(d_normed * normal_one, axis=0)
    tokens_grad = flow.mark(
        (d_hidden + norm_backward(d_normed, normal_one, inverse_one, gain_one)).astype(BF16)
    )
    out_return.step()
    d_qkv = flow.after(d_qkv)
    grad_qkv = jnp.einsum("ti,tj->ij", normed, d_qkv, preferred_element_type=F32).astype(BF16)
    gain_grads = jnp.stack([attn_gain_grad, moe_gain_grad], axis=1).astype(BF16)
    gain_grads = jnp.pad(gain_grads, ((0, 0), (0, 126)))
    grad_qkv = flow.mark(jnp.concatenate([grad_qkv, gain_grads], axis=1))
    qkv_sum = AllSum(grad_qkv, flow)
    qkv_sum.step()
    o_sum.step()
    pump(2)
    qkv_sum.step()
    o_sum.step()
    pump(3)
    qkv_sum.step()
    o_sum.step()
    mixed_out = out_return.step()
    layer_out = (hidden + mixed_out).astype(BF16)

    d_gate_te = jnp.sum(jnp.where(hot, jnp.stack(d_gate_slots)[:, :, :, None], 0.0), axis=2)
    d_gate_te = jnp.transpose(d_gate_te, (1, 2, 0))
    d_gates_all = exchange_small([d_gate_te[i] for i in range(seqs)])
    steps = cluster_steps() + [("grp", PAIR), ("exp", CORE)]
    target_exp, target_pair, inner = routes // held, (routes % held) // local, routes % local
    far = jnp.zeros_like(routes)
    for place, (name, bit) in enumerate(steps):
        if name == "exp":
            differs = bit_at(target_exp, bit) != bit_at(exp, bit)
        else:
            differs = target_pair != pair
        far = far + differs.astype(jnp.int32) * (1 << (len(steps) - 1 - place))
    column = far * local + inner
    d_gates = jnp.sum(
        jnp.where(
            column[:, :, None] == jnp.arange(d_gates_all.shape[1], dtype=jnp.int32),
            d_gates_all[:, None, :],
            0.0,
        ),
        axis=-1,
    )
    logits_grad = gates * (d_gates - jnp.sum(gates * d_gates, axis=-1, keepdims=True))

    while not all(item.done for item in sums):
        for item in sums:
            item.step()
    while qkv_sum.coming is not None:
        qkv_sum.step()
        o_sum.step()

    def finish(kind):
        low, high = [], []
        for group in sums:
            mine, coming = group.mine[kind], group.coming[kind]
            low.append(jnp.where(pair == 0, mine, coming).astype(F32))
            high.append(jnp.where(pair == 0, coming, mine).astype(F32))
        return jnp.stack(low + high)

    return (
        layer_out,
        tokens_grad,
        logits_grad,
        qkv_sum.block[:, :q_width],
        qkv_sum.block[:, q_width : q_width + kv_width],
        qkv_sum.block[:, q_width + kv_width : q_width + 2 * kv_width],
        o_sum.block,
        qkv_sum.block[:, q_width + 2 * kv_width],
        qkv_sum.block[:, q_width + 2 * kv_width + 1],
        finish(0),
        finish(1),
        finish(2),
    )


def solution(mesh):
    rows = P(("grp", "exp"), None)
    placed = (rows,) * 6 + (P("grp", None),) * 4 + (P("grp"),) * 2 + (P("exp", None, None),) * 3
    outs = (rows,) * 7 + (P(("grp", "exp")),) * 2 + (P("exp", "grp", None),) * 3
    return jax.shard_map(shards, mesh=mesh, in_specs=placed, out_specs=outs, check_vma=False)
```

time: 1960 us -> 1200 us (0.61)
  waiting for transfers between devices: 1110 us -> 626 us
  Pallas kernels: 0 us -> 300 us
  matrix products: 314 us -> 23.9 us
  local copies, waits for them, and re-layouts: 197 us -> 52.8 us
  blocking collectives: 133 us -> 0 us
  starting transfers between devices: 25.1 us -> 66.8 us
  other arithmetic: 155 us -> 116 us
    reduce_scatter x7 -> x0, waiting for transfers between devices: 824 us -> none  [the longest x1 312 us: shards(): lax.psum_scatter(grad_up.astype(jnp.bfloat16), 'grp', scatter_dimension=1...]
    ppermute x0 -> x87, waiting for transfers between devices: none -> 626 us  [the longest x73 562 us: swap(): return lax.ppermute(values, axis, [(i, i ^ bit) for i in range(size)])]
    pallas_call x0 -> x15, Pallas kernels: none -> 300 us  [the longest x4 117 us: expert_step(): call(functools.partial(expert_body, expert, n_grp), grid=(1,), in_specs=[...]
    dot_general x27 -> x5, matrix products: 314 us -> 23.9 us  [the longest x1 7.1 us: shards(): jnp.einsum('ti,tj->ij', normed, d_qkv, preferred_element_type=F32)]
    all_to_all x4 -> x0, waiting for transfers between devices: 286 us -> none  [the longest x1 82.7 us: shards(): lax.all_to_all(slot_grad.reshape(n_exp, local_experts, CAP, model_width),...]
    gather x5 -> x2, local copies, waits for them, and re-layouts: 107 us -> 1.22 us  [the longest x1 0.64 us: ring_origins(): return jnp.array(order, jnp.int32)[jnp.stack(ahead + behind)]]
    all_gather x2 -> x0, blocking collectives: 67.8 us -> none  [the longest x1 33.9 us: shards(): lax.all_gather(v_weight, 'grp', axis=0, tiled=True)]
    ppermute x0 -> x87, starting transfers between devices: none -> 66.8 us  [the longest x73 51.1 us: swap(): return lax.ppermute(values, axis, [(i, i ^ bit) for i in range(size)])]
  transfers between devices with their start and end apart: 13 -> 87, of which waited for: 10 -> 43; matrix products, arithmetic and copies ran while one was open for 30% -> 11% of each run, Pallas kernels for 0% -> 18%
where the time goes in v1:
time: 1200 us; the launch traced here: 1190 us
  waiting for transfers between devices  626 us (52%)
  Pallas kernels  300 us (25%)
  other arithmetic  116 us (10%)
  starting transfers between devices  66.8 us (6%)
  local copies, waits for them, and re-layouts  52.8 us (4%)
  matrix products  23.9 us (2%)
    ppermute x73, waiting for transfers between devices, swap(): return lax.ppermute(values, axis, [(i, i ^ bit) for i in range(size)])  562 us
    pallas_call x4, Pallas kernels, expert_step(): call(functools.partial(expert_body, expert, n_grp), grid=(1,), in_specs=[...  117 us
    convert_element_type x20, other arithmetic, add(): return (first.astype(F32) + second.astype(F32)).astype(BF16)  54.1 us
    ppermute x73, starting transfers between devices, swap(): return lax.ppermute(values, axis, [(i, i ^ bit) for i in range(size)])  51.1 us
    ppermute x8, waiting for transfers between devices, ring_pieces(): first.append(lax.ppermute(first[-1], 'grp', onward))  51.1 us
    pallas_call x1, Pallas kernels, attend(): call(attend_body, grid=(pairs,), in_specs=[fixed(length, width), fixed(1,...  38.9 us
    pallas_call x2, Pallas kernels, combine(): call(functools.partial(combine_body, count, local), in_specs=[WHOLE] + [A...  34.9 us
    pallas_call x2, Pallas kernels, collect(): call(functools.partial(collect_body, counts, local), in_specs=[WHOLE] + [...  33.7 us
  transfers between devices with their start and end apart: 87, of which 43 were waited for; matrix products, arithmetic and copies ran while one was open for 11% of the time, Pallas kernels for 18%

profile of v1, /device:TPU:0, one launch (start us, length us, event | category | flops | bytes accessed | tf_op | source)
XLA Modules:
  0.0 1194.6 jit_solution(1454179678178879226)
XLA Ops:
  5.2 9.1 collective-permute-done.4.refs_2_
  16.9 8.5 collective-permute-done.6.refs_4_
  27.6 8.0 collective-permute-done.8.refs_6_
  85.4 52.2 %collective-permute-done.1 = f32[2,2,192]{2,1,0:T(2,128)S(1)} collective-permute-done((f32[2,2,192]{2,1,0:T(2,128)S(1)}, f32[2,2,192]{2,1,0:T(2,128)S(1)}, u32[]{:S(2)}, u32[]{:S(2)}) %collective-permute-start.1) | collective-permute-done | bytes 3104 | tf_op jit(solution)/shard_map/ppermute | solution.py:43
  185.3 38.9 %attend.1 = (bf16[768,1536]{1,0:T(8,128)(2,1)}, f32[768,1]{1,0:T(8,128)}, bf16[768,1536]{1,0:T(8,128)(2,1)}, bf16[768,256]{1,0:T(8,128)(2,1)}, bf16[768,256]{1,0...) custom-call(bf16[768,1536]{1,0:T(8,128)(2,1)} %x_ref.3, f32[1,1536]{1,0:T(1,128)} %reshape_squeeze.6.gain_ref, ...), custom_call_target="tpu_custom_call" | custom-call | flops 1 | bytes 1 | tf_op jit(solution)/shard_map/attend/pallas_call | solution.py:145
  230.4 9.3 project.1
  242.3 51.3 %collective-permute-done.44.refs_2_ = bf16[768,1536]{1,0:T(8,128)(2,1)} collective-permute-done((bf16[768,1536]{1,0:T(8,128)(2,1)}, bf16[768,1536]{1,0:T(8,128)(2,1)}, u32[]{:S(2)}, u32[]{:S(2)}) %collective-permute-start.44) | collective-permute-done | bytes 2359328 | tf_op jit(solution)/shard_map/ppermute | solution.py:43
  295.5 48.7 %collective-permute-done.43.refs_1_ = bf16[768,1536]{1,0:T(8,128)(2,1)} collective-permute-done((bf16[768,1536]{1,0:T(8,128)(2,1)}, bf16[768,1536]{1,0:T(8,128)(2,1)}, u32[]{:S(2)}, u32[]{:S(2)}) %collective-permute-start.43) | collective-permute-done | bytes 2359328 | tf_op jit(solution)/shard_map/ppermute | solution.py:43
  350.2 21.6 %collective-permute-done.45.refs_3_ = bf16[384,1536]{1,0:T(8,128)(2,1)} collective-permute-done((bf16[384,1536]{1,0:T(8,128)(2,1)S(1)}, bf16[384,1536]{1,0:T(8,128)(2,1)}, u32[]{:S(2)}, u32[]{:S(2)}) %collective-permute-start.45) | collective-permute-done | bytes 1179680 | tf_op jit(solution)/shard_map/ppermute | solution.py:43
  380.0 16.9 %collect.2.y_ref.y_hbm = bf16[4,896,1536]{2,1,0:T(8,128)(2,1)} custom-call(s32[8,4,768]{2,1,0:T(4,128)} %get-tuple-element.164.rank_ref.refs_0_, bf16[768,1536]{1,0:T(8,128)(2,1)} %refs_0_, bf16[768,1536]{1,0:T(8,128)(2,1)} %collective-permute-done.36.refs_1_, bf16[768,1536]{1,0:T(8,128)(2,1)} %collective-permute-done.37.refs_2_, ...), custom_call_target="tpu_custom_call" | custom-call | flops 1 | bytes 1 | tf_op jit(solution)/shard_map/collect/pallas_call | solution.py:275
  396.9 15.4 %upstream.1.t_hbm = f32[4,896,768]{2,1,0:T(8,128)} custom-call(s32[1]{0:T(128)} %bitcast.19.first_ref, bf16[4,896,1536]{2,1,0:T(8,128)(2,1)} %collect.2.y_ref.y_hbm, bf16[8,1536,768]{2,1,0:T(8,128)(2,1)} %refs_4_.1), custom_call_target="tpu_custom_call" | custom-call | flops 1 | bytes 1 | tf_op jit(solution)/shard_map/upstream/pallas_call | solution.py:377
  413.7 16.9 %collect.3.x_hbm = bf16[4,896,1536]{2,1,0:T(8,128)(2,1)} custom-call(s32[8,4,768]{2,1,0:T(4,128)} %get-tuple-element.164.rank_ref.refs_0_, bf16[768,1536]{1,0:T(8,128)(2,1)} %get-tuple-element.134.refs_0_, bf16[768,1536]{1,0:T(8,128)(2,1)} %collective-permute-done.43.refs_1_, bf16[768,1536]{1,0:T(8,128)(2,1)} %collective-permute-done.44.refs_2_, ...), custom_call_target="tpu_custom_call" | custom-call | flops 1 | bytes 1 | tf_op jit(solution)/shard_map/collect/pallas_call | solution.py:275
  432.4 29.3 %expert.4 = (bf16[3,768,768]{2,1,0:T(8,128)(2,1)}, bf16[3,768,768]{2,1,0:T(8,128)(2,1)}, bf16[896,1536]{1,0:T(8,128)(2,1)}, bf16[896,768]{1,0:T(8,128)(2,1)}, f32[896,1]{1,0:T(8,128)}) custom-call(s32[2]{0:T(128)} %pad_add_fusion.1.info_ref, bf16[4,896,1536]{2,1,0:T(8,128)(2,1)} %collect.3.x_hbm, bf16[4,896,1536]{2,1,0:T(8,128)(2,1)} %collect.2.y_ref.y_hbm, ...), custom_call_target="tpu_custom_call" | custom-call | flops 1 | bytes 1 | tf_op jit(solution)/shard_map/expert/pallas_call | solution.py:526
  464.7 29.3 %expert.5 = (bf16[3,768,768]{2,1,0:T(8,128)(2,1)}, bf16[3,768,768]{2,1,0:T(8,128)(2,1)}, bf16[896,1536]{1,0:T(8,128)(2,1)}, bf16[896,768]{1,0:T(8,128)(2,1)}, f32[896,1]{1,0:T(8,128)}) custom-call(s32[2]{0:T(128)} %pad_add_fusion.1.info_ref, bf16[4,896,1536]{2,1,0:T(8,128)(2,1)} %collect.3.x_hbm, bf16[4,896,1536]{2,1,0:T(8,128)(2,1)} %collect.2.y_ref.y_hbm, ...), custom_call_target="tpu_custom_call" | custom-call | flops 1 | bytes 1 | tf_op jit(solution)/shard_map/expert/pallas_call | solution.py:526
  495.8 29.4 %expert.6 = (bf16[3,768,768]{2,1,0:T(8,128)(2,1)}, bf16[3,768,768]{2,1,0:T(8,128)(2,1)}, bf16[896,1536]{1,0:T(8,128)(2,1)}, bf16[896,768]{1,0:T(8,128)(2,1)}, f32[896,1]{1,0:T(8,128)}) custom-call(s32[2]{0:T(128)} %pad_add_fusion.1.info_ref, bf16[4,896,1536]{2,1,0:T(8,128)(2,1)} %collect.3.x_hbm, bf16[4,896,1536]{2,1,0:T(8,128)(2,1)} %collect.2.y_ref.y_hbm, ...), custom_call_target="tpu_custom_call" | custom-call | flops 1 | bytes 1 | tf_op jit(solution)/shard_map/expert/pallas_call | solution.py:526
  527.0 29.5 %expert.7 = (bf16[3,768,768]{2,1,0:T(8,128)(2,1)}, bf16[3,768,768]{2,1,0:T(8,128)(2,1)}, bf16[896,1536]{1,0:T(8,128)(2,1)}, bf16[896,768]{1,0:T(8,128)(2,1)}, f32[896,1]{1,0:T(8,128)}) custom-call(s32[2]{0:T(128)} %pad_add_fusion.1.info_ref, bf16[4,896,1536]{2,1,0:T(8,128)(2,1)} %collect.3.x_hbm, bf16[4,896,1536]{2,1,0:T(8,128)(2,1)} %collect.2.y_ref.y_hbm, ...), custom_call_target="tpu_custom_call" | custom-call | flops 1 | bytes 1 | tf_op jit(solution)/shard_map/expert/pallas_call | solution.py:526
  561.2 17.4 %combine.2 = (bf16[4,768,1536]{2,1,0:T(8,128)(2,1)}, bf16[4,768,1536]{2,1,0:T(8,128)(2,1)}) custom-call(s32[8,4,768]{2,1,0:T(4,128)} %get-tuple-element.164.rank_ref.refs_0_, bf16[896,1536]{1,0:T(8,128)(2,1)} %get-tuple-element.149.refs_1_, bf16[896,1536]{1,0:T(8,128)(2,1)} %get-tuple-element.150.refs_2_, bf16[896,1536]{1,0:T(8,128)(2,1)} %get-tuple-element.151.refs_3_, ...), custom_call_target="tpu_custom_call" | custom-call | flops 1 | bytes 1 | tf_op jit(solution)/shard_map/combine/pallas_call | solution.py:346
  578.9 14.9 %output.1.refs_1_ = bf16[4,896,1536]{2,1,0:T(8,128)(2,1)} custom-call(s32[1]{0:T(128)} %bitcast.19.first_ref, bf16[896,768]{1,0:T(8,128)(2,1)} %get-tuple-element.156.refs_0_, bf16[896,768]{1,0:T(8,128)(2,1)} %get-tuple-element.157.refs_1_, bf16[896,768]{1,0:T(8,128)(2,1)} %get-tuple-element.158.refs_2_, bf16[896,768]{1,0:T(8,128)(2,1)} %get-tuple-element.159.refs_3_, ...), custom_call_target="tpu_custom_call" | custom-call | flops 1 | bytes 1 | tf_op jit(solution)/shard_map/output/pallas_call | solution.py:402
  599.6 17.5 %combine.3 = (bf16[4,768,1536]{2,1,0:T(8,128)(2,1)}, bf16[4,768,1536]{2,1,0:T(8,128)(2,1)}) custom-call(s32[8,4,768]{2,1,0:T(4,128)} %get-tuple-element.164.rank_ref.refs_0_, bf16[4,896,1536]{2,1,0:T(8,128)(2,1)} %output.1.refs_1_), custom_call_target="tpu_custom_call" | custom-call | flops 1 | bytes 1 | tf_op jit(solution)/shard_map/combine/pallas_call | solution.py:346
  624.3 72.1 %collective-permute-done.57 = bf16[3,768,768]{2,1,0:T(8,128)(2,1)} collective-permute-done((bf16[3,768,768]{2,1,0:T(8,128)(2,1)}, bf16[3,768,768]{2,1,0:T(8,128)(2,1)}, u32[]{:S(2)}, u32[]{:S(2)}) %collective-permute-start.57) | collective-permute-done | bytes 3538976 | tf_op jit(solution)/shard_map/ppermute | solution.py:43
  701.1 8.6 collective-permute-done.55
  720.4 22.0 %collective-permute-done.58 = bf16[1,384,1536]{2,1,0:T(8,128)(2,1)} collective-permute-done((bf16[1,384,1536]{2,1,0:T(8,128)(2,1)}, bf16[1,384,1536]{2,1,0:T(8,128)(2,1)}, u32[]{:S(2)}, u32[]{:S(2)}) %collective-permute-start.58) | collective-permute-done | bytes 1179680 | tf_op jit(solution)/shard_map/ppermute | solution.py:43
  791.7 24.0 %attend_back.1 = (bf16[768,1536]{1,0:T(8,128)(2,1)}, bf16[768,256]{1,0:T(8,128)(2,1)}, bf16[768,256]{1,0:T(8,128)(2,1)}) custom-call(bf16[768,1536]{1,0:T(8,128)(2,1)} %get-tuple-element.188.q_ref, bf16[768,256]{1,0:T(8,128)(2,1)} %get-tuple-element.189.k_ref, bf16[768,256]{1,0:T(8,128)(2,1)} %get-tuple-element.190.v_ref, ...), custom_call_target="tpu_custom_call" | custom-call | flops 1 | bytes 1 | tf_op jit(solution)/shard_map/attend_back/pallas_call | solution.py:605
  821.3 40.4 %collective-permute-done.64 = bf16[3,2,192,768]{3,2,1,0:T(8,128)(2,1)} collective-permute-done((bf16[3,2,192,768]{3,2,1,0:T(8,128)(2,1)}, bf16[3,2,192,768]{3,2,1,0:T(8,128)(2,1)}, u32[]{:S(2)}, u32[]{:S(2)}) %collective-permute-start.64) | collective-permute-done | bytes 1769504 | tf_op jit(solution)/shard_map/ppermute | solution.py:43
  928.1 18.5 %collective-permute-done.68 = bf16[2,2,2,48,1536]{4,3,2,1,0:T(8,128)(2,1)S(1)} collective-permute-done((bf16[2,2,2,48,1536]{4,3,2,1,0:T(8,128)(2,1)S(1)}, bf16[2,2,2,48,1536]{4,3,2,1,0:T(8,128)(2,1)S(1)}, u32[]{:S(2)}, u32[]{:S(2)}) %collective-permute-start.68) | collective-permute-done | bytes 1179680 | tf_op jit(solution)/shard_map/ppermute | solution.py:43
  947.2 54.4 %collective-permute-done.72 = bf16[3,2,192,768]{3,2,1,0:T(8,128)(2,1)S(1)} collective-permute-done((bf16[3,2,192,768]{3,2,1,0:T(8,128)(2,1)S(1)}, bf16[3,2,192,768]{3,2,1,0:T(8,128)(2,1)S(1)}, u32[]{:S(2)}, u32[]{:S(2)}) %collective-permute-start.72) | collective-permute-done | bytes 1769504 | tf_op jit(solution)/shard_map/ppermute | solution.py:43
  1007.3 18.6 %collective-permute-done.85 = bf16[3,192,768]{2,1,0:T(8,128)(2,1)S(1)} collective-permute-done((bf16[3,192,768]{2,1,0:T(8,128)(2,1)S(1)}, bf16[3,192,768]{2,1,0:T(8,128)(2,1)S(1)}, u32[]{:S(2)}, u32[]{:S(2)}) %collective-permute-start.85) | collective-permute-done | bytes 884768 | tf_op jit(solution)/shard_map/ppermute | solution.py:43
  1025.9 15.2 %collective-permute-done.71 = bf16[2,2,2,48,2176]{4,3,2,1,0:T(8,128)(2,1)S(1)} collective-permute-done((bf16[2,2,2,48,2176]{4,3,2,1,0:T(8,128)(2,1)S(1)}, bf16[2,2,2,48,2176]{4,3,2,1,0:T(8,128)(2,1)S(1)}, u32[]{:S(2)}, u32[]{:S(2)}) %collective-permute-start.71) | collective-permute-done | bytes 1671200 | tf_op jit(solution)/shard_map/ppermute | solution.py:43
  1041.5 27.7 %collective-permute-done.70 = bf16[2,2,48,1536]{3,2,1,0:T(8,128)(2,1)S(1)} collective-permute-done((bf16[2,2,48,1536]{3,2,1,0:T(8,128)(2,1)S(1)}, bf16[2,2,48,1536]{3,2,1,0:T(8,128)(2,1)S(1)}, u32[]{:S(2)}, u32[]{:S(2)}) %collective-permute-start.70) | collective-permute-done | bytes 589856 | tf_op jit(solution)/shard_map/ppermute | solution.py:43
  1073.9 20.9 %collective-permute-done.74 = bf16[2,2,48,2176]{3,2,1,0:T(8,128)(2,1)S(1)} collective-permute-done((bf16[2,2,48,2176]{3,2,1,0:T(8,128)(2,1)S(1)}, bf16[2,2,48,2176]{3,2,1,0:T(8,128)(2,1)S(1)}, u32[]{:S(2)}, u32[]{:S(2)}) %collective-permute-start.74) | collective-permute-done | bytes 835616 | tf_op jit(solution)/shard_map/ppermute | solution.py:43
  1107.7 53.8 %collective-permute-done.80 = bf16[3,2,192,768]{3,2,1,0:T(8,128)(2,1)} collective-permute-done((bf16[3,2,192,768]{3,2,1,0:T(8,128)(2,1)S(1)}, bf16[3,2,192,768]{3,2,1,0:T(8,128)(2,1)}, u32[]{:S(2)}, u32[]{:S(2)}) %collective-permute-start.80) | collective-permute-done | bytes 1769504 | tf_op jit(solution)/shard_map/ppermute | solution.py:43
  1174.0 10.6 collective-permute-done.86
  (480 shorter events, 334.6 us)
Async XLA Ops:
  73.9 73.5 %collective-permute-start.3 = (bf16[192,1024]{1,0:T(8,128)(2,1)S(1)}, bf16[192,1024]{1,0:T(8,128)(2,1)}, u32[]{:S(2)}, u32[]{:S(2)}) collective-permute-start(bf16[192,1024]{1,0:T(8,128)(2,1)S(1)} %fusion.22.refs_0_), channel_id=1, source_target_pairs={{0,1},{1,0},{2,3},{3,2},{4,5},{5,4},{6,7},{7,6},{8,9},{9,8},{10,11... | collective-permute-start | bytes 1179656 | tf_op jit(solution)/shard_map/ppermute | solution.py:43
  79.7 160.0 %collective-permute-start.37 = (bf16[768,1536]{1,0:T(8,128)(2,1)S(1)}, bf16[768,1536]{1,0:T(8,128)(2,1)}, u32[]{:S(2)}, u32[]{:S(2)}) collective-permute-start(bf16[768,1536]{1,0:T(8,128)(2,1)S(1)} %copy-done.8), channel_id=1, source_target_pairs={{0,8},{4,12},{8,0},{12,4},{16,24},{20,28},{24,16},{28,20},{1,9},{5... | collective-permute-start | bytes 7077896 | tf_op jit(solution)/shard_map/ppermute | solution.py:43
  82.1 65.9 %collective-permute-start.13 = (bf16[192,1024]{1,0:T(8,128)(2,1)S(1)}, bf16[192,1024]{1,0:T(8,128)(2,1)}, u32[]{:S(2)}, u32[]{:S(2)}) collective-permute-start(bf16[192,1024]{1,0:T(8,128)(2,1)S(1)} %collective-permute-done.12.refs_10_), channel_id=1, source_target_pairs={{0,1},{1,0},{2,3},{3,2},{4,5},{5,4},{6,7},{7,6},{8,9},{9,8},{10,11... | collective-permute-start | bytes 1179656 | tf_op jit(solution)/shard_map/ppermute | solution.py:43
  82.1 66.0 %collective-permute-start.16 = (bf16[192,1024]{1,0:T(8,128)(2,1)}, bf16[192,1024]{1,0:T(8,128)(2,1)}, u32[]{:S(2)}, u32[]{:S(2)}) collective-permute-start(bf16[192,1024]{1,0:T(8,128)(2,1)} %collective-permute-done.14.refs_12_), channel_id=1, source_target_pairs={{8,0},{16,8},{24,16},{28,24},{20,28},{12,20},{4,12},{0,4},{9,1},{1... | collective-permute-start | bytes 1179656 | tf_op jit(solution)/shard_map/ppermute | solution.py:747
  151.6 90.1 %collective-permute-start.36 = (bf16[768,1536]{1,0:T(8,128)(2,1)S(1)}, bf16[768,1536]{1,0:T(8,128)(2,1)}, u32[]{:S(2)}, u32[]{:S(2)}) collective-permute-start(bf16[768,1536]{1,0:T(8,128)(2,1)S(1)} %copy-done.8), channel_id=1, source_target_pairs={{0,2},{1,3},{2,0},{3,1},{4,6},{5,7},{6,4},{7,5},{8,10},{9,11},{10,... | collective-permute-start | bytes 7077896 | tf_op jit(solution)/shard_map/ppermute | solution.py:43
  239.7 54.4 %collective-permute-start.38 = (bf16[768,1536]{1,0:T(8,128)(2,1)}, bf16[768,1536]{1,0:T(8,128)(2,1)}, u32[]{:S(2)}, u32[]{:S(2)}) collective-permute-start(bf16[768,1536]{1,0:T(8,128)(2,1)} %collective-permute-done.37.refs_2_), channel_id=1, source_target_pairs={{0,2},{1,3},{2,0},{3,1},{4,6},{5,7},{6,4},{7,5},{8,10},{9,11},{10,... | collective-permute-start | bytes 7077896 | tf_op jit(solution)/shard_map/ppermute | solution.py:43
  241.3 103.0 %collective-permute-start.43 = (bf16[768,1536]{1,0:T(8,128)(2,1)}, bf16[768,1536]{1,0:T(8,128)(2,1)}, u32[]{:S(2)}, u32[]{:S(2)}) collective-permute-start(bf16[768,1536]{1,0:T(8,128)(2,1)} %get-tuple-element.134.refs_0_), channel_id=1, source_target_pairs={{0,2},{1,3},{2,0},{3,1},{4,6},{5,7},{6,4},{7,5},{8,10},{9,11},{10,... | collective-permute-start | bytes 7077896 | tf_op jit(solution)/shard_map/ppermute | solution.py:43
  241.8 105.3 %collective-permute-start.39 = (bf16[768,1536]{1,0:T(8,128)(2,1)S(1)}, bf16[768,1536]{1,0:T(8,128)(2,1)S(1)}, u32[]{:S(2)}, u32[]{:S(2)}) collective-permute-start(bf16[768,1536]{1,0:T(8,128)(2,1)S(1)} %copy-done.8), channel_id=1, source_target_pairs={{0,1},{1,0},{2,3},{3,2},{4,5},{5,4},{6,7},{7,6},{8,9},{9,8},{10,11... | collective-permute-start | bytes 7077896 | tf_op jit(solution)/shard_map/ppermute | solution.py:43
  241.8 108.4 %collective-permute-start.40 = (bf16[768,1536]{1,0:T(8,128)(2,1)}, bf16[768,1536]{1,0:T(8,128)(2,1)}, u32[]{:S(2)}, u32[]{:S(2)}) collective-permute-start(bf16[768,1536]{1,0:T(8,128)(2,1)} %collective-permute-done.36.refs_1_), channel_id=1, source_target_pairs={{0,1},{1,0},{2,3},{3,2},{4,5},{5,4},{6,7},{7,6},{8,9},{9,8},{10,11... | collective-permute-start | bytes 7077896 | tf_op jit(solution)/shard_map/ppermute | solution.py:43
  293.6 83.0 %collective-permute-start.41 = (bf16[768,1536]{1,0:T(8,128)(2,1)}, bf16[768,1536]{1,0:T(8,128)(2,1)}, u32[]{:S(2)}, u32[]{:S(2)}) collective-permute-start(bf16[768,1536]{1,0:T(8,128)(2,1)} %collective-permute-done.37.refs_2_), channel_id=1, source_target_pairs={{0,1},{1,0},{2,3},{3,2},{4,5},{5,4},{6,7},{7,6},{8,9},{9,8},{10,11... | collective-permute-start | bytes 7077896 | tf_op jit(solution)/shard_map/ppermute | solution.py:43
  294.1 82.9 %collective-permute-start.42 = (bf16[768,1536]{1,0:T(8,128)(2,1)}, bf16[768,1536]{1,0:T(8,128)(2,1)}, u32[]{:S(2)}, u32[]{:S(2)}) collective-permute-start(bf16[768,1536]{1,0:T(8,128)(2,1)} %collective-permute-done.38.refs_3_), channel_id=1, source_target_pairs={{0,1},{1,0},{2,3},{3,2},{4,5},{5,4},{6,7},{7,6},{8,9},{9,8},{10,11... | collective-permute-start | bytes 7077896 | tf_op jit(solution)/shard_map/ppermute | solution.py:43
  350.2 62.1 %collective-permute-start.47 = (bf16[768,1536]{1,0:T(8,128)(2,1)}, bf16[768,1536]{1,0:T(8,128)(2,1)S(1)}, u32[]{:S(2)}, u32[]{:S(2)}) collective-permute-start(bf16[768,1536]{1,0:T(8,128)(2,1)} %get-tuple-element.134.refs_0_), channel_id=1, source_target_pairs={{0,1},{1,0},{2,3},{3,2},{4,5},{5,4},{6,7},{7,6},{8,9},{9,8},{10,11... | collective-permute-start | bytes 7077896 | tf_op jit(solution)/shard_map/ppermute | solution.py:43
  461.7 94.9 %collective-permute-start.52 = (bf16[3,768,768]{2,1,0:T(8,128)(2,1)}, bf16[3,768,768]{2,1,0:T(8,128)(2,1)}, u32[]{:S(2)}, u32[]{:S(2)}) collective-permute-start(bf16[3,768,768]{2,1,0:T(8,128)(2,1)} %get-tuple-element.138), channel_id=1, source_target_pairs={{0,4},{4,0},{8,12},{12,8},{16,20},{20,16},{24,28},{28,24},{1,5},{5... | collective-permute-start | bytes 10616840 | tf_op jit(solution)/shard_map/ppermute | solution.py:43
  617.1 150.4 %collective-permute-start.54 = (bf16[4,768,1536]{2,1,0:T(8,128)(2,1)}, bf16[4,768,1536]{2,1,0:T(8,128)(2,1)}, u32[]{:S(2)}, u32[]{:S(2)}) collective-permute-start(bf16[4,768,1536]{2,1,0:T(8,128)(2,1)} %get-tuple-element.166), channel_id=1, source_target_pairs={{0,1},{1,0},{2,3},{3,2},{4,5},{5,4},{6,7},{7,6},{8,9},{9,8},{10,11... | collective-permute-start | bytes 28311560 | tf_op jit(solution)/shard_map/ppermute | solution.py:43
  617.5 78.9 %collective-permute-start.57 = (bf16[3,768,768]{2,1,0:T(8,128)(2,1)}, bf16[3,768,768]{2,1,0:T(8,128)(2,1)}, u32[]{:S(2)}, u32[]{:S(2)}) collective-permute-start(bf16[3,768,768]{2,1,0:T(8,128)(2,1)} %get-tuple-element.170), channel_id=1, source_target_pairs={{0,4},{4,0},{8,12},{12,8},{16,20},{20,16},{24,28},{28,24},{1,5},{5... | collective-permute-start | bytes 10616840 | tf_op jit(solution)/shard_map/ppermute | solution.py:43
  618.4 91.3 %collective-permute-start.55 = (bf16[2,1,384,1536]{3,2,1,0:T(8,128)(2,1)}, bf16[2,1,384,1536]{3,2,1,0:T(8,128)(2,1)}, u32[]{:S(2)}, u32[]{:S(2)}) collective-permute-start(bf16[2,1,384,1536]{3,2,1,0:T(8,128)(2,1)} %get-tuple-element.162), channel_id=1, source_target_pairs={{0,8},{4,12},{8,0},{12,4},{16,24},{20,28},{24,16},{28,20},{1,9},{5... | collective-permute-start | bytes 7077896 | tf_op jit(solution)/shard_map/ppermute | solution.py:43
  619.7 90.0 %collective-permute-start.56 = (bf16[2,1,384,1536]{3,2,1,0:T(8,128)(2,1)}, bf16[2,1,384,1536]{3,2,1,0:T(8,128)(2,1)}, u32[]{:S(2)}, u32[]{:S(2)}) collective-permute-start(bf16[2,1,384,1536]{3,2,1,0:T(8,128)(2,1)} %get-tuple-element.163), channel_id=1, source_target_pairs={{0,2},{1,3},{2,0},{3,1},{4,6},{5,7},{6,4},{7,5},{8,10},{9,11},{10,... | collective-permute-start | bytes 7077896 | tf_op jit(solution)/shard_map/ppermute | solution.py:43
  623.9 93.3 %collective-permute-start.60 = (bf16[3,2,192,768]{3,2,1,0:T(8,128)(2,1)}, bf16[3,2,192,768]{3,2,1,0:T(8,128)(2,1)}, u32[]{:S(2)}, u32[]{:S(2)}) collective-permute-start(bf16[3,2,192,768]{3,2,1,0:T(8,128)(2,1)} %get-tuple-element.272), channel_id=1, source_target_pairs={{0,16},{4,20},{8,24},{12,28},{16,0},{20,4},{24,8},{28,12},{1,17},{... | collective-permute-start | bytes 5308424 | tf_op jit(solution)/shard_map/ppermute | solution.py:43
  715.9 99.7 %collective-permute-start.65 = (bf16[3,768,768]{2,1,0:T(8,128)(2,1)}, bf16[3,768,768]{2,1,0:T(8,128)(2,1)}, u32[]{:S(2)}, u32[]{:S(2)}) collective-permute-start(bf16[3,768,768]{2,1,0:T(8,128)(2,1)} %get-tuple-element.196), channel_id=1, source_target_pairs={{0,4},{4,0},{8,12},{12,8},{16,20},{20,16},{24,28},{28,24},{1,5},{5... | collective-permute-start | bytes 10616840 | tf_op jit(solution)/shard_map/ppermute | solution.py:43
  779.7 85.7 %collective-permute-start.63 = (bf16[2,2,2,2,48,1536]{5,4,2,1,0,3:T(8,128)(2,1)}, bf16[2,2,2,2,48,1536]{5,4,2,1,0,3:T(8,128)(2,1)}, u32[]{:S(2)}, u32[]{:S(2)}) collective-permute-start(bf16[2,2,2,2,48,1536]{5,4,2,1,0,3:T(8,128)(2,1)} %bitcast.254), channel_id=1, source_target_pairs={{0,1},{1,0},{2,3},{3,2},{4,5},{5,4},{6,7},{7,6},{8,9},{9,8},{10,11... | collective-permute-start | bytes 7077896 | tf_op jit(solution)/shard_map/ppermute | solution.py:43
  783.1 78.7 %collective-permute-start.64 = (bf16[3,2,192,768]{3,2,1,0:T(8,128)(2,1)}, bf16[3,2,192,768]{3,2,1,0:T(8,128)(2,1)}, u32[]{:S(2)}, u32[]{:S(2)}) collective-permute-start(bf16[3,2,192,768]{3,2,1,0:T(8,128)(2,1)} %get-tuple-element.270), channel_id=1, source_target_pairs={{0,16},{4,20},{8,24},{12,28},{16,0},{20,4},{24,8},{28,12},{1,17},{... | collective-permute-start | bytes 5308424 | tf_op jit(solution)/shard_map/ppermute | solution.py:43
  787.7 91.7 %collective-permute-start.61 = (bf16[2,1,384,1536]{3,2,1,0:T(8,128)(2,1)}, bf16[2,1,384,1536]{3,2,1,0:T(8,128)(2,1)}, u32[]{:S(2)}, u32[]{:S(2)}) collective-permute-start(bf16[2,1,384,1536]{3,2,1,0:T(8,128)(2,1)} %get-tuple-element.183), channel_id=1, source_target_pairs={{0,8},{4,12},{8,0},{12,4},{16,24},{20,28},{24,16},{28,20},{1,9},{5... | collective-permute-start | bytes 7077896 | tf_op jit(solution)/shard_map/ppermute | solution.py:43
  789.5 90.0 %collective-permute-start.62 = (bf16[2,1,384,1536]{3,2,1,0:T(8,128)(2,1)}, bf16[2,1,384,1536]{3,2,1,0:T(8,128)(2,1)}, u32[]{:S(2)}, u32[]{:S(2)}) collective-permute-start(bf16[2,1,384,1536]{3,2,1,0:T(8,128)(2,1)} %get-tuple-element.184), channel_id=1, source_target_pairs={{0,2},{1,3},{2,0},{3,1},{4,6},{5,7},{6,4},{7,5},{8,10},{9,11},{10,... | collective-permute-start | bytes 7077896 | tf_op jit(solution)/shard_map/ppermute | solution.py:43
  914.8 154.7 %collective-permute-start.75 = (bf16[3,768,768]{2,1,0:T(8,128)(2,1)}, bf16[3,768,768]{2,1,0:T(8,128)(2,1)S(1)}, u32[]{:S(2)}, u32[]{:S(2)}) collective-permute-start(bf16[3,768,768]{2,1,0:T(8,128)(2,1)} %get-tuple-element.223), channel_id=1, source_target_pairs={{0,4},{4,0},{8,12},{12,8},{16,20},{20,16},{24,28},{28,24},{1,5},{5... | collective-permute-start | bytes 10616840 | tf_op jit(solution)/shard_map/ppermute | solution.py:43
  918.8 85.1 %collective-permute-start.83 = (bf16[3,192,768]{2,1,0:T(8,128)(2,1)S(1)}, bf16[3,192,768]{2,1,0:T(8,128)(2,1)S(1)}, u32[]{:S(2)}, u32[]{:S(2)}) collective-permute-start(bf16[3,192,768]{2,1,0:T(8,128)(2,1)S(1)} %dynamic-slice_bitcast_fusion.15), channel_id=1, source_target_pairs={{0,8},{4,12},{8,0},{12,4},{16,24},{20,28},{24,16},{28,20},{1,9},{5... | collective-permute-start | bytes 2654216 | tf_op jit(solution)/shard_map/ppermute | solution.py:43
  919.1 84.8 %collective-permute-start.84 = (bf16[3,192,768]{2,1,0:T(8,128)(2,1)S(1)}, bf16[3,192,768]{2,1,0:T(8,128)(2,1)S(1)}, u32[]{:S(2)}, u32[]{:S(2)}) collective-permute-start(bf16[3,192,768]{2,1,0:T(8,128)(2,1)S(1)} %dynamic-slice_bitcast_fusion.14), channel_id=1, source_target_pairs={{0,8},{4,12},{8,0},{12,4},{16,24},{20,28},{24,16},{28,20},{1,9},{5... | collective-permute-start | bytes 2654216 | tf_op jit(solution)/shard_map/ppermute | solution.py:43
  925.0 76.7 %collective-permute-start.72 = (bf16[3,2,192,768]{3,2,1,0:T(8,128)(2,1)S(1)}, bf16[3,2,192,768]{3,2,1,0:T(8,128)(2,1)S(1)}, u32[]{:S(2)}, u32[]{:S(2)}) collective-permute-start(bf16[3,2,192,768]{3,2,1,0:T(8,128)(2,1)S(1)} %get-tuple-element.268), channel_id=1, source_target_pairs={{0,16},{4,20},{8,24},{12,28},{16,0},{20,4},{24,8},{28,12},{1,17},{... | collective-permute-start | bytes 5308424 | tf_op jit(solution)/shard_map/ppermute | solution.py:43
  1004.1 91.1 %collective-permute-start.66 = (bf16[1,384,1536]{2,1,0:T(8,128)(2,1)}, bf16[1,384,1536]{2,1,0:T(8,128)(2,1)}, u32[]{:S(2)}, u32[]{:S(2)}) collective-permute-start(bf16[1,384,1536]{2,1,0:T(8,128)(2,1)} %get-tuple-element.208), channel_id=1, source_target_pairs={{0,2},{1,3},{2,0},{3,1},{4,6},{5,7},{6,4},{7,5},{8,10},{9,11},{10,... | collective-permute-start | bytes 3538952 | tf_op jit(solution)/shard_map/ppermute | solution.py:43
  1005.2 90.0 %collective-permute-start.67 = (bf16[1,384,1536]{2,1,0:T(8,128)(2,1)S(1)}, bf16[1,384,1536]{2,1,0:T(8,128)(2,1)}, u32[]{:S(2)}, u32[]{:S(2)}) collective-permute-start(bf16[1,384,1536]{2,1,0:T(8,128)(2,1)S(1)} %get-tuple-element.209), channel_id=1, source_target_pairs={{0,8},{4,12},{8,0},{12,4},{16,24},{20,28},{24,16},{28,20},{1,9},{5... | collective-permute-start | bytes 3538952 | tf_op jit(solution)/shard_map/ppermute | solution.py:43
  1073.7 87.7 %collective-permute-start.80 = (bf16[3,2,192,768]{3,2,1,0:T(8,128)(2,1)S(1)}, bf16[3,2,192,768]{3,2,1,0:T(8,128)(2,1)}, u32[]{:S(2)}, u32[]{:S(2)}) collective-permute-start(bf16[3,2,192,768]{3,2,1,0:T(8,128)(2,1)S(1)} %get-tuple-element.266), channel_id=1, source_target_pairs={{0,16},{4,20},{8,24},{12,28},{16,0},{20,4},{24,8},{28,12},{1,17},{... | collective-permute-start | bytes 5308424 | tf_op jit(solution)/shard_map/ppermute | solution.py:43
  1095.2 70.8 %collective-permute-start.82 = (bf16[48,1536]{1,0:T(8,128)(2,1)S(1)}, bf16[48,1536]{1,0:T(8,128)(2,1)S(1)}, u32[]{:S(2)}, u32[]{:S(2)}) collective-permute-start(bf16[48,1536]{1,0:T(8,128)(2,1)S(1)} %get-tuple-element.310), channel_id=1, source_target_pairs={{0,4},{4,0},{8,12},{12,8},{16,20},{20,16},{24,28},{28,24},{1,5},{5... | collective-permute-start | bytes 442376 | tf_op jit(solution)/shard_map/ppermute | solution.py:43
  1096.9 68.9 %collective-permute-start.79 = (bf16[2,48,2176]{2,1,0:T(8,128)(2,1)S(1)}, bf16[2,48,2176]{2,1,0:T(8,128)(2,1)S(1)}, u32[]{:S(2)}, u32[]{:S(2)}) collective-permute-start(bf16[2,48,2176]{2,1,0:T(8,128)(2,1)S(1)} %get-tuple-element.302), channel_id=1, source_target_pairs={{0,16},{4,20},{8,24},{12,28},{16,0},{20,4},{24,8},{28,12},{1,17},{... | collective-permute-start | bytes 1253384 | tf_op jit(solution)/shard_map/ppermute | solution.py:43
  (132 other events, 2742.7 us)

commit v2 on v0

v2 whole, which is shorter than its diff:
```python
import functools
from types import SimpleNamespace

import jax
import jax.numpy as jnp
import numpy as np
from jax import lax
from jax.experimental import pallas as pl
from jax.experimental.pallas import tpu as pltpu
from jax.sharding import PartitionSpec as P

HEADS = 12
KV_HEADS = 2
HEAD_DIM = 128
EXPERTS = 32
TOP = 4
CAP = 112
EPSILON = 1e-06
THETA = 1000000.0
SCALE = HEAD_DIM ** (-0.5)
GRP = "grp"
EXP = "exp"
CORE = 1
PAIR = 2
VMEM = 58 * 1024 * 1024
BF16 = jnp.bfloat16
F32 = jnp.float32


def bits_of(size):
    return [1 << i for i in range(size.bit_length() - 1)]


def bit_at(index, bit):
    return lax.rem(lax.div(index, jnp.int32(bit)), jnp.int32(2))


def space(tree):
    if isinstance(tree, dict):
        return SimpleNamespace(**{name: space(value) for name, value in tree.items()})
    return [space(value) for value in tree] if isinstance(tree, list) else tree


def rope_tables(length):
    half = HEAD_DIM // 2
    frequency = THETA ** (-2.0 * np.arange(half) / HEAD_DIM)
    angles = np.arange(length)[:, None] * frequency[None, :]
    cosine, sine = np.cos(angles), np.sin(angles)
    tables = [np.concatenate([cosine, cosine], axis=1), np.concatenate([-sine, sine], axis=1)]
    return [jnp.asarray(table.astype(np.float32)) for table in tables]


def piece_tags(starts, kinds, length):
    places = jnp.arange(length, dtype=jnp.int32)
    piece_of = jnp.sum((places[:, None] >= starts[None, :]).astype(jnp.int32), axis=1) - 1
    slot_ids = jnp.arange(starts.shape[0], dtype=jnp.int32)
    kind_of = jnp.sum(jnp.where(piece_of[:, None] == slot_ids[None, :], kinds[None, :], 0), axis=1)
    return jnp.where(kind_of == 1, piece_of + 1, 0)


def call(body, **kw):
    params = pltpu.CompilerParams(vmem_limit_bytes=VMEM)
    cost = pl.CostEstimate(flops=1, bytes_accessed=1, transcendentals=0)
    return pl.pallas_call(body, compiler_params=params, cost_estimate=cost, **kw)


def shape(*dims, dtype=BF16):
    return jax.ShapeDtypeStruct(dims, dtype)


def dot(a, b, ca=1, cb=0):
    return lax.dot_general(a, b, (((ca,), (cb,)), ((), ())), preferred_element_type=F32)


ANY = pl.BlockSpec(memory_space=pl.ANY)
WHOLE = pl.BlockSpec(memory_space=pltpu.VMEM)
SCALAR = pl.BlockSpec(memory_space=pltpu.SMEM)


def fixed(*dims):
    return pl.BlockSpec(dims, lambda *_: (0,) * len(dims))


def shape(*dims, dtype=BF16):
    return jax.ShapeDtypeStruct(dims, dtype)


def dot(a, b, ca=1, cb=0):
    return lax.dot_general(a, b, (((ca,), (cb,)), ((), ())), preferred_element_type=F32)


ANY = pl.BlockSpec(memory_space=pl.ANY)
WHOLE = pl.BlockSpec(memory_space=pltpu.VMEM)


def hot_rows(rank, s, local, length):
    spot = lax.broadcasted_iota(jnp.int32, (CAP, length), 0)
    picked = rank[s]
    return jnp.concatenate(
        [(picked[e : e + 1] == spot).astype(F32).astype(BF16) for e in range(local)], axis=0
    )


def ring_spot(group, size):
    odd = lax.rem(group, jnp.int32(2))
    half = lax.div(group, jnp.int32(2))
    return (1 - odd) * half + odd * (size - 1 - half)


def ring_group(spot, size):
    spot = lax.rem(spot + 2 * size, jnp.int32(size))
    upper = lax.div(spot, jnp.int32(size // 2))
    return (1 - upper) * (2 * spot) + upper * (2 * (size - 1 - spot) + 1)


def front_body(dims, in_tree, out_tree, sem_tree, *refs):
    local, seqs, length, width, ff, n_grp, n_exp, rows_w = dims
    n_in, n_out = in_tree.num_leaves, out_tree.num_leaves
    I = space(jax.tree.unflatten(in_tree, refs[:n_in]))
    O = space(jax.tree.unflatten(out_tree, refs[n_in : n_in + n_out]))
    S = space(jax.tree.unflatten(sem_tree, refs[n_in + n_out :]))
    half = length // 2
    qkv = (HEADS + 2 * KV_HEADS) * HEAD_DIM
    grp, exp = lax.axis_index(GRP), lax.axis_index(EXP)
    me = grp * n_exp + exp
    y_bits = bits_of(n_exp)[1:]
    last_y = y_bits[-1]
    core_at = bit_at(exp, CORE)
    pair_at = bit_at(grp, PAIR)
    partner = {(EXP, bit): me + (1 - 2 * bit_at(exp, bit)) * bit for bit in bits_of(n_exp)}
    partner[GRP, PAIR] = me + (1 - 2 * pair_at) * (PAIR * n_exp)
    spot = ring_spot(grp, n_grp)
    around = [ring_group(spot + 1, n_grp) * n_exp + exp, ring_group(spot - 1, n_grp) * n_exp + exp]

    def send(src, dst, sems, device):
        return pltpu.make_async_remote_copy(
            src_ref=src, dst_ref=dst, send_sem=sems.at[0], recv_sem=sems.at[1],
            device_id=device, device_id_type=pl.DeviceIdType.LOGICAL,
        )

    barrier = pltpu.get_barrier_semaphore()
    greeted = list(partner.values()) + around
    for device in greeted:
        pl.semaphore_signal(barrier, inc=1, device_id=device, device_id_type=pl.DeviceIdType.LOGICAL)
    pl.semaphore_wait(barrier, len(greeted))


    hops = (n_grp // 2, n_grp - 1 - n_grp // 2)

    def ring_piece(full, origin):
        w = full.shape[2] // 2
        return full.at[origin, :, pl.ds(pl.multiple_of(core_at * w, 128), w)]

    def ring_send(kind, way, step):
        full = (O.wq, O.wo)[kind]
        origin = ring_group(spot - (step - 1) if way == 0 else spot + (step - 1), n_grp)
        piece = ring_piece(full, origin)
        return send(piece, piece, S.ring.at[kind, way, step], around[way])

    def ring_got(kind, way, step):
        full = (O.wq, O.wo)[kind]
        origin = ring_group(spot - step if way == 0 else spot + step, n_grp)
        return ring_piece(full, origin)

    def core_hand(kind, way, step):
        piece = ring_got(kind, way, step)
        return send(piece, piece, S.hand.at[kind, way, step], partner[EXP, CORE])

    def ring_step(kind, step):
        for way in range(2):
            @pl.when(step <= hops[way])
            def _():
                ring_send(kind, way, step).wait_recv()
                core_hand(kind, way, step).start()

            @pl.when(step + 1 <= hops[way])
            def _():
                ring_send(kind, way, step + 1).start()

    def ring_start(kind):
        for way in range(2):
            if hops[way]:
                ring_send(kind, way, jnp.int32(1)).start()

    def ring_end(kind):
        def body(step, carry):
            for way in range(2):
                @pl.when(step <= hops[way])
                def _():
                    core_hand(kind, way, step).wait()
                    ring_send(kind, way, step).wait_send()

            return carry

        lax.fori_loop(1, hops[0] + 1, body, 0)


    quads = 2 ** len(y_bits)
    first = seqs // 2

    def spread_send(all_ref, sems, k, axis, bit, low, count, to, part=None):
        src, dst = all_ref.at[pl.ds(low, count)], all_ref.at[pl.ds(to, count)]
        if part is not None:
            src, dst = src.at[:, part], dst.at[:, part]
        return send(src, dst, sems.at[k], partner[axis, bit])

    def y_spread(all_ref, sems, k, base, bits):
        return [spread_send(all_ref, sems, k + i, EXP, bit, base, 2**i, base + 2**i) for i, bit in enumerate(bits)]

    def core_spread(all_ref, sems, k, item):
        return spread_send(all_ref, sems, k, EXP, CORE, item, 1, item + first)

    own = [
        pltpu.make_async_copy(I.small, O.small.at[0], S.own.at[0]),
        pltpu.make_async_copy(I.wq, O.wq.at[grp], S.own.at[1]),
        pltpu.make_async_copy(I.wo, O.wo.at[grp], S.own.at[2]),
        pltpu.make_async_copy(I.dy, O.dy.at[0], S.own.at[3]),
    ]
    for copy in own:
        copy.start()
    for copy in own:
        copy.wait()
    ring_start(0)
    small = y_spread(O.small, S.small, 0, 0, y_bits)
    small.append(spread_send(O.small, S.small, len(y_bits), GRP, PAIR, 0, quads, quads))
    small.append(spread_send(O.small, S.small, len(y_bits) + 1, EXP, CORE, 0, first, first))
    dy_y = y_spread(O.dy, S.dy, 0, 0, y_bits)
    n_y = len(y_bits)
    dy_z = spread_send(O.dy, S.dy, n_y, GRP, PAIR, 0, 1, quads)
    dy_zy = y_spread(O.dy, S.dy, n_y + 1, quads, y_bits)
    dy_core = [core_spread(O.dy, S.dy, 2 * n_y + 1 + i, i) for i in range(first)]
    for copy in small:
        copy.start()
        copy.wait_recv()
    dy_y[0].start()
    dy_z.start()


    def slots(info, tri, sem):
        load = pltpu.make_async_copy(O.small, info, sem.at[0])
        load.start()
        load.wait()
        base = exp * (2 * local) + pair_at * local
        for r in range(0, length, 256):
            before = lax.broadcasted_iota(jnp.int32, (256, length), 0) + r
            after = lax.broadcasted_iota(jnp.int32, (256, length), 1)
            tri[r : r + 256] = jnp.where(before < after, 1.0, 0.0).astype(BF16)
        index = lax.broadcasted_iota(jnp.int32, (8, length), 0)
        name = (index + base).astype(F32)
        used = index < local

        def body(s, carry):
            member = jnp.zeros((8, length), F32)
            gate = jnp.zeros((8, length), F32)
            number = jnp.zeros((8, length), F32)
            for k in range(TOP):
                hit = (info[s, k : k + 1] == name) & used
                member = jnp.where(hit, 1.0, member)
                gate = jnp.where(hit, info[s, TOP + k : TOP + k + 1], gate)
                number = jnp.where(hit, float(k), number)
            rank = dot(member.astype(BF16), tri[...])
            O.rank[s] = jnp.where(member > 0.0, rank, -1.0).astype(jnp.int32)
            S.gate[s] = gate
            S.number[s] = number
            return carry

        lax.fori_loop(0, seqs, body, 0)

    pl.run_scoped(
        slots, pltpu.VMEM((seqs, 8, length), F32), pltpu.VMEM((length, length), BF16), pltpu.SemaphoreType.DMA((1,))
    )

    def ring_through(kind):
        def body(step, carry):
            ring_step(kind, step)
            return carry

        lax.fori_loop(1, hops[0] + 1, body, 0)

    ring_through(0)
    ring_start(1)
    ring_end(0)


    def attention(w, n1, mixed, sems):
        loads = [
            pltpu.make_async_copy(O.wq.at[i, pl.ds(0, rows_w)], w.at[pl.ds(i * rows_w, rows_w)], sems.at[0])
            for i in range(n_grp)
        ]
        for copy in loads:
            copy.start()

        lanes = -(-rows_w // 128) * 128

        def gains(buf, total):
            copies = [
                pltpu.make_async_copy(O.wq.at[i, pl.ds(rows_w, 16), pl.ds(0, lanes)], buf.at[i], sems.at[1])
                for i in range(n_grp)
            ]
            for copy in copies:
                copy.start()
            pltpu.make_async_copy(buf, buf, sems.at[1]).wait()
            total[...] = jnp.zeros_like(total)

            def body(i, carry):
                r = lax.broadcasted_iota(jnp.int32, (lanes, width), 0)
                c = lax.broadcasted_iota(jnp.int32, (lanes, width), 1)
                pick = jnp.where((c == r + i * rows_w) & (r < rows_w), 1.0, 0.0).astype(BF16)
                total[...] += dot(buf[i], pick)
                return carry

            lax.fori_loop(0, n_grp, body, 0)
            O.gains[...] = total[0:8]

        pl.run_scoped(gains, pltpu.VMEM((n_grp, 16, lanes), BF16), pltpu.VMEM((16, width), F32))
        chunk = 64

        def norm(j, carry):
            r = pl.ds(pl.multiple_of(j * chunk, chunk), chunk)
            x = I.tokens[r].astype(F32)
            inverse = lax.rsqrt(jnp.mean(x * x, axis=-1, keepdims=True) + EPSILON)
            O.inv_one[r] = inverse
            n1[r] = (x * inverse * O.gains[0:1]).astype(BF16)
            return carry

        lax.fori_loop(0, length // chunk, norm, 0)
        n1_out = pltpu.make_async_copy(n1, O.n1, sems.at[2])
        n1_out.start()
        pltpu.make_async_copy(w, w, sems.at[0]).wait()

        def heads(mask, kr, v, qr, own):
            block = 256
            for r in range(0, length, block):
                row = lax.broadcasted_iota(jnp.int32, (block, length), 0) + r
                col = lax.broadcasted_iota(jnp.int32, (block, length), 1)
                tag = I.tagc[r : r + block]
                inside = (tag == I.tagr[...]) & (tag > 0)
                mask[r : r + block] = jnp.where((col <= row) | inside, 0.0, -1e30)

            def turn(u):
                return u * I.cos[...] + pltpu.roll(u, HEAD_DIM // 2, 1) * I.sin[...]

            per = HEADS // KV_HEADS // 2
            pairs = HEADS // 2
            every = -(-hops[0] // (pairs - 2))
            for g in range(KV_HEADS):
                kv = slice(g * HEAD_DIM, (g + 1) * HEAD_DIM)
                k_at = HEADS * HEAD_DIM + g * HEAD_DIM
                v_at = k_at + KV_HEADS * HEAD_DIM
                both = dot(n1[...], w[:, k_at : k_at + HEAD_DIM])
                kr[:, kv] = turn(both).astype(BF16)
                v[:, kv] = dot(n1[...], w[:, v_at : v_at + HEAD_DIM]).astype(BF16)

                def pair(i, carry):
                    p = g * per + i
                    span = pl.ds(pl.multiple_of(p * 2 * HEAD_DIM, 2 * HEAD_DIM), 2 * HEAD_DIM)
                    q2 = dot(n1[...], w[:, span])
                    for h in range(2):
                        cols = pl.ds(pl.multiple_of((2 * p + h) * HEAD_DIM, HEAD_DIM), HEAD_DIM)
                        qr[:, cols] = turn(q2[:, h * HEAD_DIM : (h + 1) * HEAD_DIM]).astype(BF16)
                        for r in range(0, length, block):
                            keys = min(length, r + 2 * block)
                            s = dot(qr[r : r + block, cols], kr[:keys, kv], 1, 1) * SCALE
                            s = s + mask[r : r + block, :keys]
                            top = jnp.max(s, axis=-1, keepdims=True)
                            e = jnp.exp(s - top)
                            total = jnp.sum(e, axis=-1, keepdims=True)
                            probs = (e * (1.0 / total)).astype(BF16)
                            mixed[r : r + block, cols] = dot(probs, v[:keys, kv]).astype(BF16)
                            O.lse[2 * p + h, r : r + block] = top + jnp.log(total)

                    def hop(j, carry):
                        @pl.when(j <= hops[0])
                        def _():
                            ring_step(1, j)

                        return carry

                    lax.fori_loop(lax.max((p - 1) * every + 1, 1), lax.max(p * every + 1, 1), hop, 0)
                    return carry

                lax.fori_loop(0, per, pair, 0)
            outs = [
                pltpu.make_async_copy(qr, O.q, own.at[0]),
                pltpu.make_async_copy(kr, O.k, own.at[1]),
                pltpu.make_async_copy(v, O.v, own.at[2]),
                pltpu.make_async_copy(mixed, O.mixed, own.at[3]),
            ]
            for copy in outs:
                copy.start()
            for copy in outs:
                copy.wait()

        pl.run_scoped(
            heads, pltpu.VMEM((length, length), F32), pltpu.VMEM((length, KV_HEADS * HEAD_DIM), BF16),
            pltpu.VMEM((length, KV_HEADS * HEAD_DIM), BF16), pltpu.VMEM((length, HEADS * HEAD_DIM), BF16),
            pltpu.SemaphoreType.DMA((4,)),
        )
        n1_out.wait()

    def projection(mixed, wo, n2, hid, sems):
        loads = [
            pltpu.make_async_copy(O.wo.at[i], wo.at[pl.ds(i * rows_w, rows_w)], sems.at[0]) for i in range(n_grp)
        ]
        for copy in loads:
            copy.start()
        pltpu.make_async_copy(wo, wo, sems.at[0]).wait()
        block = 256

        def body(j, carry):
            r = pl.ds(pl.multiple_of(j * block, block), block)
            for c in range(0, width, 512):
                hid[r, c : c + 512] = I.tokens[r, c : c + 512].astype(F32) + dot(mixed[r], wo[:, c : c + 512])

            def point(i, carry):
                r = pl.ds(pl.multiple_of(j * block + i * 64, 64), 64)
                h = hid[r]
                inverse = lax.rsqrt(jnp.mean(h * h, axis=-1, keepdims=True) + EPSILON)
                O.inv_two[r] = inverse
                n2[r] = (h * inverse * O.gains[1:2]).astype(BF16)
                return carry

            return lax.fori_loop(0, block // 64, point, carry)

        lax.fori_loop(0, length // block, body, 0)
        outs = [
            pltpu.make_async_copy(n2, O.n2.at[0], sems.at[0]),
            pltpu.make_async_copy(hid, O.hidden, sems.at[1]),
        ]
        for copy in outs:
            copy.start()
        outs[0].wait()
        n2_start()
        outs[1].wait()


    low, high = pl.ds(0, half), pl.ds(half, half)
    steps = len(y_bits) - 1
    mid = 2**steps
    n2_pre = y_spread(O.n2, S.n2, 0, 0, y_bits[:-1])
    n2_y = spread_send(O.n2, S.n2, steps, EXP, last_y, 0, mid, mid)
    n2_z = spread_send(O.n2, S.n2, steps + 1, GRP, PAIR, 0, mid, 2 * mid)
    n2_low = spread_send(O.n2, S.n2, steps + 2, EXP, last_y, 2 * mid, mid, 3 * mid, low)
    n2_high = spread_send(O.n2, S.n2, steps + 3, GRP, PAIR, mid, mid, 3 * mid, high)
    n2_core = [core_spread(O.n2, S.n2, steps + 4 + i, i) for i in range(first)]

    def n2_start():
        for copy in n2_pre:
            copy.start()
            copy.wait_recv()
        n2_y.start()
        n2_z.start()
        for i in range(mid):
            n2_core[i].start()

    def n2_ready(step):
        for i in range(first):
            @pl.when(step == 2 * i)
            def _():
                if i == mid:
                    n2_y.wait_recv()
                    n2_high.start()
                    for j in range(mid):
                        n2_core[mid + j].start()
                    n2_z.wait_recv()
                    n2_low.start()
                    for j in range(mid):
                        n2_core[2 * mid + j].start()
                if i == 3 * mid:
                    n2_low.wait_recv()
                    n2_high.wait_recv()
                    for j in range(mid):
                        n2_core[3 * mid + j].start()

            @pl.when(step == 2 * i + 1)
            def _():
                n2_core[i].wait_recv()

    def dy_ready(step):
        for i in range(first):
            @pl.when(step == 2 * i)
            def _():
                if i == quads:
                    for j in range(1, quads):
                        dy_core[quads + j].start()

            @pl.when(step == 2 * i + 1)
            def _():
                dy_core[i].wait_recv()


    def gather(all_ref, out_ref, ready, with_slots):
        chunk = 512

        def scoped(in_buf, out_buf, in_sem, out_sem):
            def seq_of(step):
                return lax.div(step, jnp.int32(2)) + lax.rem(step, jnp.int32(2)) * first

            def fetch(step, slot):
                return pltpu.make_async_copy(all_ref.at[seq_of(step)], in_buf.at[slot], in_sem.at[slot])

            def leaving(step, slot, e):
                row = pl.multiple_of(seq_of(step) * CAP, 16)
                return pltpu.make_async_copy(
                    out_buf.at[slot, pl.ds(e * CAP, CAP)], out_ref.at[e, pl.ds(row, CAP)], out_sem.at[slot, e]
                )

            def body(step, carry):
                slot = lax.rem(step, jnp.int32(2))
                s = seq_of(step)
                ready(step)
                fetch(step, slot).start()
                fetch(step, slot).wait()

                @pl.when(step >= 2)
                def _():
                    for e in range(local):
                        leaving(step - 2, slot, e).wait()

                place = lax.broadcasted_iota(jnp.int32, (CAP, length), 0)
                ranks = O.rank[s]
                hits = [ranks[e : e + 1] == place for e in range(local)]
                if with_slots:
                    gate, number = S.gate[s], S.number[s]
                    rows = pl.ds(pl.multiple_of(s * CAP, 16), CAP)
                    for e in range(local):
                        O.gate[e, rows] = jnp.sum(jnp.where(hits[e], gate[e : e + 1], 0.0), axis=-1, keepdims=True)
                        O.choice[e, rows] = jnp.sum(
                            jnp.where(hits[e], number[e : e + 1], 0.0), axis=-1, keepdims=True
                        )
                hot = jnp.concatenate([hit.astype(F32).astype(BF16) for hit in hits], axis=0)
                for c in range(0, width, chunk):
                    out_buf[slot, :, c : c + chunk] = dot(hot, in_buf[slot, :, c : c + chunk]).astype(BF16)
                for e in range(local):
                    leaving(step, slot, e).start()
                return carry

            lax.fori_loop(0, seqs, body, 0)
            for step in (seqs - 2, seqs - 1):
                for e in range(local):
                    leaving(jnp.int32(step), step % 2, e).wait()

        pl.run_scoped(
            scoped, pltpu.VMEM((2, length, width), BF16), pltpu.VMEM((2, local * CAP, width), BF16),
            pltpu.SemaphoreType.DMA((2,)), pltpu.SemaphoreType.DMA((2, local)),
        )

    def upstream(y, w, t, sems):
        rows = seqs * CAP
        block = 448 if rows % 448 == 0 else rows

        def body(e, carry):
            loads = [
                pltpu.make_async_copy(O.y.at[e], y, sems.at[0]),
                pltpu.make_async_copy(I.w_down.at[pair_at * local + e], w, sems.at[1]),
            ]
            for copy in loads:
                copy.start()
            for copy in loads:
                copy.wait()

            @pl.when(e >= 1)
            def _():
                pltpu.make_async_copy(t, O.t.at[e], sems.at[2]).wait()

            def part(b, carry):
                span = pl.ds(pl.multiple_of(b * block, 16), block)
                t[span] = dot(y[span], w[...])
                return carry

            lax.fori_loop(0, rows // block, part, 0)
            pltpu.make_async_copy(t, O.t.at[e], sems.at[2]).start()
            return carry

        lax.fori_loop(0, local, body, 0)
        pltpu.make_async_copy(t, O.t.at[0], sems.at[2]).wait()


    def attend_and_project(mixed, sems):
        pl.run_scoped(
            lambda w, n1: attention(w, n1, mixed, sems),
            pltpu.VMEM((width, qkv), BF16), pltpu.VMEM((length, width), BF16),
        )
        for i, copy in enumerate(dy_y):
            copy.wait_recv()
            if i + 1 < n_y:
                dy_y[i + 1].start()
        for i in range(quads):
            dy_core[i].start()
        dy_z.wait_recv()
        dy_zy[0].start()
        dy_core[quads].start()
        ring_end(1)
        pl.run_scoped(
            lambda wo, n2, hid: projection(mixed, wo, n2, hid, sems),
            pltpu.VMEM((width, width), BF16), pltpu.VMEM((length, width), BF16), pltpu.VMEM((length, width), F32),
        )

    pl.run_scoped(attend_and_project, pltpu.VMEM((length, HEADS * HEAD_DIM), BF16), pltpu.SemaphoreType.DMA((3,)))
    for i, copy in enumerate(dy_zy):
        copy.wait_recv()
        if i + 1 < n_y:
            dy_zy[i + 1].start()
    gather(O.dy, O.y, dy_ready, True)
    rows = seqs * CAP
    pl.run_scoped(
        upstream, pltpu.VMEM((rows, width), BF16), pltpu.VMEM((width, ff), BF16), pltpu.VMEM((rows, ff), F32),
        pltpu.SemaphoreType.DMA((3,)),
    )
    gather(O.n2, O.x, n2_ready, False)
    for copy in small + dy_y + [dy_z] + dy_zy + dy_core + n2_pre + [n2_y, n2_z, n2_low, n2_high] + n2_core:
        copy.wait_send()


def front(dims, arrays):
    local, seqs, length, width, ff, n_grp, n_exp, rows_w = dims
    rows = seqs * CAP
    qkv = (HEADS + 2 * KV_HEADS) * HEAD_DIM
    kv = KV_HEADS * HEAD_DIM
    n_y = len(bits_of(n_exp)) - 1
    vmem = dict(
        rank=shape(seqs, 8, length, dtype=jnp.int32),
        gate=shape(local, rows, 1, dtype=F32),
        choice=shape(local, rows, 1, dtype=F32),
        gains=shape(8, width, dtype=F32),
        inv_one=shape(length, 1, dtype=F32),
        inv_two=shape(length, 1, dtype=F32),
        lse=shape(HEADS, length, 1, dtype=F32),
    )
    hbm = dict(
        small=shape(seqs, 8, length, dtype=F32),
        wq=shape(n_grp, rows_w + 16, qkv),
        wo=shape(n_grp, rows_w, width),
        dy=shape(seqs, length, width),
        n2=shape(seqs, length, width),
        n1=shape(length, width),
        q=shape(length, HEADS * HEAD_DIM),
        k=shape(length, kv),
        v=shape(length, kv),
        mixed=shape(length, HEADS * HEAD_DIM),
        hidden=shape(length, width, dtype=F32),
        x=shape(local, rows, width),
        y=shape(local, rows, width),
        t=shape(local, rows, ff, dtype=F32),
    )
    hops = n_grp // 2 + 1
    dma = pltpu.SemaphoreType.DMA
    scratch = dict(
        ring=dma((2, 2, hops, 2)),
        hand=dma((2, 2, hops, 2)),
        own=dma((4,)),
        small=dma((n_y + 2, 2)),
        dy=dma((2 * n_y + 1 + seqs // 2, 2)),
        n2=dma((n_y + 3 + seqs // 2, 2)),
        gate=pltpu.VMEM((seqs, 8, length), F32),
        number=pltpu.VMEM((seqs, 8, length), F32),
    )
    outs = dict(vmem, **hbm)
    in_leaves, in_tree = jax.tree.flatten(arrays)
    far = {id(arrays["w_down"])}
    out_leaves, out_tree = jax.tree.flatten(outs)
    near = {id(value) for value in vmem.values()}
    sem_leaves, sem_tree = jax.tree.flatten(scratch)
    results = pl.pallas_call(
        functools.partial(front_body, dims, in_tree, out_tree, sem_tree),
        in_specs=[ANY if id(leaf) in far else WHOLE for leaf in in_leaves],
        out_specs=[WHOLE if id(leaf) in near else ANY for leaf in out_leaves],
        out_shape=out_leaves,
        scratch_shapes=sem_leaves,
        compiler_params=pltpu.CompilerParams(vmem_limit_bytes=VMEM, collective_id=1, has_side_effects=True),
        name="front",
    )(*in_leaves)
    return space(jax.tree.unflatten(out_tree, results))


def share_rows(width, devices):
    return -(-width // (16 * devices)) * 16


def spread(block, devices):
    rows, width = block.shape
    share = width // devices
    extra = share_rows(width, devices) - share
    if extra == 0:
        return block
    block = jnp.pad(block.reshape(rows, devices, share), ((0, 0), (0, 0), (0, extra)))
    return block.reshape(rows, -1)


def mega_plan(local, seqs, length, width, ff, n_grp, n_exp, rows_w):
    rows = seqs * CAP
    half = length // 2
    quads = seqs // 8
    wide = width + 128
    chunks = 3 * local
    qkv = (HEADS + 2 * KV_HEADS) * HEAD_DIM
    mids = [bit for bit in reversed(bits_of(n_grp)) if bit > PAIR]
    stages = len(bits_of(n_grp)) + len(bits_of(n_exp))
    share = share_rows(width, n_grp * n_exp)
    dma = pltpu.SemaphoreType.DMA

    def returned(w):
        quad = shape(quads, half, w)
        two = shape(2, quads, half, w)
        more = [shape(quads, 2, half, w)] * 2 if quads > 1 else []
        return dict(
            came=shape(seqs // 2, length, w), kept=shape(4, quads, half, w),
            zc=two, yc=two, zcin=two, ycin=two, ylow=quad, zhigh=quad, ylowin=quad, zhighin=quad, more=more,
        )

    def summed(w):
        return dict(
            block=shape(*[2] * stages, share, w),
            came=[shape(*[2] * (stages - 1 - i), share, w) for i in range(stages)],
        )

    gain = shape(8, width, dtype=F32)
    outs = dict(
        layer=shape(length, width),
        d_gates=shape(length, 128, dtype=F32),
        d_tokens=shape(length, width),
        final=shape(3, 2 * local, width // n_grp, ff),
        o_out=shape(share, width, dtype=F32),
        qkv_out=shape(share, qkv, dtype=F32),
        gains=gain,
        theirs=shape(chunks, width // 2, ff),
        mine=shape(chunks, width // 2, ff),
        come=[shape(chunks, width >> (i + 1), ff) for i in range(len(mids) + 1)],
        act=shape(local, rows, ff),
        outs=shape(local, rows, wide),
        far=shape(seqs // 2, length, wide),
        near=shape(seqs // 2, length, wide),
        ret=[returned(width), returned(wide)],
        d_hidden=shape(length, width, dtype=F32),
        sums=[summed(width), summed(qkv)],
        gsum=[gain] * stages,
        gin=[gain] * stages,
    )
    hops = [dma((2, 2)), dma((2, 2)), dma((2, n_exp.bit_length()))]
    sems = dict(
        ret=[dict(core=dma((2, seqs // 2)), hops=hops)] * 2,
        sums=[dma((2, stages))] * 2,
        gall=dma((2, stages)),
        grad=[dma((2, chunks))] * (len(mids) + 1),
        pair=dma((2, chunks)),
        d_gate=pltpu.VMEM((local, rows, 1), F32),
        gain=pltpu.VMEM((8, width), F32),
    )
    return outs, sems


def mega_body(dims, in_tree, out_tree, sem_tree, *refs):
    local, seqs, length, width, ff, n_grp, n_exp, rows_w = dims
    n_in, n_out = in_tree.num_leaves, out_tree.num_leaves
    I = space(jax.tree.unflatten(in_tree, refs[:n_in]))
    O = space(jax.tree.unflatten(out_tree, refs[n_in : n_in + n_out]))
    S = space(jax.tree.unflatten(sem_tree, refs[n_in + n_out :]))
    rows = seqs * CAP
    half = length // 2
    wide = width + 128
    quads = seqs // 8
    qkv = (HEADS + 2 * KV_HEADS) * HEAD_DIM
    grp, exp = lax.axis_index(GRP), lax.axis_index(EXP)
    grp_bits, exp_bits = bits_of(n_grp), bits_of(n_exp)
    me = grp * n_exp + exp
    places, partners = {}, {}
    for axis, index, bits, unit in ((GRP, grp, grp_bits, n_exp), (EXP, exp, exp_bits, 1)):
        for bit in bits:
            place = bit_at(index, bit)
            places[axis, bit] = place
            partners[axis, bit] = me + (1 - 2 * place) * (bit * unit)
    pair_at, x_at = places[GRP, PAIR], places[GRP, 1]
    y_bits = exp_bits[1:]
    mids = [bit for bit in reversed(grp_bits) if bit > PAIR]

    def send(src, dst, sems, axis, bit):
        return pltpu.make_async_remote_copy(
            src_ref=src, dst_ref=dst, send_sem=sems[0], recv_sem=sems[1],
            device_id=partners[axis, bit], device_id_type=pl.DeviceIdType.LOGICAL,
        )

    barrier = pltpu.get_barrier_semaphore()
    for partner in partners.values():
        pl.semaphore_signal(barrier, inc=1, device_id=partner, device_id_type=pl.DeviceIdType.LOGICAL)
    pl.semaphore_wait(barrier, len(partners))


    def grad_send(stage, c):
        sems = S.grad[stage]
        if stage == 0:
            src, bit = O.theirs.at[c], grp_bits[0]
        else:
            bit = mids[stage - 1]
            size = O.come[stage].shape[1]
            place = 1 - places[GRP, bit]
            src = O.come[stage - 1].at[c, pl.ds(pl.multiple_of(place * size, 16), size)]
        return send(src, O.come[stage].at[c], (sems.at[0, c], sems.at[1, c]), GRP, bit)

    def pair_send(c):
        e, k = lax.div(c, jnp.int32(3)), lax.rem(c, jnp.int32(3))
        sems = S.pair
        last = O.come[len(mids)]
        size = last.shape[1] // 2
        return send(
            last.at[c, pl.ds(pl.multiple_of((1 - pair_at) * size, 16), size)], O.final.at[k, pair_at * local + e],
            (sems.at[0, c], sems.at[1, c]), GRP, PAIR,
        )

    def grad_step(stage, c):
        grad_send(stage, c).wait_recv()
        size = O.come[stage].shape[1]
        if stage == 0:
            mine = O.mine.at[c]
        else:
            place = places[GRP, mids[stage - 1]]
            mine = O.come[stage - 1].at[c, pl.ds(pl.multiple_of(place * size, 16), size)]
        parts = 2
        piece = size // parts

        def scoped(a, b, sems):
            def load(p):
                span = pl.ds(p * piece, piece)
                return [
                    pltpu.make_async_copy(mine.at[span], a.at[p], sems.at[p, 0]),
                    pltpu.make_async_copy(O.come[stage].at[c, span], b.at[p], sems.at[p, 1]),
                ]

            for p in range(parts):
                for copy in load(p):
                    copy.start()
            stores = []
            for p in range(parts):
                for copy in load(p):
                    copy.wait()

                a[p] = a[p] + b[p]
                if stage < len(mids):
                    stores.append(pltpu.make_async_copy(
                        a.at[p], O.come[stage].at[c, pl.ds(p * piece, piece)], sems.at[p, 2]
                    ))
                    stores[-1].start()
            if stage == len(mids):
                e, k = lax.div(c, jnp.int32(3)), lax.rem(c, jnp.int32(3))
                stores = [
                    pltpu.make_async_copy(a.at[pair_at], O.final.at[k, pair_at * local + e], sems.at[0, 2]),
                    pltpu.make_async_copy(
                        a.at[1 - pair_at],
                        O.come[stage].at[c, pl.ds(pl.multiple_of((1 - pair_at) * piece, 16), piece)],
                        sems.at[1, 2],
                    ),
                ]
                for copy in stores:
                    copy.start()
            for copy in stores:
                copy.wait()

        pl.run_scoped(
            scoped, pltpu.VMEM((parts, piece, ff), BF16), pltpu.VMEM((parts, piece, ff), BF16),
            pltpu.SemaphoreType.DMA((parts, 3)),
        )
        if stage < len(mids):
            grad_send(stage + 1, c).start()
        else:
            pair_send(c).start()

    def grads(stage, first, last):
        def body(c, carry):
            grad_step(stage, c)
            return carry

        lax.fori_loop(first, last, body, 0)


    block = 448 if rows % 448 == 0 else rows
    piece = width // n_grp
    band = 384
    bands = width // band
    keep = band // 2

    def expert(e, x, y, t, w, gu, d, act, theirs, mine, dx, sems):
        index = pair_at * local + e
        copies = [
            pltpu.make_async_copy(I.x.at[e], x, sems.at[0]),
            pltpu.make_async_copy(I.w_gate.at[index], w.at[:, pl.ds(0, ff)], sems.at[1]),
            pltpu.make_async_copy(I.w_up.at[index], w.at[:, pl.ds(ff, ff)], sems.at[2]),
            pltpu.make_async_copy(I.t.at[e], t, sems.at[3]),
            pltpu.make_async_copy(I.y.at[e], y, sems.at[4]),
        ]
        for copy in copies:
            copy.start()
        for copy in copies[:3]:
            copy.wait()

        def forward(b, carry):
            span = pl.ds(pl.multiple_of(b * block, 16), block)
            gu[...] = dot(x[span], w[...])

            @pl.when(b == 0)
            def _():
                copies[3].wait()

            def point(i, carry):
                inner = pl.ds(pl.multiple_of(i * 64, 64), 64)
                outer = pl.ds(pl.multiple_of(b * block + i * 64, 64), 64)
                g, u = gu[inner, :ff], gu[inner, ff:]
                tt, gate = t[outer], I.gate[e, outer]
                sig = 1.0 / (1.0 + jnp.exp(-g))
                silu = g * sig
                a32 = (silu * u).astype(BF16).astype(F32)
                S.d_gate[e, outer] = jnp.sum(a32 * tt, axis=-1, keepdims=True)
                act[outer] = (a32 * gate).astype(BF16)
                da = gate * tt
                d[outer, :ff] = (da * u * sig * (1.0 + g * (1.0 - sig))).astype(BF16)
                d[outer, ff:] = (da * silu).astype(BF16)
                return carry

            return lax.fori_loop(0, block // 64, point, carry)

        lax.fori_loop(0, rows // block, forward, 0)
        copies[4].wait()
        act_out = pltpu.make_async_copy(act, O.act.at[e], sems.at[0])
        act_out.start()

        def split(j, k, res):
            res = res.astype(BF16)
            for p in range(band // (2 * piece)):
                low = res[2 * p * piece : (2 * p + 1) * piece]
                high = res[(2 * p + 1) * piece : (2 * p + 2) * piece]
                span = pl.ds(pl.multiple_of(j * keep + p * piece, 16), piece)
                theirs[k, span] = jnp.where(x_at == 0, high, low)
                mine[k, span] = jnp.where(x_at == 0, low, high)

        def band_gate(j, carry):
            cols = pl.ds(pl.multiple_of(j * band, 128), band)
            res = dot(x[:, cols], d[...], 0, 0)
            split(j, 0, res[:, :ff])
            split(j, 1, res[:, ff:])
            return carry

        def band_down(j, carry):
            cols = pl.ds(pl.multiple_of(j * band, 128), band)
            split(j, 2, dot(y[:, cols], act[...], 0, 0))
            return carry

        def store(k, many, place):
            return [
                pltpu.make_async_copy(theirs.at[pl.ds(k, many)], O.theirs.at[pl.ds(3 * e + k, many)], sems.at[place]),
                pltpu.make_async_copy(mine.at[pl.ds(k, many)], O.mine.at[pl.ds(3 * e + k, many)], sems.at[place + 1]),
            ]

        lax.fori_loop(0, bands, band_gate, 0)
        early = store(0, 2, 1)
        for copy in early:
            copy.start()
        lax.fori_loop(0, bands, band_down, 0)
        late = store(2, 1, 3)
        for copy in late:
            copy.start()
        for copy in early:
            copy.wait()
        for k in range(2):
            grad_send(0, 3 * e + k).start()

        def back(b, carry):
            span = pl.ds(pl.multiple_of(b * block, 16), block)
            for c in range(0, width, 512):
                dx[span, c : c + 512] = dot(d[span], w[c : c + 512], 1, 1).astype(BF16)
            return carry

        lax.fori_loop(0, rows // block, back, 0)
        dx_out = pltpu.make_async_copy(dx, O.outs.at[e, :, pl.ds(0, width)], sems.at[5])
        dx_out.start()
        for copy in late:
            copy.wait()
        grad_send(0, 3 * e + 2).start()
        act_out.wait()
        dx_out.wait()

    def experts(*scratch):
        def body(e, carry):
            expert(e, *scratch)
            if local == 4:
                grads(0, lax.max(e - 1, 0), e + lax.div(e, jnp.int32(3)))
            return carry

        lax.fori_loop(0, local, body, 0)


    def collapse(tag, w):
        first = seqs // 2
        far, near = O.far, O.near
        cols = pl.ds(0, w)
        spans = [(c, min(512, w - c)) for c in range(0, w, 512)]

        def scoped(in_buf, out_buf, in_sem, out_sem):
            def coming(step, slot, e):
                s = lax.rem(step + first, jnp.int32(seqs))
                return pltpu.make_async_copy(
                    O.outs.at[e, pl.ds(pl.multiple_of(s * CAP, 16), CAP), cols],
                    in_buf.at[slot, pl.ds(e * CAP, CAP)],
                    in_sem.at[slot, e],
                )

            def leave(step, slot):
                pltpu.make_async_copy(out_buf.at[slot], near.at[0, :, cols], out_sem.at[slot]).wait()

                @pl.when(step < first)
                def _():
                    core_send(tag, step).start()

            for e in range(local):
                coming(0, 0, e).start()

            def body(step, carry):
                slot = lax.rem(step, jnp.int32(2))

                @pl.when(step + 1 < seqs)
                def _():
                    for e in range(local):
                        coming(step + 1, 1 - slot, e).start()

                for e in range(local):
                    coming(step, slot, e).wait()

                @pl.when(step >= 2)
                def _():
                    leave(step - 2, slot)

                hot = hot_rows(I.rank, lax.rem(step + first, jnp.int32(seqs)), local, length)
                for c, span in spans:
                    out_buf[slot, :, c : c + span] = dot(hot, in_buf[slot, :, c : c + span], 0, 0).astype(BF16)

                @pl.when(step < first)
                def _():
                    pltpu.make_async_copy(out_buf.at[slot], far.at[step, :, cols], out_sem.at[slot]).start()

                @pl.when(step >= first)
                def _():
                    pltpu.make_async_copy(out_buf.at[slot], near.at[step - first, :, cols], out_sem.at[slot]).start()

                return carry

            lax.fori_loop(0, seqs, body, 0)
            for step in (seqs - 2, seqs - 1):
                leave(step, step % 2)

        pl.run_scoped(
            scoped,
            pltpu.VMEM((2, local * CAP, w), BF16),
            pltpu.VMEM((2, length, w), BF16),
            pltpu.SemaphoreType.DMA((2, local)),
            pltpu.SemaphoreType.DMA((2,)),
        )

    def core_send(tag, s):
        sems = S.ret[tag].core
        came = O.ret[tag].came
        src = O.far.at[s, :, pl.ds(0, came.shape[2])]
        return send(src, came.at[s], (sems.at[0, s], sems.at[1, s]), EXP, CORE)

    def hop(tag, number, which):
        sems = S.ret[tag].hops[number - 1]
        pair = (sems.at[0, which], sems.at[1, which])
        r = O.ret[tag]
        src, dst = [(r.zc, r.zcin), (r.yc, r.ycin), (r.ylow, r.ylowin), (r.zhigh, r.zhighin)][2 * (number - 1) + which]
        across = (number == 1) == (which == 0)
        axis, bit = (GRP, PAIR) if across else (EXP, y_bits[-1])
        return send(src, dst, pair, axis, bit)

    def blend(pieces, w):
        def scoped(a, b, load_sem, store_sem):
            def load(i):
                slot = i % 2
                first, second = pieces[i][0]
                return [
                    pltpu.make_async_copy(first, a.at[slot], load_sem.at[slot, 0]),
                    pltpu.make_async_copy(second, b.at[slot], load_sem.at[slot, 1]),
                ]

            def store(i):
                return pltpu.make_async_copy(a.at[i % 2], pieces[i][1], store_sem.at[i % 2])

            for copy in load(0):
                copy.start()
            for i in range(len(pieces)):
                if i >= 1:
                    store(i - 1).wait()
                if i + 1 < len(pieces):
                    for copy in load(i + 1):
                        copy.start()
                for copy in load(i):
                    copy.wait()
                a[i % 2] = a[i % 2] + b[i % 2]
                store(i).start()
            store(len(pieces) - 1).wait()

        pl.run_scoped(
            scoped, pltpu.VMEM((2, half, w), BF16), pltpu.VMEM((2, half, w), BF16),
            pltpu.SemaphoreType.DMA((2, 2)), pltpu.SemaphoreType.DMA((2,)),
        )

    low, high = pl.ds(0, half), pl.ds(half, half)

    def return_one(tag, w):
        for s in range(seqs // 2):
            core_send(tag, s).wait_recv()
        near, came = O.near, O.ret[tag].came

        def piece_of(quad, j, part, to):
            s = quad * quads + j
            return ((near.at[s, part, pl.ds(0, w)], came.at[s, part]), to)

        zc, yc, kept = O.ret[tag].zc, O.ret[tag].yc, O.ret[tag].kept
        every = range(quads)
        blend(
            [piece_of(2, j, low, zc.at[0, j]) for j in every]
            + [piece_of(3, j, low, zc.at[1, j]) for j in every],
            w,
        )
        hop(tag, 1, 0).start()
        blend(
            [piece_of(1, j, high, yc.at[0, j]) for j in every]
            + [piece_of(3, j, high, yc.at[1, j]) for j in every],
            w,
        )
        hop(tag, 1, 1).start()
        blend(
            [piece_of(1, j, low, kept.at[2, j]) for j in every]
            + [piece_of(2, j, high, kept.at[3, j]) for j in every]
            + [piece_of(0, j, low, kept.at[0, j]) for j in every]
            + [piece_of(0, j, high, kept.at[1, j]) for j in every],
            w,
        )

    def return_two(tag, w):
        kept = O.ret[tag].kept
        every = range(quads)
        hop(tag, 1, 0).wait_recv()
        blend([((kept.at[2, j], O.ret[tag].zcin.at[1, j]), O.ret[tag].ylow.at[j]) for j in every], w)
        hop(tag, 2, 0).start()
        hop(tag, 1, 1).wait_recv()
        blend([((kept.at[3, j], O.ret[tag].ycin.at[1, j]), O.ret[tag].zhigh.at[j]) for j in every], w)
        hop(tag, 2, 1).start()

    def return_end(tag, w):
        for which in range(2):
            hop(tag, 2, which).wait_recv()
        kept = O.ret[tag].kept
        terms = [
            [[kept.at[0, j], O.ret[tag].zcin.at[0, j], O.ret[tag].ylowin.at[j]] for j in range(quads)],
            [[kept.at[1, j], O.ret[tag].ycin.at[0, j], O.ret[tag].zhighin.at[j]] for j in range(quads)],
        ]
        if quads == 1:
            return [terms[0][0], terms[1][0]]
        tot, came = O.ret[tag].more
        for part in range(2):
            for j in range(quads):
                a, b, c = terms[part][j]
                blend([((a, b), tot.at[j, part])], w)
                blend([((tot.at[j, part], c), tot.at[j, part])], w)
        count = quads
        for i, bit in enumerate(reversed(y_bits[:-1])):
            count //= 2
            sems = S.ret[tag].hops[2]
            copy = send(
                tot.at[pl.ds(count, count)], came.at[pl.ds(count, count)],
                (sems.at[0, i], sems.at[1, i]), EXP, bit,
            )
            copy.start()
            copy.wait()
            for j in range(count):
                for part in range(2):
                    blend([((tot.at[j, part], came.at[count + j, part]), tot.at[j, part])], w)
        return [[tot.at[0, 0]], [tot.at[0, 1]]]

    def return_close(tag):
        for number in (1, 2):
            for which in range(2):
                hop(tag, number, which).wait_send()

    def output_phase(act, w, res, sems):
        def load(e, slot):
            return [
                pltpu.make_async_copy(O.act.at[e], act.at[slot], sems.at[slot, 0]),
                pltpu.make_async_copy(I.w_down.at[pair_at * local + e], w.at[slot], sems.at[slot, 1]),
            ]

        def store(e, slot):
            return pltpu.make_async_copy(res.at[slot], O.outs.at[e], sems.at[slot, 2])

        for copy in load(0, 0):
            copy.start()

        def body(e, carry):
            slot = lax.rem(e, jnp.int32(2))

            @pl.when(e + 1 < local)
            def _():
                for copy in load(e + 1, 1 - slot):
                    copy.start()

            for copy in load(e, slot):
                copy.wait()

            @pl.when(e >= 2)
            def _():
                store(e - 2, slot).wait()

            def part(b, carry):
                span = pl.ds(pl.multiple_of(b * block, 16), block)
                for c in range(0, width, 512):
                    res[slot, span, c : c + 512] = dot(act[slot, span], w[slot, c : c + 512], 1, 1).astype(BF16)
                value = S.d_gate[e, span]
                top = value.astype(BF16).astype(F32)
                lane = lax.broadcasted_iota(jnp.int32, (block, 128), 1).astype(F32)
                choice = I.choice[e, span]
                res[slot, span, width:] = jnp.where(
                    lane == choice, top, jnp.where(lane == choice + TOP, value - top, 0.0)
                ).astype(BF16)
                return carry

            lax.fori_loop(0, rows // block, part, 0)
            store(e, slot).start()
            return carry

        lax.fori_loop(0, local, body, 0)
        for e in range(max(0, local - 2), local):
            store(e, e % 2).wait()


    order = [(EXP, bit) for bit in exp_bits] + [(GRP, bit) for bit in [PAIR] + mids + [1]]
    left = [(GRP, bit) for bit in reversed(grp_bits)] + [(EXP, bit) for bit in reversed(exp_bits)]
    axis_of = []
    for name in order:
        axis_of.append(left.index(name))
        left.remove(name)
    share = share_rows(width, n_grp * n_exp)

    def all_part(tag, i, place):
        block = O.sums[tag].came[i - 1] if i else O.sums[tag].block
        return block.at[(slice(None),) * axis_of[i] + (place,)]

    def all_send(tag, i):
        sems = S.sums[tag]
        return send(
            all_part(tag, i, 1 - places[order[i]]), O.sums[tag].came[i], (sems.at[0, i], sems.at[1, i]), *order[i]
        )

    def all_step(tag, i):
        all_send(tag, i).wait_recv()
        came = O.sums[tag].came[i]
        last = i + 1 == len(order)

        def scoped(a, b, *rest):
            sems = rest[-1]
            loads = [
                pltpu.make_async_copy(all_part(tag, i, places[order[i]]), a, sems.at[0]),
                pltpu.make_async_copy(came, b, sems.at[1]),
            ]
            for copy in loads:
                copy.start()
            for copy in loads:
                copy.wait()
            if last:
                rest[0][...] = a[...].astype(F32) + b[...].astype(F32)
                store = pltpu.make_async_copy(rest[0], (O.qkv_out if tag else O.o_out), sems.at[0])
            else:
                lead = len(came.shape) - 2
                inner = max(0, lead - 1)

                def body(j, carry):
                    spots, rest_of = [], j
                    for _ in range(inner):
                        spots.insert(0, lax.rem(rest_of, jnp.int32(2)))
                        rest_of = lax.div(rest_of, jnp.int32(2))
                    spots = tuple(spots)
                    a[spots] = a[spots] + b[spots]
                    return carry

                lax.fori_loop(0, 2**inner, body, 0)
                store = pltpu.make_async_copy(a, came, sems.at[0])
            store.start()
            store.wait()

        buffer = pltpu.VMEM(came.shape, BF16)
        more = [pltpu.VMEM(came.shape, F32)] if last else []
        pl.run_scoped(scoped, buffer, buffer, *more, pltpu.SemaphoreType.DMA((2,)))
        if not last:
            all_send(tag, i + 1).start()

    def gain_send(i):
        axis, bit = order[i]
        sems = S.gall
        return send(O.gsum[i], O.gin[i], (sems.at[0, i], sems.at[1, i]), axis, bit)

    def gain_step(i):
        gain_send(i).wait_recv()

        def scoped(a, sems):
            came = pltpu.make_async_copy(O.gin[i], a, sems.at[0])
            came.start()
            came.wait()
            S.gain[...] = S.gain[...] + a[...]
            to = O.gains if i + 1 == len(order) else O.gsum[i + 1]
            store = pltpu.make_async_copy(S.gain, to, sems.at[0])
            store.start()
            store.wait()

        pl.run_scoped(scoped, pltpu.VMEM((8, width), F32), pltpu.SemaphoreType.DMA((1,)))
        if i + 1 < len(order):
            gain_send(i + 1).start()


    def norm_back(up, z, inverse, gain):
        normal = z * inverse
        scaled = up * gain
        mean = jnp.mean(scaled * normal, axis=-1, keepdims=True)
        return normal, inverse * (scaled - normal * mean)

    chunk_rows = 64

    def hidden_grad(terms, branch, dm, dh, wo, sems):
        for i in range(n_grp):
            pltpu.make_async_copy(I.wo.at[i], wo.at[pl.ds(i * rows_w, rows_w)], sems.at[0]).start()
        S.gain[...] = jnp.zeros_like(S.gain)

        def scoped(bufs, hid, up):
            for part in range(2):
                span = pl.ds(part * half, half)
                loads = [
                    pltpu.make_async_copy(term, bufs.at[i], sems.at[1 + i]) for i, term in enumerate(terms[part])
                ] + [
                    pltpu.make_async_copy(I.hidden.at[span], hid, sems.at[4]),
                    pltpu.make_async_copy(I.dy.at[span], up, sems.at[5]),
                ]
                for copy in loads:
                    copy.start()
                for copy in loads:
                    copy.wait()

                def body(j, carry):
                    r = pl.ds(pl.multiple_of(j * chunk_rows, chunk_rows), chunk_rows)
                    big = pl.ds(pl.multiple_of(part * half + j * chunk_rows, chunk_rows), chunk_rows)
                    d_n2 = bufs[0, r].astype(F32)
                    for i in range(1, len(terms[part])):
                        d_n2 = d_n2 + bufs[i, r].astype(F32)
                    normal, back = norm_back(d_n2, hid[r], I.inv_two[big], I.gains[1:2])
                    value = up[r].astype(F32) + back
                    dh[big] = value
                    branch[big] = value.astype(BF16)
                    S.gain[1:2] = S.gain[1:2] + jnp.sum(d_n2 * normal, axis=0, keepdims=True)
                    return carry

                lax.fori_loop(0, half // chunk_rows, body, 0)

        count = len(terms[0])
        pl.run_scoped(
            scoped, pltpu.VMEM((count, half, width), BF16), pltpu.VMEM((half, width), F32), pltpu.VMEM((half, width), BF16)
        )
        dh_out = pltpu.make_async_copy(dh, O.d_hidden, sems.at[1])
        dh_out.start()
        pltpu.make_async_copy(wo, wo, sems.at[0]).wait()

        def body(j, carry):
            r = pl.ds(pl.multiple_of(j * 256, 256), 256)
            for c in range(0, width, 512):
                dm[r, c : c + 512] = dot(branch[r], wo[c : c + 512], 1, 1).astype(BF16)
            return carry

        lax.fori_loop(0, length // 256, body, 0)
        dh_out.wait()

    def outer_grad(left, right, tag, buf, sems):
        dims = buf.shape[1:]
        lead = len(O.sums[tag].block.shape) - len(dims)
        steps = 2**lead
        tall = left.shape[1] // steps

        def store(j):
            spots, rest = [], j
            for _ in range(lead):
                spots.insert(0, lax.rem(rest, 2))
                rest = lax.div(rest, 2)
            slot = lax.rem(j, 2)
            return pltpu.make_async_copy(buf.at[slot], O.sums[tag].block.at[tuple(spots)], sems.at[slot])

        def body(j, carry):
            @pl.when(j >= 2)
            def _():
                store(j - 2).wait()

            cols = pl.ds(pl.multiple_of(j * tall, 128), tall)
            w = right.shape[1]
            for c in range(0, w, 512):
                part = dot(left[:, cols], right[:, c : c + 512], 0, 0).astype(BF16)
                buf[(lax.rem(j, 2),) + (slice(None),) * (len(dims) - 1) + (slice(c, c + 512),)] = part.reshape(
                    *dims[:-1], 512
                )
            store(j).start()
            return carry

        lax.fori_loop(0, steps, body, 0)
        for j in (steps - 2, steps - 1):
            store(jnp.int32(j)).wait()
        all_send(tag, 0).start()

    def attention(q, k, v, mixed, dm, dqkv, mask, dk_acc, dv_acc, dq_acc):
        for r in range(0, length, 256):
            key = lax.broadcasted_iota(jnp.int32, (256, length), 0) + r
            query = lax.broadcasted_iota(jnp.int32, (256, length), 1)
            tag = I.tagc[r : r + 256]
            inside = (tag == I.tagr[...]) & (tag > 0)
            mask[r : r + 256] = jnp.where((key <= query) | inside, 0.0, -1e30)

        def unturn(w):
            return w * I.cos[...] - pltpu.roll(w, HEAD_DIM // 2, 1) * I.sin[...]

        per = HEADS // KV_HEADS
        ones = jnp.ones((8, HEAD_DIM), F32)
        for g in range(KV_HEADS):
            kv = slice(g * HEAD_DIM, (g + 1) * HEAD_DIM)
            dk_acc[...] = jnp.zeros_like(dk_acc)
            dv_acc[...] = jnp.zeros_like(dv_acc)

            def head(i, carry):
                h = g * per + i
                cols = pl.ds(pl.multiple_of(h * HEAD_DIM, HEAD_DIM), HEAD_DIM)
                product = dm[:, cols].astype(F32) * mixed[:, cols].astype(F32)
                delta = lax.dot_general(
                    ones, product, (((1,), (1,)), ((), ())),
                    precision=lax.Precision.HIGHEST, preferred_element_type=F32,
                )[:1]
                lse = I.lse[h]
                dq_acc[...] = jnp.zeros_like(dq_acc)
                for r in range(0, length, 256):
                    start = max(0, r - 256)
                    qq, mm = q[start:, cols], dm[start:, cols]
                    kk, vv = k[r : r + 256, kv], v[r : r + 256, kv]
                    s = dot(kk, qq, 1, 1) * SCALE + mask[r : r + 256, start:]
                    p = jnp.exp(s - lse[:, start:])
                    dp = dot(vv, mm, 1, 1)
                    ds = (p * (dp - delta[:, start:])).astype(BF16)
                    dk_acc[r : r + 256] += dot(ds, qq)
                    dv_acc[r : r + 256] += dot(p.astype(BF16), mm)
                    dq_acc[start:] += dot(ds, kk, 0, 0)
                dqkv[:, cols] = unturn(dq_acc[...] * SCALE).astype(BF16)
                return carry

            lax.fori_loop(0, per, head, 0)
            first = HEADS * HEAD_DIM + g * HEAD_DIM
            dqkv[:, first : first + HEAD_DIM] = unturn(dk_acc[...] * SCALE).astype(BF16)
            first += KV_HEADS * HEAD_DIM
            dqkv[:, first : first + HEAD_DIM] = dv_acc[...].astype(BF16)

    def token_grad(dqkv, wqkv, sems):
        for i in range(n_grp):
            pltpu.make_async_copy(
                I.wqkv.at[i, pl.ds(0, rows_w)], wqkv.at[pl.ds(i * rows_w, rows_w)], sems.at[0]
            ).start()

        def scoped(dn, dh, x, res):
            pltpu.make_async_copy(wqkv, wqkv, sems.at[0]).wait()
            for part in range(2):
                span = pl.ds(part * half, half)
                loads = [
                    pltpu.make_async_copy(O.d_hidden.at[span], dh, sems.at[1]),
                    pltpu.make_async_copy(I.tokens.at[span], x, sems.at[2]),
                ]
                for copy in loads:
                    copy.start()
                for c in range(0, width, 512):
                    dn[:, c : c + 512] = dot(dqkv[part * half : (part + 1) * half], wqkv[c : c + 512], 1, 1)
                for copy in loads:
                    copy.wait()

                def body(j, carry):
                    r = pl.ds(pl.multiple_of(j * chunk_rows, chunk_rows), chunk_rows)
                    big = pl.ds(pl.multiple_of(part * half + j * chunk_rows, chunk_rows), chunk_rows)
                    d_n1 = dn[r]
                    normal, back = norm_back(d_n1, x[r].astype(F32), I.inv_one[big], I.gains[0:1])
                    res[r] = (dh[r] + back).astype(BF16)
                    S.gain[0:1] = S.gain[0:1] + jnp.sum(d_n1 * normal, axis=0, keepdims=True)
                    return carry

                lax.fori_loop(0, half // chunk_rows, body, 0)
                store = pltpu.make_async_copy(res, O.d_tokens.at[span], sems.at[3])
                store.start()
                store.wait()

        pl.run_scoped(
            scoped, pltpu.VMEM((half, width), F32), pltpu.VMEM((half, width), F32),
            pltpu.VMEM((half, width), BF16), pltpu.VMEM((half, width), BF16),
        )
        store = pltpu.make_async_copy(S.gain, O.gsum[0], sems.at[0])
        store.start()
        store.wait()
        gain_send(0).start()

    def layer_end(terms):
        def scoped(bufs, hid, res, extra, sems):
            for part in range(2):
                span = pl.ds(part * half, half)
                loads = [
                    pltpu.make_async_copy(term, bufs.at[i], sems.at[i]) for i, term in enumerate(terms[part])
                ] + [pltpu.make_async_copy(I.hidden.at[span], hid, sems.at[3])]
                for copy in loads:
                    copy.start()
                for copy in loads:
                    copy.wait()

                def body(j, carry):
                    r = pl.ds(pl.multiple_of(j * chunk_rows, chunk_rows), chunk_rows)
                    total = bufs[0, r].astype(F32)
                    for i in range(1, len(terms[part])):
                        total = total + bufs[i, r].astype(F32)
                    res[r] = (hid[r] + total[:, :width]).astype(BF16)
                    extra[r] = total[:, width:]
                    return carry

                lax.fori_loop(0, half // chunk_rows, body, 0)
                stores = [
                    pltpu.make_async_copy(res, O.layer.at[span], sems.at[0]),
                    pltpu.make_async_copy(extra, O.d_gates.at[span], sems.at[1]),
                ]
                for copy in stores:
                    copy.start()
                for copy in stores:
                    copy.wait()

        pl.run_scoped(
            scoped, pltpu.VMEM((len(terms[0]), half, wide), BF16), pltpu.VMEM((half, width), F32),
            pltpu.VMEM((half, width), BF16), pltpu.VMEM((half, 128), F32), pltpu.SemaphoreType.DMA((4,)),
        )


    chunks = 3 * local
    done = [4 if local == 4 else 0] + [0] * len(mids)

    def pump(*upto):
        for stage, last in enumerate(upto):
            if stage >= len(done):
                continue
            if local != 4 and last < chunks:
                continue
            if done[stage] < last:
                grads(stage, done[stage], last)
                done[stage] = last

    pl.run_scoped(
        experts,
        pltpu.VMEM((rows, width), BF16),
        pltpu.VMEM((rows, width), BF16),
        pltpu.VMEM((rows, ff), F32),
        pltpu.VMEM((width, 2 * ff), BF16),
        pltpu.VMEM((block, 2 * ff), F32),
        pltpu.VMEM((rows, 2 * ff), BF16),
        pltpu.VMEM((rows, ff), BF16),
        pltpu.VMEM((3, width // 2, ff), BF16),
        pltpu.VMEM((3, width // 2, ff), BF16),
        pltpu.VMEM((rows, width), BF16),
        pltpu.SemaphoreType.DMA((6,)),
    )
    pump(4, 1)
    collapse(0, width)
    pump(5, 2)
    pl.run_scoped(
        output_phase,
        pltpu.VMEM((2, rows, ff), BF16),
        pltpu.VMEM((2, width, ff), BF16),
        pltpu.VMEM((2, rows, wide), BF16),
        pltpu.SemaphoreType.DMA((2, 3)),
    )
    return_one(0, width)
    pump(6, 3)
    for s in range(seqs // 2):
        core_send(0, s).wait_send()
    collapse(1, wide)
    pump(7, 4)
    return_two(0, width)
    return_one(1, wide)
    pump(8, 5)

    def backward(branch, dm, mixed, sems):
        load = pltpu.make_async_copy(I.mixed, mixed, sems.at[0])
        load.start()
        load.wait()
        terms = return_end(0, width)
        pl.run_scoped(
            functools.partial(hidden_grad, terms, branch, dm),
            pltpu.VMEM((length, width), F32), pltpu.VMEM((width, width), BF16), pltpu.SemaphoreType.DMA((6,)),
        )
        pump(9, 6)
        def out_grad(left, buf, own):
            load = pltpu.make_async_copy(I.mixed_wide, left, own.at[0])
            load.start()
            load.wait()
            outer_grad(left, branch, 0, buf, own)

        tall = share * n_grp * n_exp
        step = [2] * 3 if share > 16 else [2] * 4
        pl.run_scoped(
            out_grad, pltpu.VMEM((length, tall), BF16), pltpu.VMEM((2, *step, share, width), BF16), pltpu.SemaphoreType.DMA((2,))
        )

        def rest(dqkv):
            def first(q, k, v, *acc):
                loads = [
                    pltpu.make_async_copy(I.q, q, sems.at[0]),
                    pltpu.make_async_copy(I.k, k, sems.at[1]),
                    pltpu.make_async_copy(I.v, v, sems.at[2]),
                ]
                for copy in loads:
                    copy.start()
                for copy in loads:
                    copy.wait()
                attention(q, k, v, mixed, dm, dqkv, *acc)

            kv = KV_HEADS * HEAD_DIM
            pl.run_scoped(
                first, pltpu.VMEM((length, width), BF16), pltpu.VMEM((length, kv), BF16), pltpu.VMEM((length, kv), BF16),
                pltpu.VMEM((length, length), F32), pltpu.VMEM((length, HEAD_DIM), F32),
                pltpu.VMEM((length, HEAD_DIM), F32), pltpu.VMEM((length, HEAD_DIM), F32),
            )
            pump(10, 7)
            all_step(0, 0)
            pl.run_scoped(
                functools.partial(token_grad, dqkv),
                pltpu.VMEM((width, qkv), BF16), pltpu.SemaphoreType.DMA((4,)),
            )

            def second(n1, buf, own):
                load = pltpu.make_async_copy(I.n1, n1, own.at[0])
                load.start()
                load.wait()
                outer_grad(n1, dqkv, 1, buf, own)

            pl.run_scoped(
                second, pltpu.VMEM((length, tall), BF16), pltpu.VMEM((2, *step, share, qkv), BF16), pltpu.SemaphoreType.DMA((2,))
            )

        pl.run_scoped(rest, pltpu.VMEM((length, qkv), BF16))

    pl.run_scoped(
        backward, pltpu.VMEM((length, width), BF16), pltpu.VMEM((length, width), BF16),
        pltpu.VMEM((length, width), BF16), pltpu.SemaphoreType.DMA((3,)),
    )
    pump(11, 8)
    return_two(1, wide)
    all_step(1, 0)
    gain_step(0)
    all_step(0, 1)
    pump(12, 9)
    all_step(1, 1)
    gain_step(1)
    all_step(0, 2)
    layer_end(return_end(1, wide))
    pump(12, 10)
    for i in range(2, len(order)):
        all_step(1, i)
        gain_step(i)
        if i + 1 < len(order):
            all_step(0, i + 1)
        if i == 2:
            pump(12, 11)
    pump(*([chunks] * (len(mids) + 1)))

    def close(c, carry):
        for stage in range(len(mids) + 1):
            grad_send(stage, c).wait_send()
        pair_send(c).wait()
        return carry

    lax.fori_loop(0, chunks, close, 0)
    return_close(0)
    return_close(1)
    for s in range(seqs // 2):
        core_send(1, s).wait_send()
    for i in range(len(order)):
        all_send(0, i).wait_send()
        all_send(1, i).wait_send()
        gain_send(i).wait_send()


def mega(dims, arrays, near):
    outs, sems = mega_plan(*dims)
    in_leaves, in_tree = jax.tree.flatten(dict(arrays, **near))
    inside = {id(value) for value in near.values()}
    out_leaves, out_tree = jax.tree.flatten(outs)
    sem_leaves, sem_tree = jax.tree.flatten(sems)
    results = pl.pallas_call(
        functools.partial(mega_body, dims, in_tree, out_tree, sem_tree),
        in_specs=[WHOLE if id(leaf) in inside else ANY for leaf in in_leaves],
        out_specs=[ANY] * len(out_leaves),
        out_shape=out_leaves,
        scratch_shapes=sem_leaves,
        compiler_params=pltpu.CompilerParams(vmem_limit_bytes=VMEM, collective_id=0, has_side_effects=True),
        name="experts_and_back",
    )(*in_leaves)
    return space(jax.tree.unflatten(out_tree, results))


def shards(
    tokens,
    cotangent,
    gate_logits,
    routes,
    piece_starts,
    piece_kinds,
    q_weight,
    k_weight,
    v_weight,
    o_weight,
    attn_gain,
    moe_gain,
    gate_weight,
    up_weight,
    down_weight,
):
    grp, exp = lax.axis_index(GRP), lax.axis_index(EXP)
    n_grp, n_exp = lax.axis_size(GRP), lax.axis_size(EXP)
    devices = n_grp * n_exp
    length, width = tokens.shape
    local = gate_weight.shape[0] // 2
    q_width, kv_width = q_weight.shape[1], k_weight.shape[1]
    rows_w = q_weight.shape[0]
    dims = (local, 2 * n_exp, length, width, gate_weight.shape[2], n_grp, n_exp, rows_w)

    gates = jax.nn.softmax(gate_logits, axis=-1)
    small = jnp.concatenate([routes.T.astype(F32), gates.T], axis=0)
    gains = jnp.pad(jnp.stack([attn_gain, moe_gain]), ((0, 14), (0, q_width + 2 * kv_width - rows_w)))
    shard = jnp.concatenate([jnp.concatenate([q_weight, k_weight, v_weight], axis=1), gains], axis=0)
    cosine, sine = rope_tables(length)
    tags = piece_tags(piece_starts[0], piece_kinds[0], length)
    tagc, tagr = tags.reshape(length, 1), tags.reshape(1, length)

    a = front(
        dims,
        dict(
            tokens=tokens, dy=cotangent, small=small, wq=shard, wo=o_weight, w_down=down_weight,
            cos=cosine, sin=sine, tagc=tagc, tagr=tagr,
        ),
    )
    r = mega(
        dims,
        dict(
            x=a.x, y=a.y, t=a.t, w_gate=gate_weight, w_up=up_weight, w_down=down_weight, hidden=a.hidden,
            dy=cotangent, wo=a.wo, mixed=a.mixed, q=a.q, k=a.k, v=a.v, wqkv=a.wq, tokens=tokens,
            n1=spread(a.n1, devices), mixed_wide=spread(a.mixed, devices),
        ),
        dict(
            gate=a.gate, choice=a.choice, rank=a.rank, inv_one=a.inv_one, inv_two=a.inv_two, gains=a.gains,
            lse=a.lse.reshape(HEADS, 1, length), cos=cosine, sin=sine, tagc=tagc, tagr=tagr,
        ),
    )
    d_gates = r.d_gates[:, :TOP] + r.d_gates[:, TOP : 2 * TOP]
    logits_grad = gates * (d_gates - jnp.sum(gates * d_gates, axis=-1, keepdims=True))
    share = width // devices
    own = lax.dynamic_slice_in_dim(r.gains, (grp * n_exp + exp) * share, share, 1)
    return (
        r.layer,
        r.d_tokens,
        logits_grad,
        r.qkv_out[:share, :q_width],
        r.qkv_out[:share, q_width : q_width + kv_width],
        r.qkv_out[:share, q_width + kv_width :],
        r.o_out[:share],
        own[0],
        own[1],
        *[r.final[kind].astype(F32) for kind in range(3)],
    )


def solution(mesh):
    rows = P((GRP, EXP), None)
    placed = (rows,) * 6 + (P(GRP, None),) * 4 + (P(GRP),) * 2 + (P(EXP, None, None),) * 3
    outs = (rows,) * 7 + (P((GRP, EXP)),) * 2 + (P(EXP, GRP, None),) * 3
    return jax.shard_map(shards, mesh=mesh, in_specs=placed, out_specs=outs, check_vma=False)
```

time: 1960 us -> 920 us (0.47)
  waiting for transfers between devices: 1110 us -> 0 us
  Pallas kernels: 0 us -> 875 us
  matrix products: 314 us -> 0 us
  local copies, waits for them, and re-layouts: 197 us -> 12.7 us
  other arithmetic: 155 us -> 19.6 us
  blocking collectives: 133 us -> 0 us
  starting transfers between devices: 25.1 us -> 0 us
    pallas_call x0 -> x2, Pallas kernels: none -> 875 us  [the longest x1 569 us: mega(): pl.pallas_call(functools.partial(mega_body, dims, in_tree, out_tree, sem_...]
    reduce_scatter x7 -> x0, waiting for transfers between devices: 824 us -> none  [the longest x1 312 us: shards(): lax.psum_scatter(grad_up.astype(jnp.bfloat16), 'grp', scatter_dimension=1...]
    dot_general x27 -> x0, matrix products: 314 us -> none  [the longest x1 27.2 us: shards(): jnp.einsum('secd,edf->secf', grad_received, down_weight, preferred_elemen...]
    all_to_all x4 -> x0, waiting for transfers between devices: 286 us -> none  [the longest x1 82.7 us: shards(): lax.all_to_all(slot_grad.reshape(n_exp, local_experts, CAP, model_width),...]
    gather x5 -> x0, local copies, waits for them, and re-layouts: 107 us -> none  [the longest x1 25.7 us: shards(): returned_grad.reshape(EXPERTS * CAP, model_width)[positions]]
    all_gather x2 -> x0, blocking collectives: 67.8 us -> none  [the longest x1 33.9 us: shards(): lax.all_gather(v_weight, 'grp', axis=0, tiled=True)]
    unnamed x2 -> x0, blocking collectives: 65.4 us -> none
    reduce_sum x8 -> x2, other arithmetic: 63.4 us -> 1.47 us  [the longest x1 0.74 us: piece_tags(): jnp.sum(jnp.where(piece_of[:, None] == slot_ids[None, :], kinds[None, :],...]
  transfers between devices with their start and end apart: 13 -> 0, of which waited for: 10 -> 0; matrix products, arithmetic and copies ran while one was open for 30% -> 0% of each run, Pallas kernels for 0% -> 0%
where the time goes in v2:
time: 920 us; the launch traced here: 909 us
  Pallas kernels  875 us (95%)
  other arithmetic  19.6 us (2%)
  local copies, waits for them, and re-layouts  12.7 us (1%)
    pallas_call x1, Pallas kernels, mega(): pl.pallas_call(functools.partial(mega_body, dims, in_tree, out_tree, sem_...  569 us
    pallas_call x1, Pallas kernels, front(): pl.pallas_call(functools.partial(front_body, dims, in_tree, out_tree, sem...  306 us

profile of v2, /device:TPU:0, one launch (start us, length us, event | category | flops | bytes accessed | tf_op | source)
XLA Modules:
  0.0 908.6 jit_solution(8121958022652169272)
XLA Ops:
  0.6 0.0 copy-start.2
  0.7 0.8 reduce_max.9
  1.4 0.7 fusion.7
  2.2 0.2 copy.58
  2.4 0.2 fusion.6
  2.5 0.1 copy.59
  2.7 0.7 convert_bitcast_fusion
  3.4 0.6 pad_maximum_fusion.1.refs_3_
  4.0 0.7 convert_reduce_fusion
  4.8 0.7 select_reduce_fusion
  5.5 0.9 select_n.36.refs_4_.refs_17_
  6.5 0.6 select_n.34.refs_5_.refs_18_
  7.0 0.7 stack.10
  7.7 0.7 stack.9
  8.4 0.0 copy-done.2
  8.4 2.0 pad_maximum_fusion.refs_9_
  10.3 305.9 %front.1 = (f32[4,896,1]{2,1,0:T(8,128)}, bf16[8,768,1536]{2,1,0:T(8,128)(2,1)}, f32[8,1536]{1,0:T(8,128)}, f32[4,896,1]{2,1,0:T(8,128)}, f32[768,1536]{1,0:T(8,...) custom-call(f32[768,128]{1,0:T(8,128)} %constant.34.clone.refs_0_.re, ...), custom_call_target="tpu_custom_call" | custom-call | tf_op jit(solution)/shard_map/front/pallas_call | solution.py:664
  316.2 3.6 reduce
  319.9 0.6 reshape.79.refs_9_
  320.5 569.2 %experts_and_back.1 = (bf16[4,896,768]{2,1,0:T(8,128)(2,1)}, bf16[12,768,768]{2,1,0:T(8,128)(2,1)}, bf16[12,384,768]{2,1,0:T(8,128)(2,1)}, f32[768,128]{1,0:T(8,...) custom-call(f32[4,896,1]{2,1,0:T(8,128)} %get-tuple-element.37.refs_, ...), custom_call_target="tpu_custom_call" | custom-call | tf_op jit(solution)/shard_map/experts_and_back/pallas_call | solution.py:1690
  889.8 8.7 bitcast_convert_fusion
  898.5 0.4 multiply_reduce_fusion
  898.9 0.4 subtract_multiply_fusion
  899.3 0.8 copy.62
  900.0 0.7 slice.32
  900.8 0.6 fusion.8
  901.4 0.9 constant_dynamic-slice_fusion
  902.3 0.5 slice_bitcast_fusion
  902.8 3.2 copy.67
  906.0 1.4 copy.68
  907.4 0.0 copy-done.4
  907.4 0.7 copy.69
  (10 shorter events, 0.0 us)
Async XLA Ops:
  0.6 7.7 copy-start.2
  889.8 8.7 copy-start
  898.5 1.5 copy-start.3
  900.7 5.3 copy-start.1
  906.0 1.4 copy-start.4

commit v3 on v2

--- a/solution.py
+++ b/solution.py
@@ -226,14 +226,26 @@
     small.append(spread_send(O.small, S.small, len(y_bits) + 1, EXP, CORE, 0, first, first))
     dy_y = y_spread(O.dy, S.dy, 0, 0, y_bits)
     n_y = len(y_bits)
-    dy_z = spread_send(O.dy, S.dy, n_y, GRP, PAIR, 0, 1, quads)
-    dy_zy = y_spread(O.dy, S.dy, n_y + 1, quads, y_bits)
+    quarter = length // 4
+
+    def dy_z(j):
+        part = pl.ds(pl.multiple_of(j * quarter, 16), quarter)
+        return send(O.dy.at[0, part], O.dy.at[quads, part], S.dyz.at[j], partner[GRP, PAIR])
+
+    def dy_on(j):
+        part = pl.ds(pl.multiple_of(j * quarter, 16), quarter)
+        return send(O.dy.at[quads, part], O.dy.at[quads + 1, part], S.dyy.at[j], partner[EXP, y_bits[0]])
+
+    def dy_pass(j):
+        dy_z(j).wait_recv()
+        dy_on(j).start()
+
+    dy_zy = y_spread(O.dy, S.dy, n_y, quads, y_bits)[1:]
     dy_core = [core_spread(O.dy, S.dy, 2 * n_y + 1 + i, i) for i in range(first)]
     for copy in small:
         copy.start()
         copy.wait_recv()
     dy_y[0].start()
-    dy_z.start()
 
 
     def slots(info, tri, sem):
@@ -374,6 +386,14 @@
                         def _():
                             ring_step(1, j)
 
+                        @pl.when(j <= 4)
+                        def _():
+                            dy_z(j - 1).start()
+
+                        @pl.when((j >= 3) & (j <= 4))
+                        def _():
+                            dy_pass(j - 3)
+
                         return carry
 
                     lax.fori_loop(lax.max((p - 1) * every + 1, 1), lax.max(p * every + 1, 1), hop, 0)
@@ -430,6 +450,7 @@
         for copy in outs:
             copy.start()
         outs[0].wait()
+        dy_pass(jnp.int32(3))
         n2_start()
         outs[1].wait()
 
@@ -480,7 +501,10 @@
         for i in range(first):
             @pl.when(step == 2 * i)
             def _():
-                if i == quads:
+                if i == quads + 1:
+                    if not dy_zy:
+                        for j in range(4):
+                            dy_on(jnp.int32(j)).wait_recv()
                     for j in range(1, quads):
                         dy_core[quads + j].start()
 
@@ -489,7 +513,7 @@
                 dy_core[i].wait_recv()
 
 
-    def gather(all_ref, out_ref, ready, with_slots):
+    def gather(all_ref, out_ref, ready, with_slots, begin, end):
         chunk = 512
 
         def scoped(in_buf, out_buf, in_sem, out_sem):
@@ -512,7 +536,7 @@
                 fetch(step, slot).start()
                 fetch(step, slot).wait()
 
-                @pl.when(step >= 2)
+                @pl.when(step >= begin + 2)
                 def _():
                     for e in range(local):
                         leaving(step - 2, slot, e).wait()
@@ -535,8 +559,8 @@
                     leaving(step, slot, e).start()
                 return carry
 
-            lax.fori_loop(0, seqs, body, 0)
-            for step in (seqs - 2, seqs - 1):
+            lax.fori_loop(begin, end, body, 0)
+            for step in (end - 2, end - 1):
                 for e in range(local):
                     leaving(jnp.int32(step), step % 2, e).wait()
 
@@ -544,36 +568,6 @@
             scoped, pltpu.VMEM((2, length, width), BF16), pltpu.VMEM((2, local * CAP, width), BF16),
             pltpu.SemaphoreType.DMA((2,)), pltpu.SemaphoreType.DMA((2, local)),
         )
-
-    def upstream(y, w, t, sems):
-        rows = seqs * CAP
-        block = 448 if rows % 448 == 0 else rows
-
-        def body(e, carry):
-            loads = [
-                pltpu.make_async_copy(O.y.at[e], y, sems.at[0]),
-                pltpu.make_async_copy(I.w_down.at[pair_at * local + e], w, sems.at[1]),
-            ]
-            for copy in loads:
-                copy.start()
-            for copy in loads:
-                copy.wait()
-
-            @pl.when(e >= 1)
-            def _():
-                pltpu.make_async_copy(t, O.t.at[e], sems.at[2]).wait()
-
-            def part(b, carry):
-                span = pl.ds(pl.multiple_of(b * block, 16), block)
-                t[span] = dot(y[span], w[...])
-                return carry
-
-            lax.fori_loop(0, rows // block, part, 0)
-            pltpu.make_async_copy(t, O.t.at[e], sems.at[2]).start()
-            return carry
-
-        lax.fori_loop(0, local, body, 0)
-        pltpu.make_async_copy(t, O.t.at[0], sems.at[2]).wait()
 
 
     def attend_and_project(mixed, sems):
@@ -587,28 +581,32 @@
                 dy_y[i + 1].start()
         for i in range(quads):
             dy_core[i].start()
-        dy_z.wait_recv()
-        dy_zy[0].start()
-        dy_core[quads].start()
         ring_end(1)
+        dy_pass(jnp.int32(2))
         pl.run_scoped(
             lambda wo, n2, hid: projection(mixed, wo, n2, hid, sems),
             pltpu.VMEM((width, width), BF16), pltpu.VMEM((length, width), BF16), pltpu.VMEM((length, width), F32),
         )
 
     pl.run_scoped(attend_and_project, pltpu.VMEM((length, HEADS * HEAD_DIM), BF16), pltpu.SemaphoreType.DMA((3,)))
-    for i, copy in enumerate(dy_zy):
-        copy.wait_recv()
-        if i + 1 < n_y:
-            dy_zy[i + 1].start()
-    gather(O.dy, O.y, dy_ready, True)
-    rows = seqs * CAP
-    pl.run_scoped(
-        upstream, pltpu.VMEM((rows, width), BF16), pltpu.VMEM((width, ff), BF16), pltpu.VMEM((rows, ff), F32),
-        pltpu.SemaphoreType.DMA((3,)),
-    )
-    gather(O.n2, O.x, n2_ready, False)
-    for copy in small + dy_y + [dy_z] + dy_zy + dy_core + n2_pre + [n2_y, n2_z, n2_low, n2_high] + n2_core:
+    def rest_of_dy():
+        dy_core[quads].start()
+        if dy_zy:
+            for j in range(4):
+                dy_on(jnp.int32(j)).wait_recv()
+            for copy in dy_zy:
+                copy.start()
+                copy.wait_recv()
+
+    gather(O.dy, O.y, dy_ready, True, 0, 2 * quads)
+    gather(O.n2, O.x, n2_ready, False, 0, 2 * mid)
+    rest_of_dy()
+    gather(O.dy, O.y, dy_ready, True, 2 * quads, seqs)
+    gather(O.n2, O.x, n2_ready, False, 2 * mid, seqs)
+    for j in range(4):
+        dy_z(jnp.int32(j)).wait_send()
+        dy_on(jnp.int32(j)).wait_send()
+    for copy in small + dy_y + dy_zy + dy_core + n2_pre + [n2_y, n2_z, n2_low, n2_high] + n2_core:
         copy.wait_send()
 
 
@@ -641,7 +639,6 @@
         hidden=shape(length, width, dtype=F32),
         x=shape(local, rows, width),
         y=shape(local, rows, width),
-        t=shape(local, rows, ff, dtype=F32),
     )
     hops = n_grp // 2 + 1
     dma = pltpu.SemaphoreType.DMA
@@ -651,19 +648,20 @@
         own=dma((4,)),
         small=dma((n_y + 2, 2)),
         dy=dma((2 * n_y + 1 + seqs // 2, 2)),
+        dyz=dma((4, 2)),
+        dyy=dma((4, 2)),
         n2=dma((n_y + 3 + seqs // 2, 2)),
         gate=pltpu.VMEM((seqs, 8, length), F32),
         number=pltpu.VMEM((seqs, 8, length), F32),
     )
     outs = dict(vmem, **hbm)
     in_leaves, in_tree = jax.tree.flatten(arrays)
-    far = {id(arrays["w_down"])}
     out_leaves, out_tree = jax.tree.flatten(outs)
     near = {id(value) for value in vmem.values()}
     sem_leaves, sem_tree = jax.tree.flatten(scratch)
     results = pl.pallas_call(
         functools.partial(front_body, dims, in_tree, out_tree, sem_tree),
-        in_specs=[ANY if id(leaf) in far else WHOLE for leaf in in_leaves],
+        in_specs=[WHOLE] * len(in_leaves),
         out_specs=[WHOLE if id(leaf) in near else ANY for leaf in out_leaves],
         out_shape=out_leaves,
         scratch_shapes=sem_leaves,
@@ -699,7 +697,7 @@
     share = share_rows(width, n_grp * n_exp)
     dma = pltpu.SemaphoreType.DMA
 
-    def returned(w):
+    def first_return(w):
         quad = shape(quads, half, w)
         two = shape(2, quads, half, w)
         more = [shape(quads, 2, half, w)] * 2 if quads > 1 else []
@@ -707,6 +705,11 @@
             came=shape(seqs // 2, length, w), kept=shape(4, quads, half, w),
             zc=two, yc=two, zcin=two, ycin=two, ylow=quad, zhigh=quad, ylowin=quad, zhighin=quad, more=more,
         )
+
+    def second_return(w):
+        one, two = shape(quads, 2, half, w), shape(2, quads, 2, half, w)
+        more = [one] * 2 if quads > 1 else []
+        return dict(came=shape(seqs // 2, length, w), out=two, outin=two, pair=one, pairin=one, own=one, more=more)
 
     def summed(w):
         return dict(
@@ -727,14 +730,12 @@
         mine=shape(chunks, width // 2, ff),
         come=[shape(chunks, width >> (i + 1), ff) for i in range(len(mids) + 1)],
         act=shape(local, rows, ff),
+        d=shape(local, rows, 2 * ff),
         outs=shape(local, rows, wide),
         far=shape(seqs // 2, length, wide),
-        near=shape(seqs // 2, length, wide),
-        ret=[returned(width), returned(wide)],
+        ret=[first_return(width), second_return(wide)],
         d_hidden=shape(length, width, dtype=F32),
         sums=[summed(width), summed(qkv)],
-        gsum=[gain] * stages,
-        gin=[gain] * stages,
     )
     hops = [dma((2, 2)), dma((2, 2)), dma((2, n_exp.bit_length()))]
     sems = dict(
@@ -744,7 +745,8 @@
         grad=[dma((2, chunks))] * (len(mids) + 1),
         pair=dma((2, chunks)),
         d_gate=pltpu.VMEM((local, rows, 1), F32),
-        gain=pltpu.VMEM((8, width), F32),
+        gain=pltpu.VMEM((stages + 1, 8, width), F32),
+        gin=pltpu.VMEM((stages, 8, width), F32),
     )
     return outs, sems
 
@@ -877,33 +879,29 @@
     bands = width // band
     keep = band // 2
 
-    def expert(e, x, y, t, w, gu, d, act, theirs, mine, dx, sems):
+    slots = 2 if rows <= 1024 else 1
+
+    def expert_loads(e, slot, x, y, w, wd, sems):
         index = pair_at * local + e
-        copies = [
-            pltpu.make_async_copy(I.x.at[e], x, sems.at[0]),
-            pltpu.make_async_copy(I.w_gate.at[index], w.at[:, pl.ds(0, ff)], sems.at[1]),
-            pltpu.make_async_copy(I.w_up.at[index], w.at[:, pl.ds(ff, ff)], sems.at[2]),
-            pltpu.make_async_copy(I.t.at[e], t, sems.at[3]),
-            pltpu.make_async_copy(I.y.at[e], y, sems.at[4]),
+        return [
+            pltpu.make_async_copy(I.x.at[e], x.at[slot], sems.at[slot, 0]),
+            pltpu.make_async_copy(I.w_gate.at[index], w.at[slot, :, pl.ds(0, ff)], sems.at[slot, 1]),
+            pltpu.make_async_copy(I.w_up.at[index], w.at[slot, :, pl.ds(ff, ff)], sems.at[slot, 2]),
+            pltpu.make_async_copy(I.y.at[e], y.at[slot], sems.at[slot, 3]),
+            pltpu.make_async_copy(I.w_down.at[index], wd.at[slot], sems.at[slot, 4]),
         ]
-        for copy in copies:
-            copy.start()
-        for copy in copies[:3]:
-            copy.wait()
-
+
+    def expert(e, slot, x, y, w, wd, gu, t, d, act, dx, sems, out_sems):
         def forward(b, carry):
             span = pl.ds(pl.multiple_of(b * block, 16), block)
-            gu[...] = dot(x[span], w[...])
-
-            @pl.when(b == 0)
-            def _():
-                copies[3].wait()
+            gu[...] = dot(x[slot, span], w[slot])
+            t[...] = dot(y[slot, span], wd[slot])
 
             def point(i, carry):
                 inner = pl.ds(pl.multiple_of(i * 64, 64), 64)
                 outer = pl.ds(pl.multiple_of(b * block + i * 64, 64), 64)
                 g, u = gu[inner, :ff], gu[inner, ff:]
-                tt, gate = t[outer], I.gate[e, outer]
+                tt, gate = t[inner], I.gate[e, outer]
                 sig = 1.0 / (1.0 + jnp.exp(-g))
                 silu = g * sig
                 a32 = (silu * u).astype(BF16).astype(F32)
@@ -917,9 +915,36 @@
             return lax.fori_loop(0, block // 64, point, carry)
 
         lax.fori_loop(0, rows // block, forward, 0)
-        copies[4].wait()
-        act_out = pltpu.make_async_copy(act, O.act.at[e], sems.at[0])
-        act_out.start()
+        stores = [
+            pltpu.make_async_copy(act, O.act.at[e], out_sems.at[0]),
+            pltpu.make_async_copy(d, O.d.at[e], out_sems.at[1]),
+        ]
+        for copy in stores:
+            copy.start()
+
+        def back(b, carry):
+            span = pl.ds(pl.multiple_of(b * block, 16), block)
+            for c in range(0, width, 512):
+                dx[span, c : c + 512] = dot(d[span], w[slot, c : c + 512], 1, 1).astype(BF16)
+            return carry
+
+        lax.fori_loop(0, rows // block, back, 0)
+        stores.append(pltpu.make_async_copy(dx, O.outs.at[e, :, pl.ds(0, width)], out_sems.at[2]))
+        stores[-1].start()
+        for copy in stores:
+            copy.wait()
+
+    def expert_grads(e, x, y, d, act, theirs, mine, sems):
+        copies = [
+            pltpu.make_async_copy(I.x.at[e], x, sems.at[0]),
+            pltpu.make_async_copy(O.d.at[e], d, sems.at[1]),
+            pltpu.make_async_copy(I.y.at[e], y, sems.at[2]),
+            pltpu.make_async_copy(O.act.at[e], act, sems.at[3]),
+        ]
+        for copy in copies:
+            copy.start()
+        for copy in copies[:2]:
+            copy.wait()
 
         def split(j, k, res):
             res = res.astype(BF16)
@@ -949,106 +974,192 @@
             ]
 
         lax.fori_loop(0, bands, band_gate, 0)
-        early = store(0, 2, 1)
+        early = store(0, 2, 0)
         for copy in early:
             copy.start()
+        for copy in copies[2:]:
+            copy.wait()
         lax.fori_loop(0, bands, band_down, 0)
-        late = store(2, 1, 3)
+        late = store(2, 1, 2)
         for copy in late:
             copy.start()
         for copy in early:
             copy.wait()
         for k in range(2):
             grad_send(0, 3 * e + k).start()
-
-        def back(b, carry):
-            span = pl.ds(pl.multiple_of(b * block, 16), block)
-            for c in range(0, width, 512):
-                dx[span, c : c + 512] = dot(d[span], w[c : c + 512], 1, 1).astype(BF16)
-            return carry
-
-        lax.fori_loop(0, rows // block, back, 0)
-        dx_out = pltpu.make_async_copy(dx, O.outs.at[e, :, pl.ds(0, width)], sems.at[5])
-        dx_out.start()
         for copy in late:
             copy.wait()
         grad_send(0, 3 * e + 2).start()
-        act_out.wait()
-        dx_out.wait()
-
-    def experts(*scratch):
-        def body(e, carry):
-            expert(e, *scratch)
-            if local == 4:
-                grads(0, lax.max(e - 1, 0), e + lax.div(e, jnp.int32(3)))
-            return carry
-
-        lax.fori_loop(0, local, body, 0)
-
-
-    def collapse(tag, w):
-        first = seqs // 2
-        far, near = O.far, O.near
+
+    def forward_of(first, last):
+        def scoped(x, y, w, wd, *rest):
+            sems = rest[-2]
+
+            def load(e, slot):
+                return expert_loads(e, slot, x, y, w, wd, sems)
+
+            if slots == 2:
+                for copy in load(jnp.int32(first), 0):
+                    copy.start()
+
+            def body(e, carry):
+                slot = lax.rem(e - first, jnp.int32(slots))
+
+                @pl.when(e + 1 < last + 2 - slots)
+                def _():
+                    for copy in load(e if slots == 1 else e + 1, 0 if slots == 1 else 1 - slot):
+                        copy.start()
+
+                for copy in load(e, slot):
+                    copy.wait()
+                expert(e, slot, x, y, w, wd, *rest)
+                if local == 4 and first > 0:
+                    grads(0, lax.max(e - 2, 0), lax.max(e - 1, 0))
+                return carry
+
+            lax.fori_loop(first, last, body, 0)
+
+        if first == last:
+            return
+        pl.run_scoped(
+            scoped,
+            pltpu.VMEM((slots, rows, width), BF16),
+            pltpu.VMEM((slots, rows, width), BF16),
+            pltpu.VMEM((slots, width, 2 * ff), BF16),
+            pltpu.VMEM((slots, width, ff), BF16),
+            pltpu.VMEM((block, 2 * ff), F32),
+            pltpu.VMEM((block, ff), F32),
+            pltpu.VMEM((rows, 2 * ff), BF16),
+            pltpu.VMEM((rows, ff), BF16),
+            pltpu.VMEM((rows, width), BF16),
+            pltpu.SemaphoreType.DMA((slots, 5)),
+            pltpu.SemaphoreType.DMA((3,)),
+        )
+
+    def grads_of(first, last):
+        def scoped(*scratch):
+            def body(e, carry):
+                expert_grads(e, *scratch)
+                return carry
+
+            lax.fori_loop(first, last, body, 0)
+
+        pl.run_scoped(
+            scoped,
+            pltpu.VMEM((rows, width), BF16),
+            pltpu.VMEM((rows, width), BF16),
+            pltpu.VMEM((rows, 2 * ff), BF16),
+            pltpu.VMEM((rows, ff), BF16),
+            pltpu.VMEM((3, width // 2, ff), BF16),
+            pltpu.VMEM((3, width // 2, ff), BF16),
+            pltpu.SemaphoreType.DMA((4,)),
+        )
+
+
+    first = seqs // 2
+    turns = (3, 1, 2, 0)
+
+    def item_of(step):
+        quad = lax.div(step, jnp.int32(quads))
+        start = sum(jnp.where(quad == i, turn * quads, 0) for i, turn in enumerate(turns))
+        return start + lax.rem(step, jnp.int32(quads))
+
+    def collapse(tag, w, near):
         cols = pl.ds(0, w)
+        r = O.ret[tag]
+        low, high = pl.ds(0, half), pl.ds(half, half)
         spans = [(c, min(512, w - c)) for c in range(0, w, 512)]
 
-        def scoped(in_buf, out_buf, in_sem, out_sem):
+        def scoped(in_buf, out_buf, came, in_sem, out_sem, came_sem):
             def coming(step, slot, e):
-                s = lax.rem(step + first, jnp.int32(seqs))
+                s = item_of(step) + (0 if near else first)
                 return pltpu.make_async_copy(
                     O.outs.at[e, pl.ds(pl.multiple_of(s * CAP, 16), CAP), cols],
                     in_buf.at[slot, pl.ds(e * CAP, CAP)],
                     in_sem.at[slot, e],
                 )
 
-            def leave(step, slot):
-                pltpu.make_async_copy(out_buf.at[slot], near.at[0, :, cols], out_sem.at[slot]).wait()
-
-                @pl.when(step < first)
-                def _():
-                    core_send(tag, step).start()
+            def came_load(step, slot):
+                return pltpu.make_async_copy(r.came.at[item_of(step)], came.at[slot], came_sem.at[slot])
+
+            def leaving(slot, to_low, to_high):
+                return [
+                    pltpu.make_async_copy(out_buf.at[slot, low], to_low, out_sem.at[slot, 0]),
+                    pltpu.make_async_copy(out_buf.at[slot, high], to_high, out_sem.at[slot, 1]),
+                ]
+
+            def left(step, slot):
+                for p in range(2):
+                    span = out_buf.at[slot, (low, high)[p]]
+                    pltpu.make_async_copy(span, span, out_sem.at[slot, p]).wait()
+                if near:
+                    for i, which in ((1, 1), (2, 0)) if tag == 0 else ((1, 0),):
+                        @pl.when(step == (i + 1) * quads - 1)
+                        def _():
+                            (hop(0, 1, which) if tag == 0 else out_hop(which)).start()
+                else:
+                    core_send(tag, item_of(step)).start()
 
             for e in range(local):
-                coming(0, 0, e).start()
+                coming(jnp.int32(0), 0, e).start()
 
             def body(step, carry):
                 slot = lax.rem(step, jnp.int32(2))
 
-                @pl.when(step + 1 < seqs)
+                @pl.when(step + 1 < first)
                 def _():
                     for e in range(local):
                         coming(step + 1, 1 - slot, e).start()
 
+                @pl.when(step >= 1)
+                def _():
+                    left(step - 1, 1 - slot)
+
+                if near:
+                    core_send(tag, item_of(step)).wait_recv()
+                    came_load(step, slot).start()
                 for e in range(local):
                     coming(step, slot, e).wait()
-
-                @pl.when(step >= 2)
-                def _():
-                    leave(step - 2, slot)
-
-                hot = hot_rows(I.rank, lax.rem(step + first, jnp.int32(seqs)), local, length)
+                hot = hot_rows(I.rank, item_of(step) + (0 if near else first), local, length)
+                if near:
+                    came_load(step, slot).wait()
                 for c, span in spans:
-                    out_buf[slot, :, c : c + span] = dot(hot, in_buf[slot, :, c : c + span], 0, 0).astype(BF16)
-
-                @pl.when(step < first)
-                def _():
-                    pltpu.make_async_copy(out_buf.at[slot], far.at[step, :, cols], out_sem.at[slot]).start()
-
-                @pl.when(step >= first)
-                def _():
-                    pltpu.make_async_copy(out_buf.at[slot], near.at[step - first, :, cols], out_sem.at[slot]).start()
-
+                    total = dot(hot, in_buf[slot, :, c : c + span], 0, 0)
+                    if near:
+                        total = total + came[slot, :, c : c + span].astype(F32)
+                    out_buf[slot, :, c : c + span] = total.astype(BF16)
+                if near:
+                    j = lax.rem(step, jnp.int32(quads))
+                    if tag == 0:
+                        ends = [
+                            (r.zc.at[1, j], r.yc.at[1, j]), (r.kept.at[2, j], r.yc.at[0, j]),
+                            (r.zc.at[0, j], r.kept.at[3, j]), (r.kept.at[0, j], r.kept.at[1, j]),
+                        ]
+                    else:
+                        ends = [
+                            (ref.at[j, 0], ref.at[j, 1]) for ref in (r.out.at[1], r.out.at[0], r.pair, r.own)
+                        ]
+                    for i, (to_low, to_high) in enumerate(ends):
+                        @pl.when(lax.div(step, jnp.int32(quads)) == i)
+                        def _():
+                            for copy in leaving(slot, to_low, to_high):
+                                copy.start()
+                else:
+                    to = O.far.at[item_of(step)]
+                    for copy in leaving(slot, to.at[low, cols], to.at[high, cols]):
+                        copy.start()
                 return carry
 
-            lax.fori_loop(0, seqs, body, 0)
-            for step in (seqs - 2, seqs - 1):
-                leave(step, step % 2)
+            lax.fori_loop(0, first, body, 0)
+            left(jnp.int32(first - 1), (first - 1) % 2)
 
         pl.run_scoped(
             scoped,
             pltpu.VMEM((2, local * CAP, w), BF16),
             pltpu.VMEM((2, length, w), BF16),
+            pltpu.VMEM((2, length if near else 16, w), BF16),
             pltpu.SemaphoreType.DMA((2, local)),
+            pltpu.SemaphoreType.DMA((2, 2)),
             pltpu.SemaphoreType.DMA((2,)),
         )
 
@@ -1099,38 +1210,24 @@
             pltpu.SemaphoreType.DMA((2, 2)), pltpu.SemaphoreType.DMA((2,)),
         )
 
-    low, high = pl.ds(0, half), pl.ds(half, half)
-
-    def return_one(tag, w):
-        for s in range(seqs // 2):
-            core_send(tag, s).wait_recv()
-        near, came = O.near, O.ret[tag].came
-
-        def piece_of(quad, j, part, to):
-            s = quad * quads + j
-            return ((near.at[s, part, pl.ds(0, w)], came.at[s, part]), to)
-
-        zc, yc, kept = O.ret[tag].zc, O.ret[tag].yc, O.ret[tag].kept
-        every = range(quads)
-        blend(
-            [piece_of(2, j, low, zc.at[0, j]) for j in every]
-            + [piece_of(3, j, low, zc.at[1, j]) for j in every],
-            w,
-        )
-        hop(tag, 1, 0).start()
-        blend(
-            [piece_of(1, j, high, yc.at[0, j]) for j in every]
-            + [piece_of(3, j, high, yc.at[1, j]) for j in every],
-            w,
-        )
-        hop(tag, 1, 1).start()
-        blend(
-            [piece_of(1, j, low, kept.at[2, j]) for j in every]
-            + [piece_of(2, j, high, kept.at[3, j]) for j in every]
-            + [piece_of(0, j, low, kept.at[0, j]) for j in every]
-            + [piece_of(0, j, high, kept.at[1, j]) for j in every],
-            w,
-        )
+    def out_hop(which):
+        r, sems = O.ret[1], S.ret[1].hops[which]
+        src, dst = ((r.out, r.outin), (r.pair, r.pairin))[which]
+        axis, bit = ((EXP, y_bits[-1]), (GRP, PAIR))[which]
+        return send(src, dst, (sems.at[0, 0], sems.at[1, 0]), axis, bit)
+
+    def out_two():
+        r = O.ret[1]
+        out_hop(0).wait_recv()
+        every = [(j, p) for j in range(quads) for p in range(2)]
+        blend([((r.pair.at[j, p], r.outin.at[1, j, p]), r.pair.at[j, p]) for j, p in every], wide)
+        out_hop(1).start()
+
+    def out_end():
+        r = O.ret[1]
+        out_hop(1).wait_recv()
+        terms = [[[r.own.at[j, p], r.outin.at[0, j, p], r.pairin.at[j, p]] for j in range(quads)] for p in range(2)]
+        return last_bits(1, terms, wide)
 
     def return_two(tag, w):
         kept = O.ret[tag].kept
@@ -1150,6 +1247,9 @@
             [[kept.at[0, j], O.ret[tag].zcin.at[0, j], O.ret[tag].ylowin.at[j]] for j in range(quads)],
             [[kept.at[1, j], O.ret[tag].ycin.at[0, j], O.ret[tag].zhighin.at[j]] for j in range(quads)],
         ]
+        return last_bits(tag, terms, w)
+
+    def last_bits(tag, terms, w):
         if quads == 1:
             return [terms[0][0], terms[1][0]]
         tot, came = O.ret[tag].more
@@ -1228,7 +1328,7 @@
             store(e, e % 2).wait()
 
 
-    order = [(EXP, bit) for bit in exp_bits] + [(GRP, bit) for bit in [PAIR] + mids + [1]]
+    order = [(EXP, bit) for bit in exp_bits] + [(GRP, bit) for bit in [1, PAIR] + mids]
     left = [(GRP, bit) for bit in reversed(grp_bits)] + [(EXP, bit) for bit in reversed(exp_bits)]
     axis_of = []
     for name in order:
@@ -1289,24 +1389,11 @@
             all_send(tag, i + 1).start()
 
     def gain_send(i):
-        axis, bit = order[i]
-        sems = S.gall
-        return send(O.gsum[i], O.gin[i], (sems.at[0, i], sems.at[1, i]), axis, bit)
+        return send(S.gain.at[i], S.gin.at[i], (S.gall.at[0, i], S.gall.at[1, i]), *order[i])
 
     def gain_step(i):
         gain_send(i).wait_recv()
-
-        def scoped(a, sems):
-            came = pltpu.make_async_copy(O.gin[i], a, sems.at[0])
-            came.start()
-            came.wait()
-            S.gain[...] = S.gain[...] + a[...]
-            to = O.gains if i + 1 == len(order) else O.gsum[i + 1]
-            store = pltpu.make_async_copy(S.gain, to, sems.at[0])
-            store.start()
-            store.wait()
-
-        pl.run_scoped(scoped, pltpu.VMEM((8, width), F32), pltpu.SemaphoreType.DMA((1,)))
+        S.gain[i + 1] = S.gain[i] + S.gin[i]
         if i + 1 < len(order):
             gain_send(i + 1).start()
 
@@ -1322,7 +1409,7 @@
     def hidden_grad(terms, branch, dm, dh, wo, sems):
         for i in range(n_grp):
             pltpu.make_async_copy(I.wo.at[i], wo.at[pl.ds(i * rows_w, rows_w)], sems.at[0]).start()
-        S.gain[...] = jnp.zeros_like(S.gain)
+        S.gain[0] = jnp.zeros((8, width), F32)
 
         def scoped(bufs, hid, up):
             for part in range(2):
@@ -1348,7 +1435,7 @@
                     value = up[r].astype(F32) + back
                     dh[big] = value
                     branch[big] = value.astype(BF16)
-                    S.gain[1:2] = S.gain[1:2] + jnp.sum(d_n2 * normal, axis=0, keepdims=True)
+                    S.gain[0, 1:2] = S.gain[0, 1:2] + jnp.sum(d_n2 * normal, axis=0, keepdims=True)
                     return carry
 
                 lax.fori_loop(0, half // chunk_rows, body, 0)
@@ -1479,7 +1566,7 @@
                     d_n1 = dn[r]
                     normal, back = norm_back(d_n1, x[r].astype(F32), I.inv_one[big], I.gains[0:1])
                     res[r] = (dh[r] + back).astype(BF16)
-                    S.gain[0:1] = S.gain[0:1] + jnp.sum(d_n1 * normal, axis=0, keepdims=True)
+                    S.gain[0, 0:1] = S.gain[0, 0:1] + jnp.sum(d_n1 * normal, axis=0, keepdims=True)
                     return carry
 
                 lax.fori_loop(0, half // chunk_rows, body, 0)
@@ -1491,9 +1578,6 @@
             scoped, pltpu.VMEM((half, width), F32), pltpu.VMEM((half, width), F32),
             pltpu.VMEM((half, width), BF16), pltpu.VMEM((half, width), BF16),
         )
-        store = pltpu.make_async_copy(S.gain, O.gsum[0], sems.at[0])
-        store.start()
-        store.wait()
         gain_send(0).start()
 
     def layer_end(terms):
@@ -1534,7 +1618,7 @@
 
 
     chunks = 3 * local
-    done = [4 if local == 4 else 0] + [0] * len(mids)
+    done = [2 if local == 4 else 0] + [0] * len(mids)
 
     def pump(*upto):
         for stage, last in enumerate(upto):
@@ -1546,23 +1630,14 @@
                 grads(stage, done[stage], last)
                 done[stage] = last
 
-    pl.run_scoped(
-        experts,
-        pltpu.VMEM((rows, width), BF16),
-        pltpu.VMEM((rows, width), BF16),
-        pltpu.VMEM((rows, ff), F32),
-        pltpu.VMEM((width, 2 * ff), BF16),
-        pltpu.VMEM((block, 2 * ff), F32),
-        pltpu.VMEM((rows, 2 * ff), BF16),
-        pltpu.VMEM((rows, ff), BF16),
-        pltpu.VMEM((3, width // 2, ff), BF16),
-        pltpu.VMEM((3, width // 2, ff), BF16),
-        pltpu.VMEM((rows, width), BF16),
-        pltpu.SemaphoreType.DMA((6,)),
-    )
-    pump(4, 1)
-    collapse(0, width)
-    pump(5, 2)
+    forward_of(0, 1)
+    grads_of(0, 1)
+    forward_of(1, local)
+    collapse(0, width, False)
+    pump(3, 1)
+    grads_of(1, 2)
+    collapse(0, width, True)
+    grads_of(2, max(2, local - 1))
     pl.run_scoped(
         output_phase,
         pltpu.VMEM((2, rows, ff), BF16),
@@ -1570,15 +1645,13 @@
         pltpu.VMEM((2, rows, wide), BF16),
         pltpu.SemaphoreType.DMA((2, 3)),
     )
-    return_one(0, width)
-    pump(6, 3)
     for s in range(seqs // 2):
         core_send(0, s).wait_send()
-    collapse(1, wide)
-    pump(7, 4)
+    collapse(1, wide, False)
     return_two(0, width)
-    return_one(1, wide)
-    pump(8, 5)
+    pump(6, 3)
+    collapse(1, wide, True)
+    grads_of(max(2, local - 1), local)
 
     def backward(branch, dm, mixed, sems):
         load = pltpu.make_async_copy(I.mixed, mixed, sems.at[0])
@@ -1589,7 +1662,8 @@
             functools.partial(hidden_grad, terms, branch, dm),
             pltpu.VMEM((length, width), F32), pltpu.VMEM((width, width), BF16), pltpu.SemaphoreType.DMA((6,)),
         )
-        pump(9, 6)
+        pump(7, 5)
+
         def out_grad(left, buf, own):
             load = pltpu.make_async_copy(I.mixed_wide, left, own.at[0])
             load.start()
@@ -1621,12 +1695,8 @@
                 pltpu.VMEM((length, length), F32), pltpu.VMEM((length, HEAD_DIM), F32),
                 pltpu.VMEM((length, HEAD_DIM), F32), pltpu.VMEM((length, HEAD_DIM), F32),
             )
-            pump(10, 7)
             all_step(0, 0)
-            pl.run_scoped(
-                functools.partial(token_grad, dqkv),
-                pltpu.VMEM((width, qkv), BF16), pltpu.SemaphoreType.DMA((4,)),
-            )
+            pump(9, 7)
 
             def second(n1, buf, own):
                 load = pltpu.make_async_copy(I.n1, n1, own.at[0])
@@ -1637,6 +1707,10 @@
             pl.run_scoped(
                 second, pltpu.VMEM((length, tall), BF16), pltpu.VMEM((2, *step, share, qkv), BF16), pltpu.SemaphoreType.DMA((2,))
             )
+            pl.run_scoped(
+                functools.partial(token_grad, dqkv),
+                pltpu.VMEM((width, qkv), BF16), pltpu.SemaphoreType.DMA((4,)),
+            )
 
         pl.run_scoped(rest, pltpu.VMEM((length, qkv), BF16))
 
@@ -1644,25 +1718,33 @@
         backward, pltpu.VMEM((length, width), BF16), pltpu.VMEM((length, width), BF16),
         pltpu.VMEM((length, width), BF16), pltpu.SemaphoreType.DMA((3,)),
     )
-    pump(11, 8)
-    return_two(1, wide)
     all_step(1, 0)
     gain_step(0)
     all_step(0, 1)
+    pump(11, 8)
+    out_two()
+    gain_step(1)
+    all_step(1, 1)
     pump(12, 9)
-    all_step(1, 1)
-    gain_step(1)
+    layer_end(out_end())
     all_step(0, 2)
-    layer_end(return_end(1, wide))
+    gain_step(2)
+    all_step(1, 2)
     pump(12, 10)
-    for i in range(2, len(order)):
+    for i in range(3, len(order)):
+        all_step(0, i)
+        gain_step(i)
         all_step(1, i)
-        gain_step(i)
-        if i + 1 < len(order):
-            all_step(0, i + 1)
-        if i == 2:
+        if i == 3:
             pump(12, 11)
     pump(*([chunks] * (len(mids) + 1)))
+
+    def gains_out(sem):
+        copy = pltpu.make_async_copy(S.gain.at[len(order)], O.gains, sem.at[0])
+        copy.start()
+        copy.wait()
+
+    pl.run_scoped(gains_out, pltpu.SemaphoreType.DMA((1,)))
 
     def close(c, carry):
         for stage in range(len(mids) + 1):
@@ -1672,7 +1754,8 @@
 
     lax.fori_loop(0, chunks, close, 0)
     return_close(0)
-    return_close(1)
+    for which in range(2):
+        out_hop(which).wait_send()
     for s in range(seqs // 2):
         core_send(1, s).wait_send()
     for i in range(len(order)):
@@ -1736,14 +1819,14 @@
     a = front(
         dims,
         dict(
-            tokens=tokens, dy=cotangent, small=small, wq=shard, wo=o_weight, w_down=down_weight,
+            tokens=tokens, dy=cotangent, small=small, wq=shard, wo=o_weight,
             cos=cosine, sin=sine, tagc=tagc, tagr=tagr,
         ),
     )
     r = mega(
         dims,
         dict(
-            x=a.x, y=a.y, t=a.t, w_gate=gate_weight, w_up=up_weight, w_down=down_weight, hidden=a.hidden,
+            x=a.x, y=a.y, w_gate=gate_weight, w_up=up_weight, w_down=down_weight, hidden=a.hidden,
             dy=cotangent, wo=a.wo, mixed=a.mixed, q=a.q, k=a.k, v=a.v, wqkv=a.wq, tokens=tokens,
             n1=spread(a.n1, devices), mixed_wide=spread(a.mixed, devices),
         ),

time: 920 us -> 828 us (0.900)
  Pallas kernels: 875 us -> 784 us
    pallas_call x1, Pallas kernels: 306 us -> 255 us  [front(): pl.pallas_call(functools.partial(front_body, dims, in_tree, out_tree, sem...]
    pallas_call x1, Pallas kernels: 569 us -> 529 us  [mega(): pl.pallas_call(functools.partial(mega_body, dims, in_tree, out_tree, sem_...]
where the time goes in v3:
time: 828 us; the launch traced here: 817 us
  Pallas kernels  784 us (95%)
  other arithmetic  19.7 us (2%)
  local copies, waits for them, and re-layouts  12.6 us (2%)
    pallas_call x1, Pallas kernels, mega(): pl.pallas_call(functools.partial(mega_body, dims, in_tree, out_tree, sem_...  529 us
    pallas_call x1, Pallas kernels, front(): pl.pallas_call(functools.partial(front_body, dims, in_tree, out_tree, sem...  255 us

profile of v3, /device:TPU:0, one launch (start us, length us, event | category | flops | bytes accessed | tf_op | source)
XLA Modules:
  0.0 817.4 jit_solution(9536981666901350857)
XLA Ops:
  0.6 0.7 reduce_max.9
  1.4 0.7 fusion.7
  2.1 0.2 copy.58
  2.3 0.2 fusion.6
  2.5 0.1 copy.59
  2.6 0.7 convert_bitcast_fusion
  3.3 0.6 pad_maximum_fusion.1.refs_3_
  4.0 0.7 convert_reduce_fusion
  4.7 0.7 select_reduce_fusion
  5.5 0.9 select_n.36.refs_4_.refs_16_
  6.4 0.6 select_n.34.refs_5_.refs_17_
  7.0 0.7 stack.10
  7.6 0.7 stack.9
  8.3 2.2 pad_maximum_fusion.refs_8_
  10.5 255.4 %front.1 = (f32[4,896,1]{2,1,0:T(8,128)}, bf16[8,768,1536]{2,1,0:T(8,128)(2,1)}, f32[8,1536]{1,0:T(8,128)}, f32[4,896,1]{2,1,0:T(8,128)}, f32[768,1536]{1,0:T(8,...) custom-call(f32[768,128]{1,0:T(8,128)} %constant.34.clone.refs_0_.re, ...), custom_call_target="tpu_custom_call" | custom-call | tf_op jit(solution)/shard_map/front/pallas_call | solution.py:662
  265.8 3.6 reduce
  269.5 0.6 reshape.79.refs_9_
  270.1 528.5 %experts_and_back.1 = (bf16[4,896,768]{2,1,0:T(8,128)(2,1)}, bf16[12,768,768]{2,1,0:T(8,128)(2,1)}, bf16[12,384,768]{2,1,0:T(8,128)(2,1)}, bf16[4,896,1536]{2,1,...) custom-call(f32[4,896,1]{2,1,0:T(8,128)} %get-tuple-element.36.refs_, ...), custom_call_target="tpu_custom_call" | custom-call | tf_op jit(solution)/shard_map/experts_and_back/pallas_call | solution.py:1773
  798.7 0.0 copy-start
  798.7 8.7 %bitcast_convert_fusion = (f32[8,192,768]{2,1,0:T(8,128)}, f32[8,192,768]{2,1,0:T(8,128)}, f32[8,192,768]{2,1,0:T(8,128)}) fusion(bf16[3,8,192,768]{3,2,1,0:T(8,128)(2,1)} %get-tuple-element.59), kind=kLoop, calls=%fused_computation | loop fusion | flops 3538944 | bytes 21233664 | tf_op jit(solution)/shard_map/convert_element_type | solution.py:1852
  807.4 0.0 copy-done
  807.4 0.4 multiply_reduce_fusion
  807.8 0.4 subtract_multiply_fusion
  808.2 0.0 copy-start.1
  808.2 0.8 copy.62
  808.9 0.7 slice.32
  809.7 0.6 fusion.8
  810.3 0.8 constant_dynamic-slice_fusion
  811.1 0.5 slice_bitcast_fusion
  811.6 3.2 copy.67
  814.8 1.4 copy.68
  816.2 0.7 copy.69
  (8 shorter events, 0.0 us)
Async XLA Ops:
  798.7 8.7 %copy-start = (f32[768,128]{1,0:T(8,128)S(1)}, f32[768,128]{1,0:T(8,128)}, u32[]{:S(2)}) copy-start(f32[768,128]{1,0:T(8,128)} %get-tuple-element.55) | copy-start | bytes 1179652
  807.4 1.5 copy-start.2
  808.2 6.7 copy-start.1
  814.8 1.4 copy-start.3
